TPU v7x, 32 devices: a whole 2x2x4 slice. The times are simulated.
32 devices in a mesh: expert: 8 (over z, x), tensor: 4 (over y, core).
Axes of the slice: x: 2, y: 2, z: 4, core: 2. Of those that a mesh axis runs over, the one named last changes fastest.
Arguments:
- layer_input: bfloat16 [2, 1024, 2048], P(None, 'expert'), may hold values from -6 to 6
- positions: int32 [2, 1024], P(None, 'expert'), may hold values from 0 to 127, as said below
- parents: int32 [2, 8, 4], P(None, 'expert'), may hold values from 0 to 2, as said below
- routes: int32 [2, 1024, 4], P(None, 'expert'), may hold values from 0 to 7, as said below
- route_slots: int32 [2, 1024, 4], P(None, 'expert'), may hold values from 0 to 127, as said below
- norm1_gain: bfloat16 [2048], P('expert'), may hold values from 0.5 to 1.5
- project_weight: bfloat16 [2048, 3, 2048], P('expert', None, 'tensor'), may hold values from -0.125 to 0.125
- project_bias: bfloat16 [3, 2048], P(None, ('tensor', 'expert')), may hold values from -0.59765625 to 0.59765625
- output_weight: bfloat16 [2048, 2048], P('tensor', 'expert'), may hold values from -0.75 to 0.75
- norm2_gain: bfloat16 [2048], P('expert'), may hold values from 0.5 to 1.5
- router_weight: bfloat16 [2048, 8], P('expert'), may hold values from -0.0625 to 0.0625
- shared_vector: bfloat16 [2048], P('expert'), may hold values from -0.125 to 0.125
- shared_gate: bfloat16 [2048, 5632], P('expert', 'tensor'), may hold values from -0.125 to 0.125
- shared_up: bfloat16 [2048, 5632], P('expert', 'tensor'), may hold values from -0.125 to 0.125
- shared_down: bfloat16 [5632, 2048], P('tensor', 'expert'), may hold values from -0.078125 to 0.078125
- expert_gate: bfloat16 [8, 2048, 1408], P('expert', None, 'tensor'), may hold values from -0.125 to 0.125
- expert_up: bfloat16 [8, 2048, 1408], P('expert', None, 'tensor'), may hold values from -0.125 to 0.125
- expert_down: bfloat16 [8, 1408, 2048], P('expert', 'tensor'), may hold values from -0.15625 to 0.15625
- cotangent: bfloat16 [2, 1024, 2048], P(None, 'expert'), may hold values from -6 to 6
Outputs:
- layer_output: bfloat16 [2, 1024, 2048], P(None, 'expert')
- input_grad: float32 [2, 1024, 2048], P(None, 'expert')
- norm1_gain_grad: float32 [2048], P('expert')
- project_weight_grad: float32 [2048, 3, 2048], P('expert', None, 'tensor')
- project_bias_grad: float32 [3, 2048], P(None, ('tensor', 'expert'))
- output_weight_grad: float32 [2048, 2048], P('tensor', 'expert')
- norm2_gain_grad: float32 [2048], P('expert')
- router_weight_grad: float32 [2048, 8], P('expert')
- shared_vector_grad: float32 [2048], P('expert')
- shared_gate_grad: float32 [2048, 5632], P('expert', 'tensor')
- shared_up_grad: float32 [2048, 5632], P('expert', 'tensor')
- shared_down_grad: float32 [5632, 2048], P('tensor', 'expert')
- expert_gate_grad: float32 [8, 2048, 1408], P('expert', None, 'tensor')
- expert_up_grad: float32 [8, 2048, 1408], P('expert', None, 'tensor')
- expert_down_grad: float32 [8, 1408, 2048], P('expert', 'tensor')
Inputs may be any that keep to these rules, and one draw needn't show every extreme that they name: positions[m, t] is 32 times the number of strict ancestors of the segment of t in its tree, plus the index of t within its segment. parents[m, j, 0] = 0 for the root segment; for s > 0, parents[m, j, s] < s is the parent of segment s. `routes`: each token names 4 different experts. route_slots[m, t, k] counts the pairs (t', k') before (t, k), in the order of token then route, among the 128 tokens of the same tree, whose route names the same expert.
All inputs are finite; a program needn't handle non-finite values.
Results may differ from a plain program's by a relative error of at most 0.02.
Values may be sent and summed in bfloat16 or wider, within the bound.
A program may use at most 192 MiB of HBM per device.

v0:
```python
import jax
import jax.numpy as jnp
from jax import lax
from jax.sharding import PartitionSpec as P

HD = 128
SEG = 32


EPSILON = 1e-06
ROPE_BASE = 1000000.0


def product(left_side, right_side):
    return jnp.dot(left_side, right_side, preferred_element_type=jnp.float32)


def product_left(left_side, right_side):
    return lax.dot_general(
        left_side, right_side, (((0,), (0,)), ((), ())), preferred_element_type=jnp.float32
    )


def product_right(left_side, right_side):
    return lax.dot_general(
        left_side, right_side, (((1,), (1,)), ((), ())), preferred_element_type=jnp.float32
    )


def silu_slope(inputs):
    sigmoid_value = jax.nn.sigmoid(inputs)
    return sigmoid_value * (1.0 + inputs * (1.0 - sigmoid_value))


def rope_tables(position_row, head_size):
    half_size = head_size // 2
    inverse = ROPE_BASE ** (-(jnp.arange(half_size, dtype=jnp.float32) * 2.0 / head_size))
    angles = position_row.astype(jnp.float32)[:, None] * inverse[None, :]
    cosine = jnp.cos(angles)
    sine_table = jnp.sin(angles)
    return (jnp.concatenate([cosine, cosine], 1), jnp.concatenate([sine_table, sine_table], 1))


def rotate(vectors, cosine, sine_table):
    half_size = vectors.shape[-1] // 2
    turned = jnp.concatenate([-vectors[..., half_size:], vectors[..., :half_size]], -1)
    return vectors * cosine[:, None, :] + turned * sine_table[:, None, :]


def unrotate(gradient, cosine, sine_table):
    half_size = gradient.shape[-1] // 2
    scaled = gradient * sine_table[:, None, :]
    turned = jnp.concatenate([scaled[..., half_size:], -scaled[..., :half_size]], -1)
    return gradient * cosine[:, None, :] + turned


def tree_mask(parent_row, seg_len):
    segment_count = parent_row.shape[0]
    segment_ids = jnp.arange(segment_count, dtype=jnp.int32)
    step_matrix = (
        (parent_row[:, None] == segment_ids[None, :]) & (segment_ids[:, None] > 0)
    ).astype(jnp.float32)
    identity = jnp.eye(segment_count, dtype=jnp.float32)

    def extend(loop_index, reached):
        return jnp.minimum(
            identity + jnp.dot(step_matrix, reached, precision=lax.Precision.HIGHEST), 1.0
        )

    reached = lax.fori_loop(0, segment_count, extend, identity)
    expanded = jnp.repeat(jnp.repeat(reached, seg_len, 0), seg_len, 1) > 0.5
    token_ids = jnp.arange(segment_count * seg_len, dtype=jnp.int32)
    return expanded & (token_ids[None, :] <= token_ids[:, None])


def shards(
    layer_input,
    positions,
    parents,
    routes,
    route_slots,
    norm1_gain,
    project_weight,
    project_bias,
    output_weight,
    norm2_gain,
    router_weight,
    shared_vector,
    shared_gate,
    shared_up,
    shared_down,
    expert_gate,
    expert_up,
    expert_down,
    cotangent,
):
    micro_count, seq_rows, model_width = layer_input.shape
    top_count = routes.shape[2]
    expert_count = router_weight.shape[1]
    capacity = seq_rows * top_count * 5 // (4 * expert_count)
    slot_total = expert_count * capacity
    gathered = (
        lax.all_gather(norm1_gain, "expert", axis=0, tiled=True),
        lax.all_gather(project_weight, "expert", axis=0, tiled=True),
        lax.all_gather(project_bias, "expert", axis=1, tiled=True),
        lax.all_gather(output_weight, "expert", axis=1, tiled=True),
        lax.all_gather(norm2_gain, "expert", axis=0, tiled=True),
        lax.all_gather(router_weight, "expert", axis=0, tiled=True),
        lax.all_gather(shared_vector, "expert", axis=0, tiled=True),
        lax.all_gather(shared_gate, "expert", axis=0, tiled=True),
        lax.all_gather(shared_up, "expert", axis=0, tiled=True),
        lax.all_gather(shared_down, "expert", axis=1, tiled=True),
    )
    (
        gain_first,
        project_in,
        bias_in,
        project_out,
        gain_second,
        router_full,
        vector_full,
        shared_gates,
        shared_ups,
        shared_downs,
    ) = gathered
    local_width = project_in.shape[2]
    head_count = local_width // HD
    shared_local = shared_gates.shape[1]
    project_flat = project_in.reshape(model_width, 3 * local_width)
    bias_flat = bias_in.astype(jnp.float32).reshape(3 * local_width)
    gain_one = gain_first.astype(jnp.float32)
    gain_two = gain_second.astype(jnp.float32)
    small_weights = jnp.concatenate([router_full, vector_full[:, None]], 1)
    expert_gates = expert_gate[0]
    expert_ups = expert_up[0]
    expert_downs = expert_down[0]
    score_scale = HD ** (-0.5)
    expert_ids = jnp.arange(expert_count, dtype=jnp.int32)
    pair_ids = jnp.arange(seq_rows * top_count, dtype=jnp.int32).reshape(seq_rows, top_count)
    zero_row = jnp.zeros((1, model_width), jnp.bfloat16)
    stored = []
    layer_outputs = []
    for batch_index in range(micro_count):
        input_rows = layer_input[batch_index].astype(jnp.float32)
        norm_one = lax.rsqrt(jnp.mean(input_rows * input_rows, -1, keepdims=True) + EPSILON)
        normed_one = (input_rows * norm_one * gain_one).astype(jnp.bfloat16)
        projected = (product(normed_one, project_flat) + bias_flat).reshape(
            seq_rows, 3, head_count, HD
        )
        cosine, sine_table = rope_tables(positions[batch_index], HD)
        queries = rotate(projected[:, 0], cosine, sine_table).astype(jnp.bfloat16)
        key_rows = rotate(projected[:, 1], cosine, sine_table).astype(jnp.bfloat16)
        values = projected[:, 2].astype(jnp.bfloat16)
        allowed = tree_mask(parents[batch_index, 0], SEG)
        scores = (
            jnp.einsum("qhd,khd->hqk", queries, key_rows, preferred_element_type=jnp.float32)
            * score_scale
        )
        masked = jnp.where(allowed[None], scores, -1e30)
        highest = jnp.max(masked, -1, keepdims=True)
        exponent = jnp.exp(masked - highest)
        row_total = jnp.sum(exponent, -1, keepdims=True)
        attention_probs = exponent / row_total
        log_total = highest + jnp.log(row_total)
        heads_out = (
            jnp.einsum(
                "hqk,khd->qhd",
                attention_probs.astype(jnp.bfloat16),
                values,
                preferred_element_type=jnp.float32,
            )
            .astype(jnp.bfloat16)
            .reshape(seq_rows, local_width)
        )
        attention = lax.psum(product(heads_out, project_out), "tensor")
        hidden_state = input_rows + attention
        norm_two = lax.rsqrt(jnp.mean(hidden_state * hidden_state, -1, keepdims=True) + EPSILON)
        normed_two = (hidden_state * norm_two * gain_two).astype(jnp.bfloat16)
        small_logits = product(normed_two, small_weights)
        router_prob = jax.nn.softmax(small_logits[:, :expert_count], axis=-1)
        onehot = (routes[batch_index][..., None] == expert_ids).astype(jnp.float32)
        picked = jnp.sum(onehot * router_prob[:, None, :], -1)
        picked_sum = jnp.sum(picked, -1, keepdims=True)
        route_gates = picked / picked_sum
        shared_scale = jax.nn.sigmoid(small_logits[:, expert_count])
        gate_shared = product(normed_two, shared_gates)
        up_shared = product(normed_two, shared_ups)
        hidden_shared = (jax.nn.silu(gate_shared) * up_shared).astype(jnp.bfloat16)
        shared_part = product(hidden_shared, shared_downs)
        slot_rows = route_slots[batch_index]
        valid = slot_rows < capacity
        keep_mask = valid.astype(jnp.float32)
        slot_index = routes[batch_index] * capacity + jnp.minimum(slot_rows, capacity - 1)
        safe_index = jnp.where(valid, slot_index, 0)
        target = jnp.where(valid, slot_index, slot_total).reshape(-1)
        slot_table = (
            jnp.full((slot_total,), seq_rows * top_count, jnp.int32)
            .at[target]
            .set(pair_ids.reshape(-1), mode="drop")
        )
        padded = jnp.concatenate([normed_two, zero_row], 0)
        outgoing = padded[slot_table // top_count].reshape(expert_count, capacity, model_width)
        received = lax.all_to_all(outgoing, "expert", split_axis=0, concat_axis=0, tiled=True)
        run_owner_rows = received.reshape(-1, model_width)
        run_gate_expert = product(run_owner_rows, expert_gates)
        run_up_expert = product(run_owner_rows, expert_ups)
        run_hidden_expert = (jax.nn.silu(run_gate_expert) * run_up_expert).astype(jnp.bfloat16)
        expert_rows = product(run_hidden_expert, expert_downs).reshape(
            received.shape[0], received.shape[1], model_width
        )
        returned = lax.all_to_all(expert_rows, "expert", split_axis=0, concat_axis=0, tiled=True)
        returned, received = (returned, received)
        pair_out = returned.reshape(slot_total, -1)[safe_index] * keep_mask[..., None]
        routed = jnp.sum(route_gates[..., None] * pair_out, 1)
        shared_out, routed_full = lax.psum((shared_part, routed), "tensor")
        layer_outputs.append(
            (hidden_state + shared_scale[:, None] * shared_out + routed_full).astype(jnp.bfloat16)
        )
        stored.append(
            (
                input_rows,
                norm_one,
                normed_one,
                cosine,
                sine_table,
                queries,
                key_rows,
                values,
                allowed,
                log_total,
                heads_out,
                hidden_state,
                norm_two,
                normed_two,
                router_prob,
                onehot,
                picked_sum,
                route_gates,
                shared_scale,
                gate_shared,
                up_shared,
                hidden_shared,
                shared_out,
                pair_out,
                safe_index,
                keep_mask,
                slot_table,
                received,
            )
        )
    grad_gain_one = jnp.zeros((model_width,), jnp.float32)
    grad_gain_two = jnp.zeros((model_width,), jnp.float32)
    grad_project = jnp.zeros((model_width, 3 * local_width), jnp.float32)
    grad_bias = jnp.zeros((3 * local_width,), jnp.float32)
    grad_output = jnp.zeros((local_width, model_width), jnp.float32)
    grad_small = jnp.zeros((model_width, expert_count + 1), jnp.float32)
    grad_shared_gate = jnp.zeros((model_width, shared_local), jnp.float32)
    grad_shared_up = jnp.zeros((model_width, shared_local), jnp.float32)
    grad_shared_down = jnp.zeros((shared_local, model_width), jnp.float32)
    grad_expert_gate = jnp.zeros(expert_gates.shape, jnp.float32)
    grad_expert_up = jnp.zeros(expert_ups.shape, jnp.float32)
    grad_expert_down = jnp.zeros(expert_downs.shape, jnp.float32)
    input_grads = [None] * micro_count
    for batch_index in reversed(range(micro_count)):
        (
            input_rows,
            norm_one,
            normed_one,
            cosine,
            sine_table,
            queries,
            key_rows,
            values,
            allowed,
            log_total,
            heads_out,
            hidden_state,
            norm_two,
            normed_two,
            router_prob,
            onehot,
            picked_sum,
            route_gates,
            shared_scale,
            gate_shared,
            up_shared,
            hidden_shared,
            shared_out,
            pair_out,
            safe_index,
            keep_mask,
            slot_table,
            received,
        ) = stored[batch_index]
        upstream = cotangent[batch_index].astype(jnp.float32)
        shared_grad = (shared_scale[:, None] * upstream).astype(jnp.bfloat16)
        scale_grad = jnp.sum(upstream * shared_out, -1) * shared_scale * (1.0 - shared_scale)
        gate_part = jnp.sum(upstream[:, None, :] * pair_out, -1)
        pair_grad = (
            (route_gates[..., None] * upstream[:, None, :])
            .astype(jnp.bfloat16)
            .reshape(seq_rows * top_count, model_width)
        )
        outgoing_grad = jnp.concatenate([pair_grad, zero_row], 0)[slot_table].reshape(
            expert_count, capacity, model_width
        )
        arrived = lax.all_to_all(outgoing_grad, "expert", split_axis=0, concat_axis=0, tiled=True)
        owner_rows = received.reshape(-1, model_width)
        owner_grads = arrived.reshape(-1, model_width)
        gate_expert = product(owner_rows, expert_gates)
        up_expert = product(owner_rows, expert_ups)
        active_expert = jax.nn.silu(gate_expert)
        hidden_expert = (active_expert * up_expert).astype(jnp.bfloat16)
        hidden_expert_grad = product_right(owner_grads, expert_downs)
        grad_expert_down = grad_expert_down + product_left(hidden_expert, owner_grads)
        gate_expert_grad = (hidden_expert_grad * up_expert * silu_slope(gate_expert)).astype(
            jnp.bfloat16
        )
        up_expert_grad = (hidden_expert_grad * active_expert).astype(jnp.bfloat16)
        grad_expert_gate = grad_expert_gate + product_left(owner_rows, gate_expert_grad)
        grad_expert_up = grad_expert_up + product_left(owner_rows, up_expert_grad)
        row_grad = product_right(gate_expert_grad, expert_gates) + product_right(
            up_expert_grad, expert_ups
        )
        row_back = lax.all_to_all(
            row_grad.reshape(expert_count, capacity, model_width),
            "expert",
            split_axis=0,
            concat_axis=0,
            tiled=True,
        )
        routed_back = jnp.sum(
            row_back.reshape(slot_total, model_width)[safe_index] * keep_mask[..., None], 1
        )
        hidden_shared_grad = product_right(shared_grad, shared_downs)
        grad_shared_down = grad_shared_down + product_left(hidden_shared, shared_grad)
        gate_shared_grad = (hidden_shared_grad * up_shared * silu_slope(gate_shared)).astype(
            jnp.bfloat16
        )
        up_shared_grad = (hidden_shared_grad * jax.nn.silu(gate_shared)).astype(jnp.bfloat16)
        grad_shared_gate = grad_shared_gate + product_left(normed_two, gate_shared_grad)
        grad_shared_up = grad_shared_up + product_left(normed_two, up_shared_grad)
        normed_part = (
            product_right(gate_shared_grad, shared_gates)
            + product_right(up_shared_grad, shared_ups)
            + routed_back
        )
        normed_sum, gate_grad = lax.psum((normed_part, gate_part), "tensor")
        picked_grad = (gate_grad - jnp.sum(gate_grad * route_gates, -1, keepdims=True)) / picked_sum
        prob_grad = jnp.sum(picked_grad[..., None] * onehot, 1)
        logit_grad = router_prob * (prob_grad - jnp.sum(router_prob * prob_grad, -1, keepdims=True))
        small_grad = jnp.concatenate([logit_grad, scale_grad[:, None]], 1).astype(jnp.bfloat16)
        grad_small = grad_small + product_left(normed_two, small_grad)
        normed_two_grad = normed_sum + product_right(small_grad, small_weights)
        grad_gain_two = grad_gain_two + jnp.sum(normed_two_grad * hidden_state * norm_two, 0)
        scaled_two = normed_two_grad * gain_two
        hidden_grad = (
            upstream
            + norm_two * scaled_two
            - hidden_state * norm_two**3 * jnp.mean(scaled_two * hidden_state, -1, keepdims=True)
        )
        attention_grad = hidden_grad.astype(jnp.bfloat16)
        grad_output = grad_output + product_left(heads_out, attention_grad)
        heads_grad = (
            product_right(attention_grad, project_out)
            .astype(jnp.bfloat16)
            .reshape(seq_rows, head_count, HD)
        )
        scores = (
            jnp.einsum("qhd,khd->hqk", queries, key_rows, preferred_element_type=jnp.float32)
            * score_scale
        )
        masked = jnp.where(allowed[None], scores, -1e30)
        attention_probs = jnp.exp(masked - log_total)
        value_grad = jnp.einsum(
            "hqk,qhd->khd",
            attention_probs.astype(jnp.bfloat16),
            heads_grad,
            preferred_element_type=jnp.float32,
        )
        prob_grads = jnp.einsum(
            "qhd,khd->hqk", heads_grad, values, preferred_element_type=jnp.float32
        )
        score_grad = (
            attention_probs
            * (prob_grads - jnp.sum(attention_probs * prob_grads, -1, keepdims=True))
        ).astype(jnp.bfloat16)
        query_grad = (
            jnp.einsum("hqk,khd->qhd", score_grad, key_rows, preferred_element_type=jnp.float32)
            * score_scale
        )
        key_grad = (
            jnp.einsum("hqk,qhd->khd", score_grad, queries, preferred_element_type=jnp.float32)
            * score_scale
        )
        projected_grad = (
            jnp.stack(
                [
                    unrotate(query_grad, cosine, sine_table),
                    unrotate(key_grad, cosine, sine_table),
                    value_grad,
                ],
                1,
            )
            .astype(jnp.bfloat16)
            .reshape(seq_rows, 3 * local_width)
        )
        grad_bias = grad_bias + jnp.sum(projected_grad.astype(jnp.float32), 0)
        grad_project = grad_project + product_left(normed_one, projected_grad)
        normed_one_grad = lax.psum(
            product_right(projected_grad, project_flat).astype(jnp.bfloat16), "tensor"
        ).astype(jnp.float32)
        grad_gain_one = grad_gain_one + jnp.sum(normed_one_grad * input_rows * norm_one, 0)
        scaled_one = normed_one_grad * gain_one
        input_grads[batch_index] = (
            hidden_grad
            + norm_one * scaled_one
            - input_rows * norm_one**3 * jnp.mean(scaled_one * input_rows, -1, keepdims=True)
        )
    reduced = (
        lax.psum_scatter(
            grad_gain_one.astype(jnp.bfloat16), "expert", scatter_dimension=0, tiled=True
        ).astype(jnp.float32),
        lax.psum_scatter(
            grad_project.reshape(model_width, 3, local_width).astype(jnp.bfloat16),
            "expert",
            scatter_dimension=0,
            tiled=True,
        ).astype(jnp.float32),
        lax.psum_scatter(
            grad_bias.reshape(3, local_width).astype(jnp.bfloat16),
            "expert",
            scatter_dimension=1,
            tiled=True,
        ).astype(jnp.float32),
        lax.psum_scatter(
            grad_output.astype(jnp.bfloat16), "expert", scatter_dimension=1, tiled=True
        ).astype(jnp.float32),
        lax.psum_scatter(
            grad_gain_two.astype(jnp.bfloat16), "expert", scatter_dimension=0, tiled=True
        ).astype(jnp.float32),
        lax.psum_scatter(
            grad_small[:, :expert_count].astype(jnp.bfloat16),
            "expert",
            scatter_dimension=0,
            tiled=True,
        ).astype(jnp.float32),
        lax.psum_scatter(
            grad_small[:, expert_count].astype(jnp.bfloat16),
            "expert",
            scatter_dimension=0,
            tiled=True,
        ).astype(jnp.float32),
        lax.psum_scatter(
            grad_shared_gate.astype(jnp.bfloat16), "expert", scatter_dimension=0, tiled=True
        ).astype(jnp.float32),
        lax.psum_scatter(
            grad_shared_up.astype(jnp.bfloat16), "expert", scatter_dimension=0, tiled=True
        ).astype(jnp.float32),
        lax.psum_scatter(
            grad_shared_down.astype(jnp.bfloat16), "expert", scatter_dimension=1, tiled=True
        ).astype(jnp.float32),
    )
    return (
        jnp.stack(layer_outputs),
        jnp.stack(input_grads),
        reduced[0],
        reduced[1],
        reduced[2],
        reduced[3],
        reduced[4],
        reduced[5],
        reduced[6],
        reduced[7],
        reduced[8],
        reduced[9],
        grad_expert_gate[None],
        grad_expert_up[None],
        grad_expert_down[None],
    )


def solution(mesh):
    return jax.shard_map(
        shards,
        mesh=mesh,
        in_specs=(
            P(None, "expert", None),
            P(None, "expert"),
            P(None, "expert", None),
            P(None, "expert", None),
            P(None, "expert", None),
            P("expert"),
            P("expert", None, "tensor"),
            P(None, ("tensor", "expert")),
            P("tensor", "expert"),
            P("expert"),
            P("expert", None),
            P("expert"),
            P("expert", "tensor"),
            P("expert", "tensor"),
            P("tensor", "expert"),
            P("expert", None, "tensor"),
            P("expert", None, "tensor"),
            P("expert", "tensor", None),
            P(None, "expert", None),
        ),
        out_specs=(
            P(None, "expert", None),
            P(None, "expert", None),
            P("expert"),
            P("expert", None, "tensor"),
            P(None, ("tensor", "expert")),
            P("tensor", "expert"),
            P("expert"),
            P("expert", None),
            P("expert"),
            P("expert", "tensor"),
            P("expert", "tensor"),
            P("tensor", "expert"),
            P("expert", None, "tensor"),
            P("expert", None, "tensor"),
            P("expert", "tensor", None),
        ),
        check_vma=False,
    )
```

profile of v0, /device:TPU:0, one launch (start us, length us, event | category | flops | bytes accessed | tf_op | source)
XLA Modules:
  0.0 2046.2 jit_solution(18407728787619788415)
XLA Ops:
  12.7 22.3 %all-gather = bf16[8,1,256]{2,1,0:T(2,128)(2,1)S(1)} all-gather(bf16[1,1,256]{2,1,0:T(2,128)(2,1)S(1)} %reshape.797), channel_id=1, replica_groups=mesh['expert'=8,'tensor'=4] {'expert'}, dimensions={0}, use_global_device_ids=true | all-gather | bytes 4608 | tf_op jit(solution)/shard_map/all_gather | solution.py:103
  59.2 55.3 %all-gather.10.cloned.1.call-done = bf16[2048,3,512]{0,2,1:T(8,128)(2,1)} async-done(((bf16[256,3,512]{0,2,1:T(8,128)(2,1)}), bf16[2048,3,512]{0,2,1:T(8,128)(2,1)}) %all-gather.10.cloned.1.call-update) | async-done | bytes 6291472 | tf_op jit(solution)/shard_map/all_gather | solution.py:104
  135.1 29.8 %all-gather.12.cloned.1.call-done = bf16[512,2048]{1,0:T(8,128)(2,1)} async-done(((bf16[512,256]{1,0:T(8,128)(2,1)}), bf16[512,2048]{1,0:T(8,128)(2,1)}) %all-gather.12.cloned.1.call-update) | async-done | bytes 2097168 | tf_op jit(solution)/shard_map/all_gather | solution.py:106
  171.7 17.7 all-gather.2
  201.8 16.8 all-gather.3
  218.6 30.9 %all_gather.35 = bf16[2048,8]{0,1:T(8,128)(2,1)S(1)} all-gather(bf16[256,8]{0,1:T(8,128)(2,1)S(1)} %copy-done.131), channel_id=1, replica_groups=mesh['expert'=8,'tensor'=4] {'expert'}, dimensions={0}, use_global_device_ids=true | all-gather | bytes 36864 | tf_op jit(solution)/shard_map/all_gather | solution.py:108
  275.3 42.2 %all-to-all-done.4 = bf16[8,80,2048]{2,1,0:T(8,128)(2,1)} async-done(((bf16[8,80,2048]{2,1,0:T(8,128)(2,1)}), bf16[8,80,2048]{2,1,0:T(8,128)(2,1)}, u32[]{:S(2)}, u32[]{:S(2)}) %all-to-all-start.4) | async-done | bytes 2621472 | tf_op jit(solution)/shard_map/all_to_all | solution.py:307
  348.1 28.6 %all-to-all-done = bf16[8,80,2048]{2,1,0:T(8,128)(2,1)} async-done(((bf16[8,80,2048]{2,1,0:T(8,128)(2,1)}), bf16[8,80,2048]{2,1,0:T(8,128)(2,1)}, u32[]{:S(2)}, u32[]{:S(2)}) %all-to-all-start) | async-done | bytes 2621472 | tf_op jit(solution)/shard_map/all_to_all | solution.py:203
  385.2 54.7 %all-to-all-done.6 = bf16[8,80,2048]{2,1,0:T(8,128)(2,1)} async-done(((bf16[8,80,2048]{2,1,0:T(8,128)(2,1)}), bf16[8,80,2048]{2,1,0:T(8,128)(2,1)}, u32[]{:S(2)}, u32[]{:S(2)}) %all-to-all-start.6) | async-done | bytes 2621472 | tf_op jit(solution)/shard_map/all_to_all | solution.py:307
  460.3 43.1 %all-to-all-done.2 = bf16[8,80,2048]{2,1,0:T(8,128)(2,1)} async-done(((bf16[8,80,2048]{2,1,0:T(8,128)(2,1)}), bf16[8,80,2048]{2,1,0:T(8,128)(2,1)}, u32[]{:S(2)}, u32[]{:S(2)}) %all-to-all-start.2) | async-done | bytes 2621472 | tf_op jit(solution)/shard_map/all_to_all | solution.py:203
  512.7 180.0 %all-to-all-done.5 = f32[8,80,2048]{2,1,0:T(8,128)} async-done(((f32[8,80,2048]{2,1,0:T(8,128)}), f32[8,80,2048]{2,1,0:T(8,128)}, u32[]{:S(2)}, u32[]{:S(2)}) %all-to-all-start.5) | async-done | bytes 5242912 | tf_op jit(solution)/shard_map/all_to_all | solution.py:325
  713.8 168.0 %all-to-all-done.1 = f32[8,80,2048]{2,1,0:T(8,128)} async-done(((f32[8,80,2048]{2,1,0:T(8,128)}), f32[8,80,2048]{2,1,0:T(8,128)}, u32[]{:S(2)}, u32[]{:S(2)}) %all-to-all-start.1) | async-done | bytes 5242912 | tf_op jit(solution)/shard_map/all_to_all | solution.py:211
  891.1 174.9 %all-to-all-done.7 = f32[8,80,2048]{2,1,0:T(8,128)} async-done(((f32[8,80,2048]{2,1,0:T(8,128)}), f32[8,80,2048]{2,1,0:T(8,128)}, u32[]{:S(2)}, u32[]{:S(2)}) %all-to-all-start.7) | async-done | bytes 5242912 | tf_op jit(solution)/shard_map/all_to_all | solution.py:325
  1146.1 37.0 %all-to-all-done.3 = f32[8,80,2048]{2,1,0:T(8,128)} async-done(((f32[8,80,2048]{2,1,0:T(8,128)}), f32[8,80,2048]{2,1,0:T(8,128)}, u32[]{:S(2)}, u32[]{:S(2)}) %all-to-all-start.3) | async-done | bytes 5242912 | tf_op jit(solution)/shard_map/all_to_all | solution.py:211
  1252.1 91.7 %all-reduce.16.cloned.1.call-done = (f32[128,2048]{1,0:T(8,128)}, f32[128,2048]{1,0:T(8,128)}, f32[128,2048]{1,0:T(8,128)}, f32[128,2048]{1,0:T(8,128)}, f32[128,2048]{1,0:T(8,128)}, /*index=5*/f32[128,2048]{1,0:T(8,128)}) async-done(((f32[128,2048]{1,0:T(8,128)}, f32[128,2048]{1,0:T(8,128)}, f32[128,2048]{1,0:T(8,128)}, f32[128,2048]{1,0:T(8,128)}, f32[128,2048]{1,0:T(8,128)}, ...) | async-done | bytes 6291472 | tf_op jit(solution)/shard_map/psum | solution.py:215
  1418.1 40.3 %reduce-scatter.20.cloned.1.call-done = bf16[1408,256]{1,0:T(8,128)(2,1)} async-done(((bf16[1408,2048]{1,0:T(8,128)(2,1)}), bf16[1408,256]{1,0:T(8,128)(2,1)}) %reduce-scatter.20.cloned.1.call-update) | async-done | bytes 720912 | tf_op jit(solution)/shard_map/reduce_scatter | solution.py:460
  1460.8 111.6 %reduce-scatter.16.cloned.1.call-done = bf16[256,1408]{1,0:T(8,128)(2,1)} async-done(((bf16[2048,1408]{1,0:T(8,128)(2,1)}), bf16[256,1408]{1,0:T(8,128)(2,1)}) %reduce-scatter.16.cloned.1.call-update) | async-done | bytes 720912 | tf_op jit(solution)/shard_map/reduce_scatter | solution.py:454
  1574.7 111.4 %reduce-scatter.18.cloned.1.call-done = bf16[256,1408]{1,0:T(8,128)(2,1)} async-done(((bf16[2048,1408]{1,0:T(8,128)(2,1)}), bf16[256,1408]{1,0:T(8,128)(2,1)}) %reduce-scatter.18.cloned.1.call-update) | async-done | bytes 720912 | tf_op jit(solution)/shard_map/reduce_scatter | solution.py:457
  1690.3 60.2 %reduce-scatter.22.cloned.1.call-done = bf16[64,3]{1,0:T(8,128)(2,1)} async-done(((bf16[512,3]{1,0:T(8,128)(2,1)}), bf16[64,3]{1,0:T(8,128)(2,1)}) %reduce-scatter.22.cloned.1.call-update) | async-done | bytes 400
  1751.8 54.5 %reduce-scatter.14.cloned.1.call-done = bf16[256,8]{0,1:T(8,128)(2,1)} async-done(((bf16[2048,8]{0,1:T(8,128)(2,1)}), bf16[256,8]{0,1:T(8,128)(2,1)}) %reduce-scatter.14.cloned.1.call-update) | async-done | bytes 4112 | tf_op jit(solution)/shard_map/reduce_scatter | solution.py:442
  1807.6 36.5 %all-reduce.20.cloned.1.call-done = (bf16[128,2048]{1,0:T(8,128)(2,1)}, bf16[128,2048]{1,0:T(8,128)(2,1)}) async-done(((bf16[128,2048]{1,0:T(8,128)(2,1)}, bf16[128,2048]{1,0:T(8,128)(2,1)}), (bf16[128,2048]{1,0:T(8,128)(2,1)}, bf16[128,2048]{1,0:T(8,128)(2,1)})) %all-reduce.20.cloned.1.call-update) | async-done | bytes 1048592 | tf_op jit(solution)/shard_map/psum | solution.py:410
  1846.0 37.4 %all-reduce.10 = (bf16[2048]{0:T(1024)(128)(2,1)S(1)}, bf16[2048]{0:T(1024)(128)(2,1)S(1)}, bf16[2048]{0:T(1024)(128)(2,1)S(1)}) all-reduce(bf16[2048]{0:T(1024)(128)(2,1)S(1)} %add_convert_fusion.8, bf16[2048]{0:T(1024)(128)(2,1)S(1)} %add_convert_fusion.7, ...), channel_id=2, replica_groups=mesh['expert'=8,'tensor'=4] {'expert'}, use_global_device_ids=true, to_apply=%region_56.57.clone | all-reduce | flops 6144 | bytes 24576
  1889.1 27.1 %reduce-scatter.12.cloned.1.call-done = bf16[512,256]{1,0:T(8,128)(2,1)} async-done(((bf16[512,2048]{1,0:T(8,128)(2,1)}), bf16[512,256]{1,0:T(8,128)(2,1)}) %reduce-scatter.12.cloned.1.call-update) | async-done | bytes 262160 | tf_op jit(solution)/shard_map/reduce_scatter | solution.py:436
  1918.0 119.1 %reduce-scatter.10.cloned.1.call-done = bf16[256,3,512]{2,0,1:T(8,128)(2,1)} async-done(((bf16[2048,3,512]{2,0,1:T(8,128)(2,1)}), bf16[256,3,512]{2,0,1:T(8,128)(2,1)}) %reduce-scatter.10.cloned.1.call-update) | async-done | bytes 786448 | tf_op jit(solution)/shard_map/reduce_scatter | solution.py:424
  (593 shorter events, 440.0 us)
Async XLA Ops:
  7.2 444.0 %copy-start = (bf16[1,352,2048]{2,1,0:T(8,128)(2,1)S(1)}, bf16[1,352,2048]{2,1,0:T(8,128)(2,1)}, u32[]{:S(2)}) copy-start(bf16[1,352,2048]{2,1,0:T(8,128)(2,1)} %param.40) | copy-start | bytes 4325380
  7.2 107.2 %all-gather.10.cloned.1.call-start = ((), (), s32[]{:S(2)}) async-start(), calls=%async_computation.15 | async-start | bytes 7077888 | tf_op jit(solution)/shard_map/all_gather | solution.py:104
  9.7 155.2 %all-gather.12.cloned.1.call-start = ((), (), s32[]{:S(2)}) async-start(), calls=%async_computation.16 | async-start | bytes 2359296 | tf_op jit(solution)/shard_map/all_gather | solution.py:106
  10.5 239.1 %all-reduce.18.cloned.1.call-start = ((), (), s32[]{:S(2)}) async-start(), calls=%async_computation.28 | async-start | bytes 4194304 | tf_op jit(solution)/shard_map/psum | solution.py:175
  266.8 50.7 %all-to-all-start.4 = ((bf16[8,80,2048]{2,1,0:T(8,128)(2,1)}), bf16[8,80,2048]{2,1,0:T(8,128)(2,1)}, u32[]{:S(2)}, u32[]{:S(2)}) async-start(bf16[8,80,2048]{2,1,0:T(8,128)(2,1)} %bitcast.386), calls=%async_computation.4 | async-start | bytes 5242880 | tf_op jit(solution)/shard_map/all_to_all | solution.py:307
  317.5 59.2 %all-to-all-start = ((bf16[8,80,2048]{2,1,0:T(8,128)(2,1)}), bf16[8,80,2048]{2,1,0:T(8,128)(2,1)}, u32[]{:S(2)}, u32[]{:S(2)}) async-start(bf16[8,80,2048]{2,1,0:T(8,128)(2,1)} %bitcast.383), calls=%async_computation | async-start | bytes 5242880 | tf_op jit(solution)/shard_map/all_to_all | solution.py:203
  376.7 63.2 %all-to-all-start.6 = ((bf16[8,80,2048]{2,1,0:T(8,128)(2,1)}), bf16[8,80,2048]{2,1,0:T(8,128)(2,1)}, u32[]{:S(2)}, u32[]{:S(2)}) async-start(bf16[8,80,2048]{2,1,0:T(8,128)(2,1)} %bitcast.385), calls=%async_computation.6 | async-start | bytes 5242880 | tf_op jit(solution)/shard_map/all_to_all | solution.py:307
  439.9 63.6 %all-to-all-start.2 = ((bf16[8,80,2048]{2,1,0:T(8,128)(2,1)}), bf16[8,80,2048]{2,1,0:T(8,128)(2,1)}, u32[]{:S(2)}, u32[]{:S(2)}) async-start(bf16[8,80,2048]{2,1,0:T(8,128)(2,1)} %bitcast.384), calls=%async_computation.2 | async-start | bytes 5242880 | tf_op jit(solution)/shard_map/all_to_all | solution.py:203
  503.4 189.3 %all-to-all-start.5 = ((f32[8,80,2048]{2,1,0:T(8,128)}), f32[8,80,2048]{2,1,0:T(8,128)}, u32[]{:S(2)}, u32[]{:S(2)}) async-start(f32[8,80,2048]{2,1,0:T(8,128)} %bitcast.381), calls=%async_computation.5 | async-start | bytes 10485760 | tf_op jit(solution)/shard_map/all_to_all | solution.py:325
  508.1 563.6 %all-gather.14.cloned.1.call-start = ((), (), s32[]{:S(2)}) async-start(), calls=%async_computation.17 | async-start | bytes 6488064 | tf_op jit(solution)/shard_map/all_gather | solution.py:110
  692.7 189.0 %all-to-all-start.1 = ((f32[8,80,2048]{2,1,0:T(8,128)}), f32[8,80,2048]{2,1,0:T(8,128)}, u32[]{:S(2)}, u32[]{:S(2)}) async-start(f32[8,80,2048]{2,1,0:T(8,128)} %fusion.28), calls=%async_computation.1 | async-start | bytes 10485760 | tf_op jit(solution)/shard_map/all_to_all | solution.py:211
  697.4 378.8 %all-gather.16.cloned.1.call-start = ((), (), s32[]{:S(2)}) async-start(), calls=%async_computation.18 | async-start | bytes 6488064 | tf_op jit(solution)/shard_map/all_gather | solution.py:111
  881.7 184.2 %all-to-all-start.7 = ((f32[8,80,2048]{2,1,0:T(8,128)}), f32[8,80,2048]{2,1,0:T(8,128)}, u32[]{:S(2)}, u32[]{:S(2)}) async-start(f32[8,80,2048]{2,1,0:T(8,128)} %bitcast.382), calls=%async_computation.7 | async-start | bytes 10485760 | tf_op jit(solution)/shard_map/all_to_all | solution.py:325
  886.4 194.4 %all-gather.18.cloned.1.call-start = ((), (), s32[]{:S(2)}) async-start(), calls=%async_computation.19 | async-start | bytes 6488064 | tf_op jit(solution)/shard_map/all_gather | solution.py:112
  1066.0 117.1 %all-to-all-start.3 = ((f32[8,80,2048]{2,1,0:T(8,128)}), f32[8,80,2048]{2,1,0:T(8,128)}, u32[]{:S(2)}, u32[]{:S(2)}) async-start(f32[8,80,2048]{2,1,0:T(8,128)} %fusion.26), calls=%async_computation.3 | async-start | bytes 10485760 | tf_op jit(solution)/shard_map/all_to_all | solution.py:211
  1070.6 273.2 %all-reduce.16.cloned.1.call-start = ((), (), s32[]{:S(2)}) async-start(), calls=%async_computation.27 | async-start | bytes 12582912 | tf_op jit(solution)/shard_map/psum | solution.py:215
  1223.4 235.1 %reduce-scatter.20.cloned.1.call-start = ((), (), s32[]{:S(2)}) async-start(), calls=%async_computation.25 | async-start | bytes 6488064 | tf_op jit(solution)/shard_map/reduce_scatter | solution.py:460
  1230.2 342.1 %reduce-scatter.16.cloned.1.call-start = ((), (), s32[]{:S(2)}) async-start(), calls=%async_computation.23 | async-start | bytes 6488064 | tf_op jit(solution)/shard_map/reduce_scatter | solution.py:454
  1237.1 449.0 %reduce-scatter.18.cloned.1.call-start = ((), (), s32[]{:S(2)}) async-start(), calls=%async_computation.24 | async-start | bytes 6488064 | tf_op jit(solution)/shard_map/reduce_scatter | solution.py:457
  1244.2 506.2 %reduce-scatter.22.cloned.1.call-start = ((), (), s32[]{:S(2)}) async-start(), calls=%async_computation.26 | async-start | bytes 147456
  1368.1 438.3 %reduce-scatter.14.cloned.1.call-start = ((), (), s32[]{:S(2)}) async-start(), calls=%async_computation.22 | async-start | bytes 36864 | tf_op jit(solution)/shard_map/reduce_scatter | solution.py:442
  1369.6 474.5 %all-reduce.20.cloned.1.call-start = ((), (), s32[]{:S(2)}) async-start(), calls=%async_computation.29 | async-start | bytes 2097152 | tf_op jit(solution)/shard_map/psum | solution.py:410
  1374.3 541.9 %reduce-scatter.12.cloned.1.call-start = ((), (), s32[]{:S(2)}) async-start(), calls=%async_computation.21 | async-start | bytes 2359296 | tf_op jit(solution)/shard_map/reduce_scatter | solution.py:436
  1377.3 659.8 %reduce-scatter.10.cloned.1.call-start = ((), (), s32[]{:S(2)}) async-start(), calls=%async_computation.20 | async-start | bytes 7077888 | tf_op jit(solution)/shard_map/reduce_scatter | solution.py:424
  (144 other events, 5515.3 us)
Sparse Core Ops, SparseCore 0:
  10.7 103.7 all-gather.9
  116.5 48.3 all-gather.11
  170.7 49.7 all-reduce.17
  511.0 178.2 all-gather.13
  700.4 177.9 all-gather.15
  889.2 182.4 all-gather.17
  1223.5 120.2 all-reduce.15
  1347.9 110.5 reduce-scatter.19
  1462.6 109.7 reduce-scatter.15
  1576.3 109.7 reduce-scatter.17
  1689.8 60.6 reduce-scatter.21
  1753.7 52.5 reduce-scatter.13
  1808.9 35.1 all-reduce.19
  1847.5 68.6 reduce-scatter.11
  1919.6 117.3 reduce-scatter.9
where the time goes:
time: 2060 us; the launch traced here: 2050 us
  waiting for transfers between devices  1470 us (71%)
  matrix products  175 us (8%)
  blocking collectives  149 us (7%)
  local copies, waits for them, and re-layouts  134 us (7%)
  other arithmetic  65.3 us (3%)
  starting transfers between devices  37.9 us (2%)
    all_to_all x2, waiting for transfers between devices, shards(): lax.all_to_all(row_grad.reshape(expert_count, capacity, model_width), 'ex...  355 us
    all_to_all x2, waiting for transfers between devices, shards(): lax.all_to_all(expert_rows, 'expert', split_axis=0, concat_axis=0, tiled=...  205 us
    reduce_scatter x1, waiting for transfers between devices, shards(): lax.psum_scatter(grad_project.reshape(model_width, 3, local_width).astype...  119 us
    reduce_scatter x1, waiting for transfers between devices, shards(): lax.psum_scatter(grad_shared_gate.astype(jnp.bfloat16), 'expert', scatter...  112 us
    reduce_scatter x1, waiting for transfers between devices, shards(): lax.psum_scatter(grad_shared_up.astype(jnp.bfloat16), 'expert', scatter_d...  111 us
    all_to_all x2, waiting for transfers between devices, shards(): lax.all_to_all(outgoing_grad, 'expert', split_axis=0, concat_axis=0, tile...  96.8 us
    psum x1, waiting for transfers between devices, shards(): shared_out, routed_full = lax.psum((shared_part, routed), 'tensor')  91.7 us
    all_to_all x2, waiting for transfers between devices, shards(): lax.all_to_all(outgoing, 'expert', split_axis=0, concat_axis=0, tiled=True)  71.7 us
  transfers between devices with their start and end apart: 23, of which 19 were waited for; matrix products, arithmetic and copies ran while one was open for 15% of the time, Pallas kernels for 0%

commit v1 on v0

--- a/solution.py
+++ b/solution.py
@@ -1,7 +1,7 @@
 import jax
 import jax.numpy as jnp
 from jax import lax
-from jax.sharding import PartitionSpec as P
+from jax.sharding import Mesh, PartitionSpec as P
 
 HD = 128
 SEG = 32
@@ -73,7 +73,7 @@
     return expanded & (token_ids[None, :] <= token_ids[:, None])
 
 
-def shards(
+def gathered_shards(
     layer_input,
     positions,
     parents,
@@ -480,47 +480,418 @@
     )
 
 
-def solution(mesh):
+AXES = ("z", "x", "y", "c")
+CHIPS = ("z", "x", "y")
+
+
+def gather_chips(rows):
+    return lax.all_gather(rows, CHIPS, axis=0, tiled=True)
+
+
+def scatter_chips(rows):
+    return lax.psum_scatter(rows, CHIPS, scatter_dimension=0, tiled=True)
+
+
+def tree_masks(parent_rows, seg_len):
+    tree_count, segment_count = parent_rows.shape
+    segment_ids = jnp.arange(segment_count, dtype=jnp.int32)
+    step_matrix = (
+        (parent_rows[:, :, None] == segment_ids) & (segment_ids[:, None] > 0)
+    )
+    reached = jnp.broadcast_to(jnp.eye(segment_count, dtype=bool), step_matrix.shape)
+    for _ in range(segment_count):
+        reached = jnp.eye(segment_count, dtype=bool) | jnp.any(
+            step_matrix[:, :, :, None] & reached[:, None, :, :], 2
+        )
+    expanded = jnp.repeat(jnp.repeat(reached, seg_len, 1), seg_len, 2)
+    token_ids = jnp.arange(segment_count * seg_len, dtype=jnp.int32)
+    return expanded & (token_ids[None, :] <= token_ids[:, None])
+
+
+def turn(rows):
+    half = rows.shape[-1] // 2
+    return jnp.concatenate([-rows[..., half:], rows[..., :half]], -1)
+
+
+def turn_back(rows):
+    half = rows.shape[-1] // 2
+    return jnp.concatenate([rows[..., half:], -rows[..., :half]], -1)
+
+
+def chip_shards(
+    layer_input,
+    positions,
+    parents,
+    routes,
+    route_slots,
+    norm1_gain,
+    project_weight,
+    project_bias,
+    output_weight,
+    norm2_gain,
+    router_weight,
+    shared_vector,
+    shared_gate,
+    shared_up,
+    shared_down,
+    expert_gate,
+    expert_up,
+    expert_down,
+    cotangent,
+):
+    f32, bf16 = jnp.float32, jnp.bfloat16
+    micro_count, seq_rows, model_width = layer_input.shape
+    top_count = routes.shape[2]
+    expert_count = router_weight.shape[1]
+    capacity = seq_rows * top_count * 5 // (4 * expert_count)
+    z, x, y, c = [lax.axis_index(a) for a in AXES]
+    here = z * 2 + x
+    trees = expert_count
+    tokens = trees * seq_rows
+    own_rows = seq_rows // 2
+    slice_rows = norm1_gain.shape[0]
+    score_scale = HD ** (-0.5)
+
+    def own(array):
+        return lax.dynamic_slice(
+            array, (c, y * own_rows, 0), (1, own_rows, model_width)
+        )[0]
+
+    own_input = own(layer_input)
+    own_cotangent = own(cotangent)
+
+    def mine(array):
+        return lax.dynamic_index_in_dim(array, c, 0, keepdims=False).astype(bf16).reshape(-1)
+
+    pieces = [
+        norm1_gain,
+        norm2_gain,
+        shared_vector,
+        router_weight.T.reshape(-1),
+        project_bias.reshape(-1),
+        mine(positions),
+        mine(parents),
+        mine(routes),
+        mine(route_slots),
+    ]
+    sizes = [p.shape[0] for p in pieces]
+    small = lax.all_gather(jnp.concatenate(pieces), AXES, axis=0, tiled=False)
+    small = small.reshape(trees, 2, 2, -1)
+    starts = [sum(sizes[:i]) for i in range(len(sizes))]
+
+    def part(i):
+        return small[..., starts[i] : starts[i] + sizes[i]]
+
+    gain_one = part(0)[:, 0, 0].reshape(-1).astype(f32)
+    gain_two = part(1)[:, 0, 0].reshape(-1).astype(f32)
+    vector_full = part(2)[:, 0, 0].reshape(-1)
+    router_full = (
+        part(3)[:, 0, 0]
+        .reshape(trees, expert_count, slice_rows)
+        .transpose(1, 0, 2)
+        .reshape(expert_count, model_width)
+    )
+    small_weights = jnp.concatenate([router_full, vector_full[None]], 0)
+    bias_full = part(4).reshape(trees, 4, 3, -1).transpose(2, 1, 0, 3).reshape(3, -1)
+    head = y * trees + here
+    bias_head = lax.dynamic_slice(bias_full, (0, head * HD), (3, HD)).astype(f32)
+
+    def by_tree(i):
+        return lax.dynamic_index_in_dim(part(i)[:, 0], c, 1, keepdims=False)
+
+    all_positions = by_tree(5).reshape(-1).astype(f32)
+    all_parents = by_tree(6).astype(jnp.int32)
+    all_routes = by_tree(7).reshape(tokens, top_count).astype(jnp.int32)
+    all_slots = by_tree(8).reshape(tokens, top_count).astype(jnp.int32)
+
+    local_heads = project_weight.shape[2] // HD
+    half_rows = slice_rows // 2
+
+    def swap_cores(array):
+        return lax.all_to_all(array, "c", split_axis=0, concat_axis=0, tiled=True)
+
+    def swap_chips(array):
+        return lax.all_to_all(array, ("z", "x"), split_axis=0, concat_axis=0, tiled=True)
+
+    def join_cores(array, axis):
+        return lax.all_gather(array, "c", axis=axis, tiled=True)
+
+    send = project_weight.transpose(1, 0, 2).reshape(3, 2, half_rows, local_heads, HD)
+    send = send.transpose(1, 3, 0, 2, 4)
+    send = swap_cores(send).reshape(2 * local_heads, 3, half_rows, HD)
+    got = swap_chips(send)
+    got = join_cores(got.transpose(1, 0, 2, 3)[:, :, None], 2)
+    project_head = got.reshape(3, model_width, HD)
+    send = output_weight.reshape(local_heads, HD, 2, half_rows).transpose(2, 0, 1, 3)
+    send = swap_cores(send).reshape(2 * local_heads, HD, half_rows)
+    got = swap_chips(send)
+    got = join_cores(got.transpose(1, 0, 2)[:, :, None], 2)
+    output_head = got.reshape(HD, model_width)
+
+    sub = shared_down.shape[0] // trees
+    send = jnp.stack(
+        [shared_gate.T.reshape(trees, sub, -1), shared_up.T.reshape(trees, sub, -1), shared_down.reshape(trees, sub, -1)],
+        1,
+    )
+    got = swap_chips(send).transpose(1, 2, 0, 3).reshape(3, sub, model_width)
+    shared_three = join_cores(got, 1)
+    expert_three = join_cores(jnp.stack([expert_gate[0].T, expert_up[0].T, expert_down[0]]), 1)
+    routed_units = expert_three.shape[1]
+    shared_units = shared_three.shape[1]
+    three = jnp.concatenate([expert_three, shared_three], 1)
+    gate_rows, up_rows, down_rows = three[0], three[1], three[2]
+
+    all_input = gather_chips(own_input).astype(f32)
+    all_cotangent = gather_chips(own_cotangent)
+    norm_one = lax.rsqrt(jnp.mean(all_input * all_input, -1, keepdims=True) + EPSILON)
+    normed_one = (all_input * norm_one * gain_one).astype(bf16)
+    half_size = HD // 2
+    inverse = ROPE_BASE ** (-(jnp.arange(half_size, dtype=f32) * 2.0 / HD))
+    angles = all_positions[:, None] * inverse[None, :]
+    cosine = jnp.cos(angles)
+    sine = jnp.sin(angles)
+    cosine = jnp.concatenate([cosine, cosine], 1)
+    sine = jnp.concatenate([sine, sine], 1)
+    raw = [product(normed_one, project_head[i]) + bias_head[i] for i in range(3)]
+    tree_shape = (trees, seq_rows, HD)
+    queries = (raw[0] * cosine + turn(raw[0]) * sine).astype(bf16).reshape(tree_shape)
+    key_rows = (raw[1] * cosine + turn(raw[1]) * sine).astype(bf16).reshape(tree_shape)
+    values = raw[2].astype(bf16).reshape(tree_shape)
+    allowed = tree_masks(all_parents, SEG)
+    scores = (
+        jnp.einsum("tqd,tkd->tqk", queries, key_rows, preferred_element_type=f32)
+        * score_scale
+    )
+    masked = jnp.where(allowed, scores, -1e30)
+    highest = jnp.max(masked, -1, keepdims=True)
+    exponent = jnp.exp(masked - highest)
+    attention_probs = exponent / jnp.sum(exponent, -1, keepdims=True)
+    probs_low = attention_probs.astype(bf16)
+    heads_out = (
+        jnp.einsum("tqk,tkd->tqd", probs_low, values, preferred_element_type=f32)
+        .astype(bf16)
+        .reshape(tokens, HD)
+    )
+    attention = scatter_chips(product(heads_out, output_head).astype(bf16)).astype(f32)
+    own_rows_in = own_input.astype(f32)
+    own_norm_one = lax.rsqrt(jnp.mean(own_rows_in * own_rows_in, -1, keepdims=True) + EPSILON)
+    hidden_state = own_rows_in + attention
+    norm_two = lax.rsqrt(jnp.mean(hidden_state * hidden_state, -1, keepdims=True) + EPSILON)
+    own_normed_two = (hidden_state * norm_two * gain_two).astype(bf16)
+
+    def route(rows, route_rows):
+        logits = product_right(small_weights, rows)
+        prob = jax.nn.softmax(logits[:expert_count], axis=0)
+        expert_ids = jnp.arange(expert_count, dtype=jnp.int32)
+        onehot = (route_rows.T[:, None, :] == expert_ids[None, :, None]).astype(f32)
+        picked_sum = jnp.sum(jnp.sum(onehot, 0) * prob, 0, keepdims=True)
+        scale = jax.nn.sigmoid(logits[expert_count])
+        return prob, onehot, picked_sum, scale
+
+    normed_two = gather_chips(own_normed_two)
+    prob, onehot, picked_sum, shared_scale = route(normed_two, all_routes)
+    kept = (all_slots.T < capacity).astype(f32)
+    gates = jnp.sum(onehot * kept[:, None, :], 0) * prob / picked_sum
+    gate_here = lax.dynamic_index_in_dim(gates, here, 0, keepdims=False)
+
+    scales = jnp.concatenate(
+        [
+            jnp.broadcast_to(gate_here, (routed_units, tokens)),
+            jnp.broadcast_to(shared_scale, (shared_units, tokens)),
+        ],
+        0,
+    )
+    gate_units = product_right(gate_rows, normed_two)
+    up_units = product_right(up_rows, normed_two)
+    grad_units = product_right(down_rows, all_cotangent)
+    sigmoid = jax.nn.sigmoid(gate_units)
+    active = gate_units * sigmoid
+    hidden = active * up_units
+    both = hidden * grad_units
+    expert_dot = jnp.sum(both[:routed_units], 0)
+    shared_dot = jnp.sum(both[routed_units:], 0)
+    scaled_hidden = (hidden * scales).astype(bf16)
+    hidden_grad = grad_units * scales
+    gate_grad = (
+        hidden_grad * up_units * (sigmoid * (1.0 + gate_units * (1.0 - sigmoid)))
+    ).astype(bf16)
+    up_grad = (hidden_grad * active).astype(bf16)
+    ffn_part = product_left(scaled_hidden, down_rows).astype(bf16)
+    normed_part = (product_left(gate_grad, gate_rows) + product_left(up_grad, up_rows)).astype(bf16)
+    dots = jnp.where(jnp.arange(expert_count)[:, None] == here, expert_dot, 0.0)
+    dots = jnp.concatenate([dots, shared_dot[None]], 0)
+    ffn_out = scatter_chips(ffn_part).astype(f32)
+    own_output = (hidden_state + ffn_out).astype(bf16)
+    normed_sum = scatter_chips(normed_part).astype(f32)
+    all_dots = lax.psum(dots, CHIPS)
+    three_grad = jnp.stack(
+        [product(gate_grad, normed_two), product(up_grad, normed_two), product(scaled_hidden, all_cotangent)]
+    ).astype(bf16)
+
+    valid_gate = jnp.sum(onehot * kept[:, None, :], 0)
+    every_gate = jnp.sum(onehot, 0) * prob / picked_sum
+    kept_dots = all_dots[:expert_count] * valid_gate
+    picked_grad = (kept_dots - jnp.sum(kept_dots * every_gate, 0, keepdims=True)) / picked_sum
+    prob_grad = picked_grad * jnp.sum(onehot, 0)
+    logit_grad = prob * (prob_grad - jnp.sum(prob * prob_grad, 0, keepdims=True))
+    scale_grad = all_dots[expert_count] * shared_scale * (1.0 - shared_scale)
+    small_grad = jnp.concatenate([logit_grad, scale_grad[None]], 0).astype(bf16)
+    first = here * seq_rows + y * own_rows
+    own_small = lax.dynamic_slice(small_grad, (0, first), (expert_count + 1, own_rows))
+    grad_small = product(own_small, own_normed_two)
+    normed_two_grad = normed_sum + product_left(own_small, small_weights)
+    upstream = own_cotangent.astype(f32)
+    grad_gain_two = jnp.sum(normed_two_grad * hidden_state * norm_two, 0)
+    scaled_two = normed_two_grad * gain_two
+    hidden_grad_rows = (
+        upstream
+        + norm_two * scaled_two
+        - hidden_state * norm_two**3 * jnp.mean(scaled_two * hidden_state, -1, keepdims=True)
+    )
+    attention_grad = gather_chips(hidden_grad_rows.astype(bf16))
+
+    output_grad = product_left(heads_out, attention_grad).astype(bf16)
+    heads_grad = product_right(attention_grad, output_head).astype(bf16).reshape(tree_shape)
+    value_grad = jnp.einsum("tqk,tqd->tkd", probs_low, heads_grad, preferred_element_type=f32)
+    prob_grads = jnp.einsum("tqd,tkd->tqk", heads_grad, values, preferred_element_type=f32)
+    score_grad = (
+        attention_probs
+        * (prob_grads - jnp.sum(attention_probs * prob_grads, -1, keepdims=True))
+    ).astype(bf16)
+    query_grad = jnp.einsum("tqk,tkd->tqd", score_grad, key_rows, preferred_element_type=f32)
+    key_grad = jnp.einsum("tqk,tqd->tkd", score_grad, queries, preferred_element_type=f32)
+    query_grad = (query_grad * score_scale).reshape(tokens, HD)
+    key_grad = (key_grad * score_scale).reshape(tokens, HD)
+    query_grad = query_grad * cosine + turn_back(query_grad * sine)
+    key_grad = key_grad * cosine + turn_back(key_grad * sine)
+    raw_grads = [g.astype(bf16) for g in (query_grad, key_grad, value_grad.reshape(tokens, HD))]
+    bias_grad = jnp.stack([jnp.sum(g.astype(f32), 0) for g in raw_grads])
+    project_grad = jnp.stack([product_left(normed_one, g) for g in raw_grads]).astype(bf16)
+    normed_part = sum(product_right(g, project_head[i]) for i, g in enumerate(raw_grads))
+    normed_one_grad = scatter_chips(normed_part.astype(bf16)).astype(f32)
+    grad_gain_one = jnp.sum(normed_one_grad * own_rows_in * own_norm_one, 0)
+    scaled_one = normed_one_grad * gain_one
+    own_grad = (
+        hidden_grad_rows
+        + own_norm_one * scaled_one
+        - own_rows_in * own_norm_one**3 * jnp.mean(scaled_one * own_rows_in, -1, keepdims=True)
+    )
+    layer_output = lax.all_gather(own_output, ("c", "y"), axis=0, tiled=True).reshape(micro_count, seq_rows, model_width)
+    input_grad = lax.all_gather(own_grad, ("c", "y"), axis=0, tiled=True).reshape(micro_count, seq_rows, model_width)
+
+    bias_place = lax.dynamic_update_slice(jnp.zeros((3, bias_full.shape[1]), f32), bias_grad, (0, head * HD))
+    vectors = jnp.concatenate([grad_small, grad_gain_one[None], grad_gain_two[None]], 0)
+    vectors = lax.psum(jnp.concatenate([vectors.reshape(-1), bias_place.reshape(-1)]), AXES)
+    split = (expert_count + 3) * model_width
+    bias_sum = vectors[split:].reshape(3, -1)
+    vectors = lax.dynamic_slice(vectors[:split].reshape(-1, model_width), (0, here * slice_rows), (expert_count + 3, slice_rows))
+    bias_width = project_bias.shape[1]
+    bias_out = lax.dynamic_slice(bias_sum, (0, ((y * 2 + c) * trees + here) * bias_width), (3, bias_width))
+
+    def sum_cores(array, axis):
+        return lax.psum_scatter(array, "c", scatter_dimension=axis, tiled=True)
+
+    send = project_grad.reshape(3, trees, 2, half_rows, HD)
+    send = sum_cores(send, 2).reshape(3, trees, half_rows, HD).transpose(1, 0, 2, 3)
+    got = swap_chips(send).reshape(2, local_heads, 3, half_rows, HD)
+    got = swap_cores(got).reshape(2, local_heads, 3, half_rows, HD)
+    project_out = got.transpose(0, 3, 2, 1, 4).reshape(slice_rows, 3, local_heads * HD).astype(f32)
+    send = output_grad.reshape(HD, trees, 2, half_rows)
+    send = sum_cores(send, 2).reshape(HD, trees, half_rows).transpose(1, 0, 2)
+    got = swap_chips(send).reshape(2, local_heads, HD, half_rows)
+    got = swap_cores(got).reshape(2, local_heads, HD, half_rows)
+    output_out = got.transpose(1, 2, 0, 3).reshape(local_heads * HD, slice_rows).astype(f32)
+    expert_sum = sum_cores(three_grad[:, :routed_units], 1).astype(f32)
+    shared_sum = sum_cores(three_grad[:, routed_units:], 1)
+    send = shared_sum.reshape(3, sub, trees, slice_rows).transpose(2, 0, 1, 3)
+    got = swap_chips(send).transpose(1, 0, 2, 3).reshape(3, trees * sub, slice_rows).astype(f32)
+    return (
+        layer_output,
+        input_grad,
+        vectors[expert_count + 1],
+        project_out,
+        bias_out,
+        output_out,
+        vectors[expert_count + 2],
+        vectors[:expert_count].T,
+        vectors[expert_count],
+        got[0].T,
+        got[1].T,
+        got[2],
+        expert_sum[0].T[None],
+        expert_sum[1].T[None],
+        expert_sum[2][None],
+    )
+
+
+def spread(body, mesh, rows, columns):
+    def named(*dims):
+        names = {"expert": rows, "tensor": columns, "both": (*columns, *rows), None: None}
+        return P(*(names[d] for d in dims))
+
     return jax.shard_map(
-        shards,
+        body,
         mesh=mesh,
         in_specs=(
-            P(None, "expert", None),
-            P(None, "expert"),
-            P(None, "expert", None),
-            P(None, "expert", None),
-            P(None, "expert", None),
-            P("expert"),
-            P("expert", None, "tensor"),
-            P(None, ("tensor", "expert")),
-            P("tensor", "expert"),
-            P("expert"),
-            P("expert", None),
-            P("expert"),
-            P("expert", "tensor"),
-            P("expert", "tensor"),
-            P("tensor", "expert"),
-            P("expert", None, "tensor"),
-            P("expert", None, "tensor"),
-            P("expert", "tensor", None),
-            P(None, "expert", None),
+            named(None, "expert", None),
+            named(None, "expert"),
+            named(None, "expert", None),
+            named(None, "expert", None),
+            named(None, "expert", None),
+            named("expert"),
+            named("expert", None, "tensor"),
+            named(None, "both"),
+            named("tensor", "expert"),
+            named("expert"),
+            named("expert", None),
+            named("expert"),
+            named("expert", "tensor"),
+            named("expert", "tensor"),
+            named("tensor", "expert"),
+            named("expert", None, "tensor"),
+            named("expert", None, "tensor"),
+            named("expert", "tensor", None),
+            named(None, "expert", None),
         ),
         out_specs=(
-            P(None, "expert", None),
-            P(None, "expert", None),
-            P("expert"),
-            P("expert", None, "tensor"),
-            P(None, ("tensor", "expert")),
-            P("tensor", "expert"),
-            P("expert"),
-            P("expert", None),
-            P("expert"),
-            P("expert", "tensor"),
-            P("expert", "tensor"),
-            P("tensor", "expert"),
-            P("expert", None, "tensor"),
-            P("expert", None, "tensor"),
-            P("expert", "tensor", None),
+            named(None, "expert", None),
+            named(None, "expert", None),
+            named("expert"),
+            named("expert", None, "tensor"),
+            named(None, "both"),
+            named("tensor", "expert"),
+            named("expert"),
+            named("expert", None),
+            named("expert"),
+            named("expert", "tensor"),
+            named("expert", "tensor"),
+            named("tensor", "expert"),
+            named("expert", None, "tensor"),
+            named("expert", None, "tensor"),
+            named("expert", "tensor", None),
         ),
         check_vma=False,
     )
+
+
+def solution(mesh):
+    expert_devices, tensor_devices = mesh.shape["expert"], mesh.shape["tensor"]
+
+    def layer(*arrays):
+        heads = arrays[6].shape[2] // HD
+        trees = arrays[0].shape[1] // (SEG * arrays[2].shape[2])
+        if (
+            tensor_devices == 4
+            and expert_devices % 2 == 0
+            and heads == 2 * expert_devices
+            and arrays[10].shape[1] == expert_devices
+            and trees == expert_devices
+            and arrays[0].shape[0] == 2
+        ):
+            grid = Mesh(mesh.devices.reshape(expert_devices // 2, 2, 2, 2), AXES)
+            body = spread(chip_shards, grid, ("z", "x"), ("y", "c"))
+        else:
+            body = spread(gathered_shards, mesh, ("expert",), ("tensor",))
+        return body(*arrays)
+
+    return layer

time: 2060 us -> 1250 us (0.61)
  waiting for transfers between devices: 1470 us -> 756 us
  matrix products: 175 us -> 119 us
  local copies, waits for them, and re-layouts: 134 us -> 93.5 us
  blocking collectives: 149 us -> 175 us
    all_to_all x8 -> x5, waiting for transfers between devices: 728 us -> 22.2 us  [swap_chips(): lax.all_to_all(array, ('z', 'x'), split_axis=0, concat_axis=0, tiled=True)]
    reduce_scatter x6 -> x7, waiting for transfers between devices: 464 us -> 258 us  [the longest x4 255 us: scatter_chips(): return lax.psum_scatter(rows, CHIPS, scatter_dimension=0, tiled=True)]
    all_gather x5 -> x9, waiting for transfers between devices: 85.1 us -> 224 us  [the longest x4 193 us: gather_chips(): return lax.all_gather(rows, CHIPS, axis=0, tiled=True)]
    all_gather x5 -> x1, blocking collectives: 105 us -> 2.35 us  [join_cores(): return lax.all_gather(array, 'c', axis=axis, tiled=True)]
    all_to_all x0 -> x5, blocking collectives: none -> 97.3 us  [the longest x1 80 us: swap_chips(): lax.all_to_all(array, ('z', 'x'), split_axis=0, concat_axis=0, tiled=True)]
    unnamed x16 -> x21, waiting for transfers between devices: 62.4 us -> 146 us
    gather x12 -> x0, local copies, waits for them, and re-layouts: 78.8 us -> none  [the longest x4 26.7 us: shards(): row_back.reshape(slot_total, model_width)[safe_index] * keep_mask[..., None]]
    psum x1, blocking collectives: 6.97 us -> 75 us  [chip_shards(): all_dots = lax.psum(dots, CHIPS)]
  transfers between devices with their start and end apart: 23 -> 24, of which waited for: 19 -> 15; matrix products, arithmetic and copies ran while one was open for 15% -> 14% of each run, Pallas kernels for 0% -> 0%
where the time goes in v1:
time: 1250 us; the launch traced here: 1240 us
  waiting for transfers between devices  756 us (60%)
  blocking collectives  175 us (14%)
  matrix products  119 us (10%)
  local copies, waits for them, and re-layouts  93.5 us (7%)
  other arithmetic  55 us (4%)
  starting transfers between devices  25.5 us (2%)
  between operations  17.3 us (1%)
    reduce_scatter x4, waiting for transfers between devices, scatter_chips(): return lax.psum_scatter(rows, CHIPS, scatter_dimension=0, tiled=True)  255 us
    all_gather x4, waiting for transfers between devices, gather_chips(): return lax.all_gather(rows, CHIPS, axis=0, tiled=True)  193 us
    unnamed x21, waiting for transfers between devices  146 us
    psum x1, waiting for transfers between devices, chip_shards(): lax.psum(jnp.concatenate([vectors.reshape(-1), bias_place.reshape(-1)]),...  106 us
    all_to_all x1, blocking collectives, swap_chips(): lax.all_to_all(array, ('z', 'x'), split_axis=0, concat_axis=0, tiled=True)  80 us
    psum x1, blocking collectives, chip_shards(): all_dots = lax.psum(dots, CHIPS)  75 us
    dot_general x8, matrix products, product_right(): lax.dot_general(left_side, right_side, (((1,), (1,)), ((), ())), preferre...  42.4 us
    dot_general x8, matrix products, product_left(): lax.dot_general(left_side, right_side, (((0,), (0,)), ((), ())), preferre...  37.6 us
  transfers between devices with their start and end apart: 24, of which 15 were waited for; matrix products, arithmetic and copies ran while one was open for 14% of the time, Pallas kernels for 0%

profile of v1, /device:TPU:0, one launch (start us, length us, event | category | flops | bytes accessed | tf_op | source)
XLA Modules:
  0.0 1240.9 jit_solution(16201231549749411099)
XLA Ops:
  25.0 18.8 %all-to-all-done.1 = bf16[8,3,128,128]{3,2,1,0:T(8,128)(2,1)S(1)} async-done(((bf16[8,3,128,128]{3,2,1,0:T(8,128)(2,1)}), bf16[8,3,128,128]{3,2,1,0:T(8,128)(2,1)S(1)}, u32[]{:S(2)}, u32[]{:S(2)}) %all-to-all-start.1) | async-done | bytes 786464 | tf_op jit(solution)/shard_map/all_to_all | solution.py:614
  54.7 122.9 %all-reduce.8.cloned.1.call-done = bf16[133248]{0:T(1024)(128)(2,1)} async-done(((bf16[133248]{0:T(1024)(128)(2,1)}), bf16[133248]{0:T(1024)(128)(2,1)}) %all-reduce.8.cloned.1.call-update) | async-done | bytes 266512
  216.8 80.0 %all_to_all.52 = bf16[8,3,176,256]{3,2,1,0:T(8,128)(2,1)S(1)} all-to-all(bf16[8,3,176,256]{3,2,1,0:T(8,128)(2,1)S(1)} %copy.351), channel_id=1, replica_groups=mesh['z'=4,'x'=2,'y'=2,'c'=2] {'z','x'}, dimensions={0} | all-to-all | bytes 4325376 | tf_op jit(solution)/shard_map/all_to_all | solution.py:614
  298.5 14.6 %reduce-scatter.11.cloned.1.call-done = bf16[64,2048]{1,0:T(8,128)(2,1)} async-done(((bf16[1024,2048]{1,0:T(8,128)(2,1)}), bf16[64,2048]{1,0:T(8,128)(2,1)}) %reduce-scatter.11.cloned.1.call-update) | async-done | bytes 262160 | tf_op jit(solution)/shard_map/reduce_scatter | solution.py:492
  321.7 21.8 %all-gather.15.cloned.1.call-done = bf16[3,704,2048]{2,1,0:T(8,128)(2,1)} async-done(((bf16[3,352,2048]{2,1,0:T(8,128)(2,1)}), bf16[3,704,2048]{2,1,0:T(8,128)(2,1)}) %all-gather.15.cloned.1.call-update) | async-done | bytes 8650768 | tf_op jit(solution)/shard_map/all_gather | solution.py:617
  343.5 8.5 constant_dynamic-update-slice_fusion.1
  352.0 8.6 all-gather.17.cloned.1.call-done
  365.6 75.1 %all-gather.19.cloned.1.call-done = bf16[1024,2048]{1,0:T(8,128)(2,1)} async-done(((bf16[64,2048]{1,0:T(8,128)(2,1)}), bf16[1024,2048]{1,0:T(8,128)(2,1)}) %all-gather.19.cloned.1.call-update) | async-done | bytes 4194320 | tf_op jit(solution)/shard_map/all_gather | solution.py:488
  440.7 10.3 fusion.17
  451.1 8.6 fusion.15
  459.7 59.0 %all-gather.31.cloned.1.call-done = bf16[1,1024,2048]{2,1,0:T(8,128)(2,1)} async-done(((bf16[1,64,2048]{2,1,0:T(8,128)(2,1)}), bf16[1,1024,2048]{2,1,0:T(8,128)(2,1)}) %all-gather.31.cloned.1.call-update) | async-done | bytes 4194320 | tf_op jit(solution)/shard_map/all_gather | solution.py:488
  518.7 13.1 %multiply_multiply_fusion = (f32[1056,1024]{1,0:T(8,128)S(1)}, f32[1056,1024]{1,0:T(8,128)}) fusion(f32[1056,1024]{1,0:T(8,128)} %fusion.17, f32[1056,1024]{1,0:T(8,128)} %fusion.15, bf16[1,1024,2048]{2,1,0:T(8,128)(2,1)} %all-gather.31.cloned.1.call-done, bf16[3,1056,2048]{2,1,0:T(8,128)(2,1)} %constant_dynamic-update-slice_fusion), kind=kOutput, calls=%fused_computation.47 | convolution fusion | flops 4435673088 | bytes 25821184 | tf_op jit(solution)/shard_map/dot_general | solution.py:25
  535.3 75.0 %psum.14 = f32[9,1024]{1,0:T(8,128)S(1)} all-reduce(f32[9,1024]{1,0:T(8,128)S(1)} %pad_maximum_fusion.13), channel_id=1, replica_groups=mesh['z'=4,'x'=2,'y'=2,'c'=2] {'z','x','y'}, use_global_device_ids=true, to_apply=%region_18.19 | all-reduce | flops 9216 | bytes 73728 | tf_op jit(solution)/shard_map/psum | solution.py:726
  619.8 7.9 fusion.14
  627.7 9.5 add_convert_fusion.1
  637.4 91.5 %reduce-scatter.15.cloned.1.call-done = bf16[64,2048]{1,0:T(8,128)(2,1)} async-done(((bf16[1024,2048]{1,0:T(8,128)(2,1)}), bf16[64,2048]{1,0:T(8,128)(2,1)}) %reduce-scatter.15.cloned.1.call-update) | async-done | bytes 262160 | tf_op jit(solution)/shard_map/reduce_scatter | solution.py:492
  732.8 9.6 fusion.5
  748.8 59.0 %all-gather.23.cloned.1.call-done = bf16[1024,2048]{1,0:T(8,128)(2,1)} async-done(((bf16[64,2048]{1,0:T(8,128)(2,1)}), bf16[1024,2048]{1,0:T(8,128)(2,1)}) %all-gather.23.cloned.1.call-update) | async-done | bytes 4194320 | tf_op jit(solution)/shard_map/all_gather | solution.py:488
  841.6 9.5 fusion.19
  870.7 8.3 pad_maximum_fusion
  889.6 48.5 %reduce-scatter.17.cloned.1.call-done = bf16[64,2048]{1,0:T(8,128)(2,1)} async-done(((bf16[1024,2048]{1,0:T(8,128)(2,1)}), bf16[64,2048]{1,0:T(8,128)(2,1)}) %reduce-scatter.17.cloned.1.call-update) | async-done | bytes 262160 | tf_op jit(solution)/shard_map/reduce_scatter | solution.py:492
  948.5 100.1 %reduce-scatter.13.cloned.1.call-done = bf16[64,2048]{1,0:T(8,128)(2,1)} async-done(((bf16[1024,2048]{1,0:T(8,128)(2,1)}), bf16[64,2048]{1,0:T(8,128)(2,1)}) %reduce-scatter.13.cloned.1.call-update) | async-done | bytes 262160 | tf_op jit(solution)/shard_map/reduce_scatter | solution.py:492
  1054.4 21.9 %all-reduce.10.cloned.1.call-done = bf16[3,8,2,128,128]{4,3,2,1,0:T(8,128)(2,1)} async-done(((bf16[3,8,2,128,128]{4,3,2,1,0:T(8,128)(2,1)}), bf16[3,8,2,128,128]{4,3,2,1,0:T(8,128)(2,1)}) %all-reduce.10.cloned.1.call-update) | async-done | bytes 1572880
  1118.0 106.3 %all-reduce.6.cloned.1.call-done = f32[28672]{0:T(1024)} async-done(((f32[28672]{0:T(1024)}), f32[28672]{0:T(1024)}) %all-reduce.6.cloned.1.call-update) | async-done | bytes 114704 | tf_op jit(solution)/shard_map/psum | solution.py:784
  (352 shorter events, 235.0 us)
Async XLA Ops:
  15.6 28.1 %all-to-all-start.1 = ((bf16[8,3,128,128]{3,2,1,0:T(8,128)(2,1)}), bf16[8,3,128,128]{3,2,1,0:T(8,128)(2,1)S(1)}, u32[]{:S(2)}, u32[]{:S(2)}) async-start(bf16[8,3,128,128]{3,2,1,0:T(8,128)(2,1)} %bitcast.11), calls=%async_computation.1 | async-start | bytes 1572864 | tf_op jit(solution)/shard_map/all_to_all | solution.py:614
  22.9 154.8 %all-reduce.8.cloned.1.call-start = ((), (), s32[]{:S(2)}) async-start(), calls=%async_computation.34 | async-start | bytes 536576
  24.9 159.3 %all-gather.29.cloned.1.call-start = ((), (), s32[]{:S(2)}) async-start(), calls=%async_computation.32 | async-start | bytes 2359296 | tf_op jit(solution)/shard_map/all_gather | solution.py:617
  44.6 141.2 %all-gather.27.cloned.1.call-start = ((), (), s32[]{:S(2)}) async-start(), calls=%async_computation.31 | async-start | bytes 4456448 | tf_op jit(solution)/shard_map/all_gather | solution.py:488
  51.2 130.3 %all-to-all-start.3 = ((bf16[8,128,128]{2,1,0:T(8,128)(2,1)}), bf16[8,128,128]{2,1,0:T(8,128)(2,1)S(1)}, u32[]{:S(2)}, u32[]{:S(2)}) async-start(bf16[8,128,128]{2,1,0:T(8,128)(2,1)} %bitcast.24), calls=%async_computation.3 | async-start | bytes 524288 | tf_op jit(solution)/shard_map/all_to_all | solution.py:614
  54.6 258.5 %reduce-scatter.11.cloned.1.call-start = ((), (), s32[]{:S(2)}) async-start(), calls=%async_computation.17 | async-start | bytes 4456448 | tf_op jit(solution)/shard_map/reduce_scatter | solution.py:492
  207.5 135.9 %all-gather.15.cloned.1.call-start = ((), (), s32[]{:S(2)}) async-start(), calls=%async_computation.18 | async-start | bytes 12976128 | tf_op jit(solution)/shard_map/all_gather | solution.py:617
  212.5 148.1 %all-gather.17.cloned.1.call-start = ((), (), s32[]{:S(2)}) async-start(), calls=%async_computation.19 | async-start | bytes 6488064 | tf_op jit(solution)/shard_map/all_gather | solution.py:617
  298.4 142.3 %all-gather.19.cloned.1.call-start = ((), (), s32[]{:S(2)}) async-start(), calls=%async_computation.20 | async-start | bytes 4456448 | tf_op jit(solution)/shard_map/all_gather | solution.py:488
  316.1 202.6 %all-gather.31.cloned.1.call-start = ((), (), s32[]{:S(2)}) async-start(), calls=%async_computation.33 | async-start | bytes 4456448 | tf_op jit(solution)/shard_map/all_gather | solution.py:488
  317.8 411.0 %reduce-scatter.15.cloned.1.call-start = ((), (), s32[]{:S(2)}) async-start(), calls=%async_computation.23 | async-start | bytes 4456448 | tf_op jit(solution)/shard_map/reduce_scatter | solution.py:492
  637.2 170.6 %all-gather.23.cloned.1.call-start = ((), (), s32[]{:S(2)}) async-start(), calls=%async_computation.24 | async-start | bytes 4456448 | tf_op jit(solution)/shard_map/all_gather | solution.py:488
  732.7 148.1 %reduce-scatter.19.cloned.1.call-start = ((), (), s32[]{:S(2)}) async-start(), calls=%async_computation.28 | async-start | bytes 786432 | tf_op jit(solution)/shard_map/reduce_scatter | solution.py:792
  813.9 72.6 %reduce-scatter.21.cloned.1.call-start = ((), (), s32[]{:S(2)}) async-start(), calls=%async_computation.29 | async-start | bytes 6488064 | tf_op jit(solution)/shard_map/reduce_scatter | solution.py:792
  827.1 111.0 %reduce-scatter.17.cloned.1.call-start = ((), (), s32[]{:S(2)}) async-start(), calls=%async_computation.25 | async-start | bytes 4456448 | tf_op jit(solution)/shard_map/reduce_scatter | solution.py:492
  841.6 207.1 %reduce-scatter.13.cloned.1.call-start = ((), (), s32[]{:S(2)}) async-start(), calls=%async_computation.21 | async-start | bytes 4456448 | tf_op jit(solution)/shard_map/reduce_scatter | solution.py:492
  851.1 225.2 %all-reduce.10.cloned.1.call-start = ((), (), s32[]{:S(2)}) async-start(), calls=%async_computation.35 | async-start | bytes 3145728
  870.6 226.3 %reduce-scatter.23.cloned.1.call-start = ((), (), s32[]{:S(2)}) async-start(), calls=%async_computation.30 | async-start | bytes 12976128 | tf_op jit(solution)/shard_map/reduce_scatter | solution.py:792
  882.5 56.8 %all-to-all-start.7 = ((bf16[8,128,128]{2,1,0:T(8,128)(2,1)}), bf16[8,128,128]{2,1,0:T(8,128)(2,1)S(1)}, u32[]{:S(2)}, u32[]{:S(2)}) async-start(bf16[8,128,128]{2,1,0:T(8,128)(2,1)} %copy.375), calls=%async_computation.12 | async-start | bytes 524288 | tf_op jit(solution)/shard_map/all_to_all | solution.py:614
  940.1 139.1 %all-to-all-start.9 = ((bf16[8,3,176,256]{3,2,1,0:T(8,128)(2,1)}), bf16[8,3,176,256]{3,2,1,0:T(8,128)(2,1)S(1)}, u32[]{:S(2)}, u32[]{:S(2)}) async-start(bf16[8,3,176,256]{3,2,1,0:T(8,128)(2,1)} %bitcast.312), calls=%async_computation.15 | async-start | bytes 4325376 | tf_op jit(solution)/shard_map/all_to_all | solution.py:614
  943.7 280.6 %all-reduce.6.cloned.1.call-start = ((), (), s32[]{:S(2)}) async-start(), calls=%async_computation.27 | async-start | bytes 229376 | tf_op jit(solution)/shard_map/psum | solution.py:784
  948.5 279.4 %all-gather.21.cloned.1.call-start = ((), (), s32[]{:S(2)}) async-start(), calls=%async_computation.22 | async-start | bytes 1310720 | tf_op jit(solution)/shard_map/all_gather | solution.py:779
  1051.3 176.5 %all-gather.25.cloned.1.call-start = ((), (), s32[]{:S(2)}) async-start(), calls=%async_computation.26 | async-start | bytes 2621440 | tf_op jit(solution)/shard_map/all_gather | solution.py:780
  1083.1 26.3 %all-to-all-start.5 = ((bf16[8,3,128,128]{3,2,1,0:T(8,128)(2,1)}), bf16[8,3,128,128]{3,2,1,0:T(8,128)(2,1)}, u32[]{:S(2)}, u32[]{:S(2)}) async-start(bf16[8,3,128,128]{3,2,1,0:T(8,128)(2,1)} %copy.371), calls=%async_computation.9 | async-start | bytes 1572864 | tf_op jit(solution)/shard_map/all_to_all | solution.py:614
  (55 other events, 721.1 us)
Sparse Core Ops, SparseCore 0:
  29.6 147.9 all-reduce.7
  1051.4 21.2 all-gather.20
  1074.9 22.5 all-gather.24
Sparse Core Ops, SparseCore 1:
  44.7 8.6 all-gather.28
  56.9 77.2 all-gather.26
  207.6 105.4 reduce-scatter.10
  314.8 28.6 all-gather.14
  345.7 14.9 all-gather.16
  363.8 76.9 all-gather.18
  444.3 74.3 all-gather.30
  637.3 91.5 reduce-scatter.14
  732.8 75.0 all-gather.22
  814.0 6.5 reduce-scatter.18
  827.2 10.7 reduce-scatter.20
  841.6 96.4 reduce-scatter.16
  940.4 108.2 reduce-scatter.12
  1051.7 24.6 all-reduce.9
  1078.7 18.2 reduce-scatter.22
  1102.6 121.6 all-reduce.5

commit v2 on v1

--- a/solution.py
+++ b/solution.py
@@ -1,6 +1,8 @@
 import jax
 import jax.numpy as jnp
 from jax import lax
+from jax.experimental import pallas as pl
+from jax.experimental.pallas import tpu as pltpu
 from jax.sharding import Mesh, PartitionSpec as P
 
 HD = 128
@@ -481,15 +483,484 @@
 
 
 AXES = ("z", "x", "y", "c")
-CHIPS = ("z", "x", "y")
-
-
-def gather_chips(rows):
-    return lax.all_gather(rows, CHIPS, axis=0, tiled=True)
-
-
-def scatter_chips(rows):
-    return lax.psum_scatter(rows, CHIPS, scatter_dimension=0, tiled=True)
+
+
+MESH_ID = pl.DeviceIdType.MESH
+VMEM_LIMIT = 60 * 1024 * 1024
+
+
+def positions_here():
+    return tuple(lax.axis_index(a) for a in AXES)
+
+
+def planes_from(z):
+    return (z, z + 1 - 2 * (z % 2), 2 - z // 2, 3 * (1 - z // 2))
+
+
+def greet(barrier, partners):
+    for partner in partners:
+        pl.semaphore_signal(barrier, inc=1, device_id=partner, device_id_type=MESH_ID)
+    pl.semaphore_wait(barrier, len(partners))
+
+
+def near_partners(z, x, y):
+    planes = planes_from(z)
+    return [{"x": 1 - x}, {"y": 1 - y}] + [{"z": p} for p in planes[1:]]
+
+
+class Sends:
+    def __init__(self):
+        self.open = []
+
+    def start(self, source, target, send, receive, where):
+        copy = pltpu.make_async_remote_copy(
+            src_ref=source, dst_ref=target, send_sem=send, recv_sem=receive, device_id=where, device_id_type=MESH_ID
+        )
+        copy.start()
+        self.open.append(copy)
+
+    def finish(self):
+        for copy in self.open:
+            copy.wait_send()
+        self.open = []
+
+
+def arrive(buffer, receive):
+    pltpu.make_async_copy(buffer, buffer, receive).wait()
+
+
+class Gather:
+    def __init__(self, held, send, receive, cut, sends):
+        self.held, self.send, self.receive, self.sends = held, send, receive, sends
+        width = held.shape[-1]
+        self.left, self.right = pl.ds(0, cut), pl.ds(cut, width - cut)
+        self.z, self.x, self.y, _ = positions_here()
+        self.planes = planes_from(self.z)
+
+    def block(self, plane, x, y, columns=None):
+        if columns is None:
+            return self.held.at[plane, x, y]
+        return self.held.at[plane, x, y, :, columns]
+
+    def pass_on(self, plane, x, y, columns, slot, axis):
+        here = self.x if axis == "x" else self.y
+        ref = self.block(plane, x, y, columns)
+        self.sends.start(ref, ref, self.send.at[slot, plane], self.receive.at[slot, plane], {axis: 1 - here})
+
+    def begin(self):
+        own = self.block(self.z, self.x, self.y)
+        for step, plane in enumerate(self.planes[1:]):
+            self.sends.start(own, own, self.send.at[6, step], self.receive.at[6, self.z], {"z": plane})
+
+    def first(self, step):
+        plane, x, y = self.planes[step], self.x, self.y
+        if step:
+            arrive(self.block(plane, x, y), self.receive.at[6, plane])
+        self.pass_on(plane, x, y, self.left, 0, "x")
+        self.pass_on(plane, x, y, self.right, 1, "y")
+        self.pass_on(plane, x, y, self.left, 2, "y")
+        self.pass_on(plane, x, y, self.right, 3, "x")
+
+    def second(self, step):
+        plane, x, y = self.planes[step], self.x, self.y
+        arrive(self.block(plane, 1 - x, y, self.left), self.receive.at[0, plane])
+        self.pass_on(plane, 1 - x, y, self.left, 4, "y")
+        arrive(self.block(plane, x, 1 - y, self.right), self.receive.at[1, plane])
+        self.pass_on(plane, x, 1 - y, self.right, 5, "x")
+
+    def whole(self, step):
+        plane, x, y = self.planes[step], self.x, self.y
+        arrive(self.block(plane, x, 1 - y, self.left), self.receive.at[2, plane])
+        arrive(self.block(plane, 1 - x, y, self.right), self.receive.at[3, plane])
+        arrive(self.block(plane, 1 - x, 1 - y, self.left), self.receive.at[4, plane])
+        arrive(self.block(plane, 1 - x, 1 - y, self.right), self.receive.at[5, plane])
+
+    @staticmethod
+    def semaphores():
+        return [pltpu.SemaphoreType.DMA((7, 4)), pltpu.SemaphoreType.DMA((7, 4))]
+
+
+class Reduce:
+    def __init__(self, parts, buffers, cut, sends):
+        self.parts, self.sends = parts, sends
+        self.one_left, self.one_right, self.two_left, self.two_right, self.last, self.send, self.receive = buffers
+        width = parts.shape[-1]
+        self.left, self.right = pl.ds(0, cut), pl.ds(cut, width - cut)
+        self.z, self.x, self.y, _ = positions_here()
+        self.planes = planes_from(self.z)
+
+    @staticmethod
+    def buffers(rows, width, cut):
+        bf16 = jnp.bfloat16
+        return [
+            pltpu.VMEM((4, 2, rows, cut), bf16),
+            pltpu.VMEM((4, 2, rows, width - cut), bf16),
+            pltpu.VMEM((4, rows, cut), bf16),
+            pltpu.VMEM((4, rows, width - cut), bf16),
+            pltpu.VMEM((4, rows, width), bf16),
+            pltpu.SemaphoreType.DMA((5, 4)),
+            pltpu.SemaphoreType.DMA((5, 4)),
+        ]
+
+    def first(self, step):
+        plane = self.planes[step]
+        self.sends.start(
+            self.parts.at[plane, :, 1 - self.y, :, self.left], self.one_left.at[plane],
+            self.send.at[0, plane], self.receive.at[0, plane], {"y": 1 - self.y},
+        )
+        self.sends.start(
+            self.parts.at[plane, 1 - self.x, :, :, self.right], self.one_right.at[plane],
+            self.send.at[1, plane], self.receive.at[1, plane], {"x": 1 - self.x},
+        )
+
+    def add(self, ref, other):
+        ref[...] = (ref[...].astype(jnp.float32) + other[...].astype(jnp.float32)).astype(ref.dtype)
+
+    def second(self, step):
+        plane, x, y = self.planes[step], self.x, self.y
+        arrive(self.one_left.at[plane], self.receive.at[0, plane])
+        away = self.parts.at[plane, 1 - x, y, :, self.left]
+        self.add(away, self.one_left.at[plane, 1 - x])
+        self.sends.start(away, self.two_left.at[plane], self.send.at[2, plane], self.receive.at[2, plane], {"x": 1 - x})
+        arrive(self.one_right.at[plane], self.receive.at[1, plane])
+        away = self.parts.at[plane, x, 1 - y, :, self.right]
+        self.add(away, self.one_right.at[plane, 1 - y])
+        self.sends.start(away, self.two_right.at[plane], self.send.at[3, plane], self.receive.at[3, plane], {"y": 1 - y})
+        self.add(self.parts.at[plane, x, y, :, self.left], self.one_left.at[plane, x])
+        self.add(self.parts.at[plane, x, y, :, self.right], self.one_right.at[plane, y])
+
+    def third(self, step):
+        plane, x, y = self.planes[step], self.x, self.y
+        here = self.parts.at[plane, x, y]
+        arrive(self.two_left.at[plane], self.receive.at[2, plane])
+        arrive(self.two_right.at[plane], self.receive.at[3, plane])
+        self.add(here.at[:, self.left], self.two_left.at[plane])
+        self.add(here.at[:, self.right], self.two_right.at[plane])
+        if step:
+            self.sends.start(here, self.last.at[self.z], self.send.at[4, plane], self.receive.at[4, self.z], {"z": plane})
+
+    def total(self):
+        here = self.parts[self.z, self.x, self.y].astype(jnp.float32)
+        for plane in self.planes[1:]:
+            arrive(self.last.at[plane], self.receive.at[4, plane])
+            here = here + self.last[plane].astype(jnp.float32)
+        return here
+
+
+def gather_call(own, collective):
+    rows, width = own.shape
+
+    def kernel(own_ref, out_ref, send, receive):
+        z, x, y, _ = positions_here()
+        greet(pltpu.get_barrier_semaphore(), near_partners(z, x, y))
+        out_ref[z, x, y] = own_ref[...]
+        sends = Sends()
+        gather = Gather(out_ref, send, receive, width // 2, sends)
+        gather.first(0)
+        gather.begin()
+        gather.second(0)
+        for step in range(1, 4):
+            gather.first(step)
+            gather.second(step)
+        for step in range(4):
+            gather.whole(step)
+        sends.finish()
+
+    vmem = pl.BlockSpec(memory_space=pltpu.VMEM)
+    return pl.pallas_call(
+        kernel,
+        name=f"gather_{collective}",
+        out_shape=jax.ShapeDtypeStruct((4, 2, 2, rows, width), own.dtype),
+        in_specs=[vmem],
+        out_specs=vmem,
+        scratch_shapes=Gather.semaphores(),
+        compiler_params=pltpu.CompilerParams(
+            collective_id=collective, has_side_effects=True, vmem_limit_bytes=VMEM_LIMIT
+        ),
+    )(own)
+
+
+def reduce_call(parts, collective):
+    rows, width = parts.shape[-2:]
+
+    def kernel(parts_ref, out_ref, held, *buffers):
+        z, x, y, _ = positions_here()
+        held[...] = parts_ref[...]
+        greet(pltpu.get_barrier_semaphore(), near_partners(z, x, y))
+        sends = Sends()
+        add = Reduce(held, buffers, width // 2, sends)
+        for step in (3, 2, 1, 0):
+            add.first(step)
+        add.second(3)
+        add.second(2)
+        add.third(3)
+        add.second(1)
+        add.third(2)
+        add.second(0)
+        add.third(1)
+        add.third(0)
+        out_ref[...] = add.total()
+        sends.finish()
+
+    vmem = pl.BlockSpec(memory_space=pltpu.VMEM)
+    return pl.pallas_call(
+        kernel,
+        name=f"reduce_{collective}",
+        out_shape=jax.ShapeDtypeStruct((rows, width), jnp.float32),
+        in_specs=[vmem],
+        out_specs=vmem,
+        scratch_shapes=[pltpu.VMEM(parts.shape, parts.dtype), *Reduce.buffers(rows, width, width // 2)],
+        compiler_params=pltpu.CompilerParams(
+            collective_id=collective, has_side_effects=True, vmem_limit_bytes=VMEM_LIMIT
+        ),
+    )(parts)
+
+
+EXTRA = 128
+
+
+def dot_nn(a, b):
+    return lax.dot_general(a, b, (((1,), (0,)), ((), ())), preferred_element_type=jnp.float32)
+
+
+def dot_nt(a, b):
+    return lax.dot_general(a, b, (((1,), (1,)), ((), ())), preferred_element_type=jnp.float32)
+
+
+def dot_tn(a, b):
+    return lax.dot_general(a, b, (((0,), (0,)), ((), ())), preferred_element_type=jnp.float32)
+
+
+def chips_but(z, x, y):
+    found = []
+    for dz in range(4):
+        for dx in range(2):
+            for dy in range(2):
+                if dz or dx or dy:
+                    found.append({"z": lax.rem(z + dz, 4), "x": (x + dx) % 2, "y": (y + dy) % 2})
+    return found
+
+
+def experts_call(own, cotangents, three, routed_units):
+    bf16, f32 = jnp.bfloat16, jnp.float32
+    rows, wide = own.shape
+    width = wide - EXTRA
+    units = three.shape[1]
+    shared_units = units - routed_units
+    tile = routed_units // 2
+    assert shared_units == tile
+    chunk = 4 * rows
+    tokens = 4 * chunk
+    cut = width // 2
+    column = 1024
+    half_tile = tile // 2
+    keep = tile + half_tile
+
+    def kernel(own_ref, cot_ref, three_ref, sum_ref, out_ref, dot_ref, expert_ref, shared_ref, held, weights, hidden, gate_grad, up_grad,
+               part_n, part_o, dots_mine, staged, *rest):
+        (g_send, g_recv, w_sem, d_send, d_recv, free, x_send, x_recv, s_sem) = rest[:9]
+        n_bufs, o_bufs = rest[9:16], rest[16:23]
+        z, x, y, c = positions_here()
+        here = z * 2 + x
+        loads = [pltpu.make_async_copy(three_ref.at[i], weights.at[i], w_sem.at[i]) for i in range(3)]
+        for load in loads:
+            load.start()
+        others = chips_but(z, x, y)
+        greet(pltpu.get_barrier_semaphore(), others + [{"c": 1 - c}])
+        held[z, x, y] = own_ref[...]
+        sends = Sends()
+        gather = Gather(held, g_send, g_recv, cut, sends)
+        sum_n = Reduce(part_n, n_bufs, cut, sends)
+        sum_o = Reduce(part_o, o_bufs, cut, sends)
+        lanes = lax.broadcasted_iota(jnp.int32, (16, EXTRA), 1)
+        rows_of = lax.broadcasted_iota(jnp.int32, (16, EXTRA), 0)
+        pick = ((rows_of == 0) & ((lanes == here) | (lanes == here + 8))) | ((rows_of == 1) & ((lanes == 16) | (lanes == 17)))
+        pick = pick.astype(f32).astype(bf16)
+
+        def units_of(step):
+            plane = gather.planes[step]
+            place = pl.ds(pl.multiple_of(plane * chunk, chunk), chunk)
+            rows_n = held[plane, :, :, :, 0:width].reshape(chunk, width)
+            rows_c = cot_ref[plane].reshape(chunk, width)
+            scales = dot_nt(pick, held[plane, :, :, :, width:wide].reshape(chunk, EXTRA))
+
+            def one(i, _):
+                span = pl.ds(pl.multiple_of(i * tile, 32), tile)
+                scale = jnp.where(i == 2, scales[1:2], scales[0:1])
+                gate = dot_nt(weights[0, span, :], rows_n)
+                up = dot_nt(weights[1, span, :], rows_n)
+                down = dot_nt(weights[2, span, :], rows_c)
+                sig = 1.0 / (1.0 + jnp.exp(-gate))
+                active = gate * sig
+                hid = active * up
+                dot = jnp.sum(hid * down, 0, keepdims=True)
+                hidden[span, place] = (hid * scale).astype(bf16)
+                grad = down * scale
+                gate_grad[span, place] = (grad * up * (sig + active * (1.0 - sig))).astype(bf16)
+                up_grad[span, place] = (grad * active).astype(bf16)
+                routed, shared = lax.cond(i == 2, lambda: (jnp.zeros_like(dot), dot), lambda: (dot, jnp.zeros_like(dot)))
+                return (_[0] + routed, _[1] + shared)
+
+            zero = jnp.zeros((1, chunk), f32)
+            routed, shared = lax.fori_loop(0, 3, one, (zero, zero))
+            row = lax.broadcasted_iota(jnp.int32, (8, chunk), 0)
+            both = jnp.where(row == 0, routed, jnp.where(row == 1, shared, 0.0))
+            for t in range(2):
+                dots_mine[plane, t] = both[:, t * 2 * rows : (t + 1) * 2 * rows]
+
+        def back_of(step):
+            plane = gather.planes[step]
+            place = pl.ds(pl.multiple_of(plane * chunk, chunk), chunk)
+
+            def one(i, _):
+                span = pl.ds(pl.multiple_of(i * column, column), column)
+                value = dot_tn(gate_grad[:, place], weights[0, :, span]) + dot_tn(up_grad[:, place], weights[1, :, span])
+                part_n[plane, :, :, :, span] = value.astype(bf16).reshape(2, 2, rows, column)
+                return 0
+
+            lax.fori_loop(0, width // column, one, 0)
+
+        def out_of(step):
+            plane = gather.planes[step]
+            place = pl.ds(pl.multiple_of(plane * chunk, chunk), chunk)
+
+            def one(i, _):
+                span = pl.ds(pl.multiple_of(i * column, column), column)
+                value = dot_tn(hidden[:, place], weights[2, :, span])
+                part_o[plane, :, :, :, span] = value.astype(bf16).reshape(2, 2, rows, column)
+                return 0
+
+            lax.fori_loop(0, width // column, one, 0)
+
+        gather.first(0)
+        gather.begin()
+        gather.second(0)
+        gather.first(1)
+        for load in loads:
+            load.wait()
+        for step in range(4):
+            gather.whole(step)
+            units_of(step)
+            if step < 3:
+                gather.second(step + 1)
+            if step < 2:
+                gather.first(step + 2)
+            back_of(step)
+            sum_n.first(step)
+            if step:
+                sum_n.second(step - 1)
+            out_of(step)
+            if step > 1:
+                sum_n.third(step - 2)
+            sum_o.first(step)
+            if step:
+                sum_o.second(step - 1)
+        for i, other in enumerate(others):
+            sends.start(dots_mine.at[other["z"], other["x"]], dot_ref.at[z, x, y], d_send.at[i], d_recv.at[z, x, y], other)
+        dot_ref[z, x, y] = dots_mine[z, x]
+        pl.semaphore_signal(free, inc=1, device_id={"c": 1 - c}, device_id_type=MESH_ID)
+
+        def gradient(kind, first, count, span):
+            if kind < 2:
+                side = (gate_grad, up_grad)[kind]
+                return dot_nn(side[pl.ds(first, count), :], held[:, :, :, :, span].reshape(tokens, column))
+            return dot_nn(hidden[pl.ds(first, count), :], cot_ref[:, :, :, :, span].reshape(tokens, column))
+
+        def away(core, kind):
+            def one(i, _):
+                span = pl.ds(pl.multiple_of(i * column, column), column)
+                first = pl.multiple_of(core * tile, 32)
+                weights[kind, 0:tile, span] = gradient(kind, first, tile, span).astype(bf16)
+                first = pl.multiple_of(routed_units + core * half_tile, 16)
+                weights[kind, tile:keep, span] = gradient(kind, first, half_tile, span).astype(bf16)
+                return 0
+
+            lax.fori_loop(0, width // column, one, 0)
+
+        away(1 - c, 0)
+        sum_n.second(3)
+        sum_n.third(2)
+        sum_o.third(1)
+        pl.semaphore_wait(free, 1)
+        for kind in range(3):
+            if kind:
+                away(1 - c, kind)
+            sends.start(weights.at[kind, 0:keep], weights.at[kind, keep : 2 * keep], x_send.at[kind], x_recv.at[kind], {"c": 1 - c})
+            if kind == 0:
+                sum_n.third(3)
+                sum_o.second(3)
+                sum_o.third(2)
+            if kind == 1:
+                sum_o.third(3)
+        sum_o.third(0)
+        writes = []
+        for kind in range(3):
+            arrive(weights.at[kind, keep : 2 * keep], x_recv.at[kind])
+            if kind > 1:
+                writes[kind - 2].wait()
+
+            def one(i, _):
+                span = pl.ds(pl.multiple_of(i * column, column), column)
+                first = pl.multiple_of(c * tile, 32)
+                value = gradient(kind, first, tile, span)
+                staged[kind % 2, :, span] = value + weights[kind, keep : keep + tile, span].astype(f32)
+                first = pl.multiple_of(routed_units + c * half_tile, 16)
+                value = gradient(kind, first, half_tile, span)
+                shared_ref[kind, :, span] = (value + weights[kind, keep + tile : 2 * keep, span].astype(f32)).astype(bf16)
+                return 0
+
+            lax.fori_loop(0, width // column, one, 0)
+            write = pltpu.make_async_copy(staged.at[kind % 2], expert_ref.at[kind], s_sem.at[kind])
+            write.start()
+            writes.append(write)
+        sum_ref[...] = sum_n.total()
+        out_ref[...] = sum_o.total()
+        for other in others:
+            arrive(dot_ref.at[other["z"], other["x"], other["y"]], d_recv.at[other["z"], other["x"], other["y"]])
+        writes[1].wait()
+        writes[2].wait()
+        sends.finish()
+
+    vmem = pl.BlockSpec(memory_space=pltpu.VMEM)
+    anywhere = pl.BlockSpec(memory_space=pl.ANY)
+    dma = pltpu.SemaphoreType.DMA
+    flops = 2 * tokens * width * units * 9
+    return pl.pallas_call(
+        kernel,
+        name="experts",
+        out_shape=(
+            jax.ShapeDtypeStruct((rows, width), f32),
+            jax.ShapeDtypeStruct((rows, width), f32),
+            jax.ShapeDtypeStruct((4, 2, 2, 8, 2 * rows), f32),
+            jax.ShapeDtypeStruct((3, tile, width), f32),
+            jax.ShapeDtypeStruct((3, half_tile, width), bf16),
+        ),
+        in_specs=[vmem, vmem, anywhere],
+        out_specs=(vmem, vmem, vmem, anywhere, vmem),
+        scratch_shapes=[
+            pltpu.VMEM((4, 2, 2, rows, wide), bf16),
+            pltpu.VMEM((3, units, width), bf16),
+            pltpu.VMEM((units, tokens), bf16),
+            pltpu.VMEM((units, tokens), bf16),
+            pltpu.VMEM((units, tokens), bf16),
+            pltpu.VMEM((4, 2, 2, rows, width), bf16),
+            pltpu.VMEM((4, 2, 2, rows, width), bf16),
+            pltpu.VMEM((4, 2, 8, 2 * rows), f32),
+            pltpu.VMEM((2, tile, width), f32),
+            *Gather.semaphores(),
+            dma((3,)),
+            dma((15,)),
+            dma((4, 2, 2)),
+            pltpu.SemaphoreType.REGULAR,
+            dma((3,)),
+            dma((3,)),
+            dma((3,)),
+            *Reduce.buffers(rows, width, cut),
+            *Reduce.buffers(rows, width, cut),
+        ],
+        compiler_params=pltpu.CompilerParams(collective_id=2, has_side_effects=True, vmem_limit_bytes=VMEM_LIMIT),
+        cost_estimate=pl.CostEstimate(flops=flops, bytes_accessed=40 * 1024 * 1024, transcendentals=tokens * units),
+    )(own, cotangents, three)
 
 
 def tree_masks(parent_rows, seg_len):
@@ -548,6 +1019,7 @@
     here = z * 2 + x
     trees = expert_count
     tokens = trees * seq_rows
+    blocks = (trees // 2, 2, 2, seq_rows // 2, model_width)
     own_rows = seq_rows // 2
     slice_rows = norm1_gain.shape[0]
     score_scale = HD ** (-0.5)
@@ -571,8 +1043,6 @@
         project_bias.reshape(-1),
         mine(positions),
         mine(parents),
-        mine(routes),
-        mine(route_slots),
     ]
     sizes = [p.shape[0] for p in pieces]
     small = lax.all_gather(jnp.concatenate(pieces), AXES, axis=0, tiled=False)
@@ -601,8 +1071,6 @@
 
     all_positions = by_tree(5).reshape(-1).astype(f32)
     all_parents = by_tree(6).astype(jnp.int32)
-    all_routes = by_tree(7).reshape(tokens, top_count).astype(jnp.int32)
-    all_slots = by_tree(8).reshape(tokens, top_count).astype(jnp.int32)
 
     local_heads = project_weight.shape[2] // HD
     half_rows = slice_rows // 2
@@ -637,12 +1105,10 @@
     shared_three = join_cores(got, 1)
     expert_three = join_cores(jnp.stack([expert_gate[0].T, expert_up[0].T, expert_down[0]]), 1)
     routed_units = expert_three.shape[1]
-    shared_units = shared_three.shape[1]
     three = jnp.concatenate([expert_three, shared_three], 1)
-    gate_rows, up_rows, down_rows = three[0], three[1], three[2]
-
-    all_input = gather_chips(own_input).astype(f32)
-    all_cotangent = gather_chips(own_cotangent)
+
+    all_input = gather_call(own_input, 3).reshape(tokens, model_width).astype(f32)
+    all_cotangent = gather_call(own_cotangent, 4)
     norm_one = lax.rsqrt(jnp.mean(all_input * all_input, -1, keepdims=True) + EPSILON)
     normed_one = (all_input * norm_one * gain_one).astype(bf16)
     half_size = HD // 2
@@ -672,74 +1138,54 @@
         .astype(bf16)
         .reshape(tokens, HD)
     )
-    attention = scatter_chips(product(heads_out, output_head).astype(bf16)).astype(f32)
+    attention = reduce_call(product(heads_out, output_head).astype(bf16).reshape(blocks), 5)
     own_rows_in = own_input.astype(f32)
     own_norm_one = lax.rsqrt(jnp.mean(own_rows_in * own_rows_in, -1, keepdims=True) + EPSILON)
     hidden_state = own_rows_in + attention
     norm_two = lax.rsqrt(jnp.mean(hidden_state * hidden_state, -1, keepdims=True) + EPSILON)
     own_normed_two = (hidden_state * norm_two * gain_two).astype(bf16)
 
-    def route(rows, route_rows):
-        logits = product_right(small_weights, rows)
-        prob = jax.nn.softmax(logits[:expert_count], axis=0)
-        expert_ids = jnp.arange(expert_count, dtype=jnp.int32)
-        onehot = (route_rows.T[:, None, :] == expert_ids[None, :, None]).astype(f32)
-        picked_sum = jnp.sum(jnp.sum(onehot, 0) * prob, 0, keepdims=True)
-        scale = jax.nn.sigmoid(logits[expert_count])
-        return prob, onehot, picked_sum, scale
-
-    normed_two = gather_chips(own_normed_two)
-    prob, onehot, picked_sum, shared_scale = route(normed_two, all_routes)
-    kept = (all_slots.T < capacity).astype(f32)
-    gates = jnp.sum(onehot * kept[:, None, :], 0) * prob / picked_sum
-    gate_here = lax.dynamic_index_in_dim(gates, here, 0, keepdims=False)
-
-    scales = jnp.concatenate(
+    first = y * own_rows
+    my_routes = lax.dynamic_slice(routes, (c, first, 0), (1, own_rows, top_count))[0]
+    my_slots = lax.dynamic_slice(route_slots, (c, first, 0), (1, own_rows, top_count))[0]
+    logits = product_right(own_normed_two, small_weights)
+    prob = jax.nn.softmax(logits[:, :expert_count], axis=-1)
+    shared_scale = jax.nn.sigmoid(logits[:, expert_count:])
+    onehot = (my_routes[..., None] == jnp.arange(expert_count, dtype=jnp.int32)).astype(f32)
+    kept = jnp.sum(onehot * (my_slots < capacity).astype(f32)[..., None], 1)
+    onehot = jnp.sum(onehot, 1)
+    picked_sum = jnp.sum(onehot * prob, -1, keepdims=True)
+    every_gate = onehot * prob / picked_sum
+    row_scales = jnp.concatenate([every_gate * kept, shared_scale], 1)
+    high = row_scales.astype(bf16)
+    low = (row_scales - high.astype(f32)).astype(bf16)
+    extra = jnp.concatenate(
         [
-            jnp.broadcast_to(gate_here, (routed_units, tokens)),
-            jnp.broadcast_to(shared_scale, (shared_units, tokens)),
+            high[:, :expert_count],
+            low[:, :expert_count],
+            high[:, expert_count:],
+            low[:, expert_count:],
+            jnp.zeros((own_rows, EXTRA - 2 * expert_count - 2), bf16),
         ],
-        0,
-    )
-    gate_units = product_right(gate_rows, normed_two)
-    up_units = product_right(up_rows, normed_two)
-    grad_units = product_right(down_rows, all_cotangent)
-    sigmoid = jax.nn.sigmoid(gate_units)
-    active = gate_units * sigmoid
-    hidden = active * up_units
-    both = hidden * grad_units
-    expert_dot = jnp.sum(both[:routed_units], 0)
-    shared_dot = jnp.sum(both[routed_units:], 0)
-    scaled_hidden = (hidden * scales).astype(bf16)
-    hidden_grad = grad_units * scales
-    gate_grad = (
-        hidden_grad * up_units * (sigmoid * (1.0 + gate_units * (1.0 - sigmoid)))
-    ).astype(bf16)
-    up_grad = (hidden_grad * active).astype(bf16)
-    ffn_part = product_left(scaled_hidden, down_rows).astype(bf16)
-    normed_part = (product_left(gate_grad, gate_rows) + product_left(up_grad, up_rows)).astype(bf16)
-    dots = jnp.where(jnp.arange(expert_count)[:, None] == here, expert_dot, 0.0)
-    dots = jnp.concatenate([dots, shared_dot[None]], 0)
-    ffn_out = scatter_chips(ffn_part).astype(f32)
+        1,
+    )
+    normed_sum, ffn_out, dots, expert_sum, shared_sum = experts_call(
+        jnp.concatenate([own_normed_two, extra], 1), all_cotangent, three, routed_units
+    )
     own_output = (hidden_state + ffn_out).astype(bf16)
-    normed_sum = scatter_chips(normed_part).astype(f32)
-    all_dots = lax.psum(dots, CHIPS)
-    three_grad = jnp.stack(
-        [product(gate_grad, normed_two), product(up_grad, normed_two), product(scaled_hidden, all_cotangent)]
-    ).astype(bf16)
-
-    valid_gate = jnp.sum(onehot * kept[:, None, :], 0)
-    every_gate = jnp.sum(onehot, 0) * prob / picked_sum
-    kept_dots = all_dots[:expert_count] * valid_gate
-    picked_grad = (kept_dots - jnp.sum(kept_dots * every_gate, 0, keepdims=True)) / picked_sum
-    prob_grad = picked_grad * jnp.sum(onehot, 0)
-    logit_grad = prob * (prob_grad - jnp.sum(prob * prob_grad, 0, keepdims=True))
-    scale_grad = all_dots[expert_count] * shared_scale * (1.0 - shared_scale)
-    small_grad = jnp.concatenate([logit_grad, scale_grad[None]], 0).astype(bf16)
-    first = here * seq_rows + y * own_rows
-    own_small = lax.dynamic_slice(small_grad, (0, first), (expert_count + 1, own_rows))
-    grad_small = product(own_small, own_normed_two)
-    normed_two_grad = normed_sum + product_left(own_small, small_weights)
+    dots = lax.dynamic_slice(dots, (0, 0, 0, 0, first), (*dots.shape[:4], own_rows))
+    dots = dots.reshape(trees, 2, 8, own_rows)
+    expert_dots = (dots[:, 0, 0] + dots[:, 1, 0]).T
+    shared_dot = jnp.sum(dots[:, :, 1], (0, 1))[:, None]
+
+    kept_dots = expert_dots * kept
+    picked_grad = (kept_dots - jnp.sum(kept_dots * every_gate, -1, keepdims=True)) / picked_sum
+    prob_grad = picked_grad * onehot
+    logit_grad = prob * (prob_grad - jnp.sum(prob * prob_grad, -1, keepdims=True))
+    scale_grad = shared_dot * shared_scale * (1.0 - shared_scale)
+    own_small = jnp.concatenate([logit_grad, scale_grad], 1).astype(bf16)
+    grad_small = product_left(own_small, own_normed_two)
+    normed_two_grad = normed_sum + product(own_small, small_weights)
     upstream = own_cotangent.astype(f32)
     grad_gain_two = jnp.sum(normed_two_grad * hidden_state * norm_two, 0)
     scaled_two = normed_two_grad * gain_two
@@ -748,7 +1194,7 @@
         + norm_two * scaled_two
         - hidden_state * norm_two**3 * jnp.mean(scaled_two * hidden_state, -1, keepdims=True)
     )
-    attention_grad = gather_chips(hidden_grad_rows.astype(bf16))
+    attention_grad = gather_call(hidden_grad_rows.astype(bf16), 6).reshape(tokens, model_width)
 
     output_grad = product_left(heads_out, attention_grad).astype(bf16)
     heads_grad = product_right(attention_grad, output_head).astype(bf16).reshape(tree_shape)
@@ -768,7 +1214,7 @@
     bias_grad = jnp.stack([jnp.sum(g.astype(f32), 0) for g in raw_grads])
     project_grad = jnp.stack([product_left(normed_one, g) for g in raw_grads]).astype(bf16)
     normed_part = sum(product_right(g, project_head[i]) for i, g in enumerate(raw_grads))
-    normed_one_grad = scatter_chips(normed_part.astype(bf16)).astype(f32)
+    normed_one_grad = reduce_call(normed_part.astype(bf16).reshape(blocks), 7)
     grad_gain_one = jnp.sum(normed_one_grad * own_rows_in * own_norm_one, 0)
     scaled_one = normed_one_grad * gain_one
     own_grad = (
@@ -801,8 +1247,6 @@
     got = swap_chips(send).reshape(2, local_heads, HD, half_rows)
     got = swap_cores(got).reshape(2, local_heads, HD, half_rows)
     output_out = got.transpose(1, 2, 0, 3).reshape(local_heads * HD, slice_rows).astype(f32)
-    expert_sum = sum_cores(three_grad[:, :routed_units], 1).astype(f32)
-    shared_sum = sum_cores(three_grad[:, routed_units:], 1)
     send = shared_sum.reshape(3, sub, trees, slice_rows).transpose(2, 0, 1, 3)
     got = swap_chips(send).transpose(1, 0, 2, 3).reshape(3, trees * sub, slice_rows).astype(f32)
     return (

time: 1250 us -> 848 us (0.68)
  waiting for transfers between devices: 756 us -> 230 us
  Pallas kernels: 0 us -> 388 us
  blocking collectives: 175 us -> 16.7 us
  matrix products: 119 us -> 44.8 us
  local copies, waits for them, and re-layouts: 93.5 us -> 67.4 us
  other arithmetic: 55 us -> 42.2 us
    pallas_call x0 -> x6, Pallas kernels: none -> 388 us  [the longest x1 152 us: experts_call(): pl.pallas_call(kernel, name='experts', out_shape=(jax.ShapeDtypeStruct((r...]
    reduce_scatter x4 -> x0, waiting for transfers between devices: 255 us -> none  [scatter_chips(): return lax.psum_scatter(rows, CHIPS, scatter_dimension=0, tiled=True)]
    all_gather x4 -> x0, waiting for transfers between devices: 193 us -> none  [gather_chips(): return lax.all_gather(rows, CHIPS, axis=0, tiled=True)]
    unnamed x21 -> x11, waiting for transfers between devices: 146 us -> 1.34 us
    all_to_all x1 -> x0, blocking collectives: 80 us -> none  [swap_chips(): lax.all_to_all(array, ('z', 'x'), split_axis=0, concat_axis=0, tiled=True)]
    psum x1 -> x0, blocking collectives: 75 us -> none  [chip_shards(): all_dots = lax.psum(dots, CHIPS)]
    all_to_all x5 -> x6, waiting for transfers between devices: 22.2 us -> 77.9 us  [swap_chips(): lax.all_to_all(array, ('z', 'x'), split_axis=0, concat_axis=0, tiled=True)]
    all_gather x3, waiting for transfers between devices: 30.4 us -> 0.03 us  [join_cores(): return lax.all_gather(array, 'c', axis=axis, tiled=True)]
  transfers between devices with their start and end apart: 24 -> 16, of which waited for: 15 -> 8; matrix products, arithmetic and copies ran while one was open for 14% -> 13% of each run, Pallas kernels for 0% -> 23%
where the time goes in v2:
time: 848 us; the launch traced here: 838 us
  Pallas kernels  388 us (46%)
  waiting for transfers between devices  230 us (27%)
  local copies, waits for them, and re-layouts  67.4 us (8%)
  matrix products  44.8 us (5%)
  other arithmetic  42.2 us (5%)
  starting transfers between devices  31.8 us (4%)
  between operations  17.1 us (2%)
  blocking collectives  16.7 us (2%)
    pallas_call x1, Pallas kernels, experts_call(): pl.pallas_call(kernel, name='experts', out_shape=(jax.ShapeDtypeStruct((r...  152 us
    pallas_call x3, Pallas kernels, gather_call(): pl.pallas_call(kernel, name=f'gather_{collective}', out_shape=jax.ShapeDt...  139 us
    psum x1, waiting for transfers between devices, chip_shards(): lax.psum(jnp.concatenate([vectors.reshape(-1), bias_place.reshape(-1)]),...  115 us
    pallas_call x2, Pallas kernels, reduce_call(): pl.pallas_call(kernel, name=f'reduce_{collective}', out_shape=jax.ShapeDt...  96.4 us
    all_to_all x6, waiting for transfers between devices, swap_chips(): lax.all_to_all(array, ('z', 'x'), split_axis=0, concat_axis=0, tiled=True)  77.9 us
    all_to_all x6, starting transfers between devices, swap_chips(): lax.all_to_all(array, ('z', 'x'), split_axis=0, concat_axis=0, tiled=True)  27.5 us
    all_gather x1, waiting for transfers between devices, chip_shards(): lax.all_gather(own_grad, ('c', 'y'), axis=0, tiled=True)  19.5 us
  transfers between devices with their start and end apart: 16, of which 8 were waited for; matrix products, arithmetic and copies ran while one was open for 13% of the time, Pallas kernels for 23%

profile of v2, /device:TPU:0, one launch (start us, length us, event | category | flops | bytes accessed | tf_op | source)
XLA Modules:
  0.0 838.0 jit_solution(16396048930299413144)
XLA Ops:
  10.1 4.4 all_to_all.50
  15.6 7.3 all-to-all-start.1
  27.4 15.9 %all-to-all-done.1 = bf16[8,3,128,128]{3,2,1,0:T(8,128)(2,1)S(1)} async-done(((bf16[8,3,128,128]{3,2,1,0:T(8,128)(2,1)}), bf16[8,3,128,128]{3,2,1,0:T(8,128)(2,1)S(1)}, u32[]{:S(2)}, u32[]{:S(2)}) %all-to-all-start.1) | async-done | bytes 786464 | tf_op jit(solution)/shard_map/all_to_all | solution.py:1082
  48.9 48.9 %all-to-all-done.4 = bf16[8,3,176,256]{3,2,1,0:T(8,128)(2,1)S(1)} async-done(((bf16[8,3,176,256]{3,2,1,0:T(8,128)(2,1)}), bf16[8,3,176,256]{3,2,1,0:T(8,128)(2,1)S(1)}, u32[]{:S(2)}, u32[]{:S(2)}) %all-to-all-start.4) | async-done | bytes 2162720 | tf_op jit(solution)/shard_map/all_to_all | solution.py:1082
  99.6 4.8 all_to_all.51
  113.5 50.0 %gather_3.1 = bf16[4,2,2,64,2048]{4,3,2,1,0:T(8,128)(2,1)} custom-call(bf16[64,2048]{1,0:T(8,128)(2,1)} %get-tuple-element.141.own_ref), custom_call_target="tpu_custom_call" | custom-call | tf_op jit(solution)/shard_map/gather_3/pallas_call | solution.py:670
  168.5 45.5 %gather_4.1.cot_ref = bf16[4,2,2,64,2048]{4,3,2,1,0:T(8,128)(2,1)} custom-call(bf16[64,2048]{1,0:T(8,128)(2,1)} %dynamic-slice_bitcast_fusion.1.own_ref), custom_call_target="tpu_custom_call" | custom-call | tf_op jit(solution)/shard_map/gather_4/pallas_call | solution.py:670
  218.0 5.2 fusion.3
  223.3 6.4 copy.374
  245.7 4.2 fusion.10
  254.4 51.7 %reduce_5.1 = f32[64,2048]{1,0:T(8,128)} custom-call(bf16[4,2,2,64,2048]{4,3,2,1,0:T(8,128)(2,1)} %bitcast.273), custom_call_target="tpu_custom_call" | custom-call | tf_op jit(solution)/shard_map/reduce_5/pallas_call | solution.py:706
  313.9 11.1 %pad_maximum_fusion.three_ref = bf16[3,1056,2048]{2,1,0:T(8,128)(2,1)} fusion(bf16[3,352,2048]{2,1,0:T(8,128)(2,1)} %all-gather.11.cloned.1.call-done, bf16[3,704,2048]{2,1,0:T(8,128)(2,1)} %all-gather.9.cloned.1.call-done), kind=kLoop, calls=%fused_computation.1 | loop fusion | flops 25952256 | bytes 25952256 | tf_op jit(solution)/shard_map/concatenate | solution.py:1108
  325.0 151.9 %experts.1 = (f32[64,2048]{1,0:T(8,128)}, f32[64,2048]{1,0:T(8,128)}, f32[4,2,2,8,128]{4,3,2,1,0:T(8,128)}, f32[3,352,2048]{2,1,0:T(8,128)}, bf16[3,176,2048]{2,1,0:T(8,128)(2,1)}) custom-call(bf16[64,2176]{1,0:T(8,128)(2,1)} %concatenate.74.own_ref, bf16[4,2,2,64,2048]{4,3,2,1,0:T(8,128)(2,1)} %gather_4.1.cot_ref, ...), custom_call_target="tpu_custom_call" | custom-call | flops 39862665216 | bytes 41943040 | tf_op jit(solution)/shard_map/experts/pallas_call | solution.py:928
  482.0 44.0 %gather_6.1 = bf16[4,2,2,64,2048]{4,3,2,1,0:T(8,128)(2,1)} custom-call(bf16[64,2048]{1,0:T(8,128)(2,1)} %get-tuple-element.142.own_ref), custom_call_target="tpu_custom_call" | custom-call | tf_op jit(solution)/shard_map/gather_6/pallas_call | solution.py:670
  526.0 4.2 convolution_convert_fusion.7
  549.5 4.5 fusion.70
  560.7 44.7 %reduce_7.1 = f32[64,2048]{1,0:T(8,128)} custom-call(bf16[4,2,2,64,2048]{4,3,2,1,0:T(8,128)(2,1)} %bitcast.276), custom_call_target="tpu_custom_call" | custom-call | tf_op jit(solution)/shard_map/reduce_7/pallas_call | solution.py:706
  607.3 5.9 all-to-all-start.7
  630.6 9.0 %all-to-all-done.5 = bf16[8,3,128,128]{3,2,1,0:T(8,128)(2,1)S(1)} async-done(((bf16[8,3,128,128]{3,2,1,0:T(8,128)(2,1)}), bf16[8,3,128,128]{3,2,1,0:T(8,128)(2,1)S(1)}, u32[]{:S(2)}, u32[]{:S(2)}) %all-to-all-start.5) | async-done | bytes 786464 | tf_op jit(solution)/shard_map/all_to_all | solution.py:1082
  644.5 5.1 all_to_all.52
  654.7 7.5 fusion.62
  662.1 115.1 %all-reduce.6.cloned.1.call-done = f32[28672]{0:T(1024)} async-done(((f32[28672]{0:T(1024)}), f32[28672]{0:T(1024)}) %all-reduce.6.cloned.1.call-update) | async-done | bytes 114704 | tf_op jit(solution)/shard_map/psum | solution.py:1230
  782.1 14.8 %all-gather.13.cloned.1.call-done = bf16[256,2048]{1,0:T(8,128)(2,1)} async-done(((bf16[64,2048]{1,0:T(8,128)(2,1)}), bf16[256,2048]{1,0:T(8,128)(2,1)}) %all-gather.13.cloned.1.call-update) | async-done | bytes 1048592 | tf_op jit(solution)/shard_map/all_gather | solution.py:1225
  802.0 19.5 %all-gather.15.cloned.1.call-done = f32[256,2048]{1,0:T(8,128)} async-done(((f32[64,2048]{1,0:T(8,128)}), f32[256,2048]{1,0:T(8,128)}) %all-gather.15.cloned.1.call-update) | async-done | bytes 2097168 | tf_op jit(solution)/shard_map/all_gather | solution.py:1226
  (295 shorter events, 139.4 us)
Async XLA Ops:
  8.0 158.7 %copy-start = (s32[2,128,4]{1,2,0:T(4,128)S(1)}, s32[2,128,4]{1,2,0:T(4,128)}, u32[]{:S(2)}) copy-start(s32[2,128,4]{1,2,0:T(4,128)} %param.22) | copy-start | bytes 12292
  15.6 27.7 %all-to-all-start.1 = ((bf16[8,3,128,128]{3,2,1,0:T(8,128)(2,1)}), bf16[8,3,128,128]{3,2,1,0:T(8,128)(2,1)S(1)}, u32[]{:S(2)}, u32[]{:S(2)}) async-start(bf16[8,3,128,128]{3,2,1,0:T(8,128)(2,1)} %bitcast.10), calls=%async_computation.1 | async-start | bytes 1572864 | tf_op jit(solution)/shard_map/all_to_all | solution.py:1082
  43.3 54.6 %all-to-all-start.4 = ((bf16[8,3,176,256]{3,2,1,0:T(8,128)(2,1)}), bf16[8,3,176,256]{3,2,1,0:T(8,128)(2,1)S(1)}, u32[]{:S(2)}, u32[]{:S(2)}) async-start(bf16[8,3,176,256]{3,2,1,0:T(8,128)(2,1)} %copy.357), calls=%async_computation.4 | async-start | bytes 4325376 | tf_op jit(solution)/shard_map/all_to_all | solution.py:1082
  46.9 168.3 %all-reduce.8.cloned.1.call-start = ((), (), s32[]{:S(2)}) async-start(), calls=%async_computation.18 | async-start | bytes 405504
  48.3 187.5 %all-gather.17.cloned.1.call-start = ((), (), s32[]{:S(2)}) async-start(), calls=%async_computation.17 | async-start | bytes 2359296 | tf_op jit(solution)/shard_map/all_gather | solution.py:1085
  48.9 265.0 %all-gather.11.cloned.1.call-start = ((), (), s32[]{:S(2)}) async-start(), calls=%async_computation.12 | async-start | bytes 6488064 | tf_op jit(solution)/shard_map/all_gather | solution.py:1085
  104.4 128.6 %all-to-all-start.3 = ((bf16[8,128,128]{2,1,0:T(8,128)(2,1)}), bf16[8,128,128]{2,1,0:T(8,128)(2,1)S(1)}, u32[]{:S(2)}, u32[]{:S(2)}) async-start(bf16[8,128,128]{2,1,0:T(8,128)(2,1)} %bitcast.23), calls=%async_computation.3 | async-start | bytes 524288 | tf_op jit(solution)/shard_map/all_to_all | solution.py:1082
  108.1 205.8 %all-gather.9.cloned.1.call-start = ((), (), s32[]{:S(2)}) async-start(), calls=%async_computation.11 | async-start | bytes 12976128 | tf_op jit(solution)/shard_map/all_gather | solution.py:1085
  111.6 494.0 %reduce-scatter.5.cloned.1.call-start = ((), (), s32[]{:S(2)}) async-start(), calls=%async_computation.16 | async-start | bytes 786432 | tf_op jit(solution)/shard_map/reduce_scatter | solution.py:1238
  325.0 153.0 %copy-start.33 = (f32[64]{0:T(128)S(1)}, f32[64]{0:T(128)}, u32[]{:S(2)}) copy-start(f32[64]{0:T(128)} %copy-done.32) | copy-start | bytes 772
  325.0 153.0 %copy-start.29 = (f32[64]{0:T(128)S(1)}, f32[64]{0:T(128)}, u32[]{:S(2)}) copy-start(f32[64]{0:T(128)} %copy-done.28) | copy-start | bytes 772
  325.0 153.0 %copy-start.31 = (f32[64]{0:T(128)S(1)}, f32[64]{0:T(128)}, u32[]{:S(2)}) copy-start(f32[64]{0:T(128)} %copy-done.30) | copy-start | bytes 772
  325.0 153.1 %copy-start.35 = (f32[64]{0:T(128)S(1)}, f32[64]{0:T(128)}, u32[]{:S(2)}) copy-start(f32[64]{0:T(128)} %copy-done.34) | copy-start | bytes 772
  325.0 154.6 %copy-start.43 = (f32[64]{0:T(128)S(1)}, f32[64]{0:T(128)}, u32[]{:S(2)}) copy-start(f32[64]{0:T(128)} %get-tuple-element.189) | copy-start | bytes 772
  538.4 76.1 %all-reduce.10.cloned.1.call-start = ((), (), s32[]{:S(2)}) async-start(), calls=%async_computation.19 | async-start | bytes 3145728
  607.3 14.1 %all-to-all-start.7 = ((bf16[8,128,128]{2,1,0:T(8,128)(2,1)}), bf16[8,128,128]{2,1,0:T(8,128)(2,1)S(1)}, u32[]{:S(2)}, u32[]{:S(2)}) async-start(bf16[8,128,128]{2,1,0:T(8,128)(2,1)} %copy.379), calls=%async_computation.8 | async-start | bytes 524288 | tf_op jit(solution)/shard_map/all_to_all | solution.py:1082
  621.4 18.1 %all-to-all-start.5 = ((bf16[8,3,128,128]{3,2,1,0:T(8,128)(2,1)}), bf16[8,3,128,128]{3,2,1,0:T(8,128)(2,1)S(1)}, u32[]{:S(2)}, u32[]{:S(2)}) async-start(bf16[8,3,128,128]{3,2,1,0:T(8,128)(2,1)} %copy.375), calls=%async_computation.5 | async-start | bytes 1572864 | tf_op jit(solution)/shard_map/all_to_all | solution.py:1082
  625.0 152.3 %all-reduce.6.cloned.1.call-start = ((), (), s32[]{:S(2)}) async-start(), calls=%async_computation.15 | async-start | bytes 229376 | tf_op jit(solution)/shard_map/psum | solution.py:1230
  625.8 171.1 %all-gather.13.cloned.1.call-start = ((), (), s32[]{:S(2)}) async-start(), calls=%async_computation.13 | async-start | bytes 1310720 | tf_op jit(solution)/shard_map/all_gather | solution.py:1225
  639.5 5.0 all-to-all-start.8
  649.7 171.8 %all-to-all-start.9 = ((bf16[8,3,176,256]{3,2,1,0:T(8,128)(2,1)}), bf16[8,3,176,256]{3,2,1,0:T(8,128)(2,1)S(1)}, u32[]{:S(2)}, u32[]{:S(2)}) async-start(bf16[8,3,176,256]{3,2,1,0:T(8,128)(2,1)} %bitcast.278), calls=%async_computation.10 | async-start | bytes 4325376 | tf_op jit(solution)/shard_map/all_to_all | solution.py:1082
  653.3 168.2 %all-gather.15.cloned.1.call-start = ((), (), s32[]{:S(2)}) async-start(), calls=%async_computation.14 | async-start | bytes 2621440 | tf_op jit(solution)/shard_map/all_gather | solution.py:1226
  654.7 126.2 %copy-start.21 = (bf16[2,4,128,128]{3,1,2,0:T(4,128)(2,1)S(1)}, bf16[2,4,128,128]{3,1,2,0:T(4,128)(2,1)}, u32[]{:S(2)}) copy-start(bf16[2,4,128,128]{3,1,2,0:T(4,128)(2,1)} %copy-done.20) | copy-start | bytes 786436
  654.7 142.2 %copy-start.9 = (bf16[2,4,3,128,128]{4,3,1,2,0:T(8,128)(2,1)S(1)}, bf16[2,4,3,128,128]{4,3,1,2,0:T(8,128)(2,1)}, u32[]{:S(2)}) copy-start(bf16[2,4,3,128,128]{4,3,1,2,0:T(8,128)(2,1)} %all_to_all.52) | copy-start | bytes 2359300
  (40 other events, 590.9 us)
Sparse Core Ops, SparseCore 0:
  53.9 151.5 all-reduce.7
  632.0 145.2 all-reduce.5
  779.4 17.4 all-gather.12
  798.9 22.5 all-gather.14
Sparse Core Ops, SparseCore 1:
  50.9 11.0 all-gather.16
  99.6 12.8 all-gather.10
  113.9 20.6 all-gather.8
  538.5 7.1 reduce-scatter.4
  554.1 19.4 all-reduce.9

commit v3 on v2

--- a/solution.py
+++ b/solution.py
@@ -508,20 +508,31 @@
     return [{"x": 1 - x}, {"y": 1 - y}] + [{"z": p} for p in planes[1:]]
 
 
+def run(*steps):
+    for step in steps:
+        step()
+
+
 class Sends:
     def __init__(self):
         self.open = []
 
-    def start(self, source, target, send, receive, where):
+    def start(self, source, target, send, receive, where, only=None):
         copy = pltpu.make_async_remote_copy(
             src_ref=source, dst_ref=target, send_sem=send, recv_sem=receive, device_id=where, device_id_type=MESH_ID
         )
-        copy.start()
-        self.open.append(copy)
+        if only is None:
+            copy.start()
+        else:
+            pl.when(only)(copy.start)
+        self.open.append((copy, only))
 
     def finish(self):
-        for copy in self.open:
-            copy.wait_send()
+        for copy, only in self.open:
+            if only is None:
+                copy.wait_send()
+            else:
+                pl.when(only)(copy.wait_send)
         self.open = []
 
 
@@ -530,12 +541,15 @@
 
 
 class Gather:
+    ready = (5, 8, 11, 14)
+
     def __init__(self, held, send, receive, cut, sends):
         self.held, self.send, self.receive, self.sends = held, send, receive, sends
         width = held.shape[-1]
         self.left, self.right = pl.ds(0, cut), pl.ds(cut, width - cut)
         self.z, self.x, self.y, _ = positions_here()
         self.planes = planes_from(self.z)
+        self.inner = jnp.logical_or(self.z == 1, self.z == 2)
 
     def block(self, plane, x, y, columns=None):
         if columns is None:
@@ -547,19 +561,23 @@
         ref = self.block(plane, x, y, columns)
         self.sends.start(ref, ref, self.send.at[slot, plane], self.receive.at[slot, plane], {axis: 1 - here})
 
-    def begin(self):
-        own = self.block(self.z, self.x, self.y)
-        for step, plane in enumerate(self.planes[1:]):
-            self.sends.start(own, own, self.send.at[6, step], self.receive.at[6, self.z], {"z": plane})
-
-    def first(self, step):
+    def along(self, plane, slot, to, only=None):
+        ref = self.block(plane, self.x, self.y)
+        self.sends.start(ref, ref, self.send.at[slot, plane], self.receive.at[6, plane], {"z": to}, only)
+
+    def plane(self, step):
+        plane = self.planes[step]
+        arrive(self.block(plane, self.x, self.y), self.receive.at[6, plane])
+        self.along(plane, 6, 3 - self.z if step == 1 else self.planes[1], self.inner)
+
+    def first(self, step, part):
         plane, x, y = self.planes[step], self.x, self.y
-        if step:
-            arrive(self.block(plane, x, y), self.receive.at[6, plane])
-        self.pass_on(plane, x, y, self.left, 0, "x")
-        self.pass_on(plane, x, y, self.right, 1, "y")
-        self.pass_on(plane, x, y, self.left, 2, "y")
-        self.pass_on(plane, x, y, self.right, 3, "x")
+        if part == 0:
+            self.pass_on(plane, x, y, self.left, 0, "x")
+            self.pass_on(plane, x, y, self.right, 1, "y")
+        else:
+            self.pass_on(plane, x, y, self.left, 2, "y")
+            self.pass_on(plane, x, y, self.right, 3, "x")
 
     def second(self, step):
         plane, x, y = self.planes[step], self.x, self.y
@@ -568,16 +586,46 @@
         arrive(self.block(plane, x, 1 - y, self.right), self.receive.at[1, plane])
         self.pass_on(plane, x, 1 - y, self.right, 5, "x")
 
-    def whole(self, step):
+    def third(self, step):
         plane, x, y = self.planes[step], self.x, self.y
         arrive(self.block(plane, x, 1 - y, self.left), self.receive.at[2, plane])
         arrive(self.block(plane, 1 - x, y, self.right), self.receive.at[3, plane])
+
+    def fourth(self, step):
+        plane, x, y = self.planes[step], self.x, self.y
         arrive(self.block(plane, 1 - x, 1 - y, self.left), self.receive.at[4, plane])
         arrive(self.block(plane, 1 - x, 1 - y, self.right), self.receive.at[5, plane])
 
+    def steps(self):
+        def begin():
+            self.first(0, 0)
+            self.along(self.z, 6, self.planes[1])
+            self.along(self.z, 7, 3 - self.z, self.inner)
+            self.first(0, 1)
+
+        found = [begin, lambda: self.plane(1), lambda: self.second(0)]
+        for step in range(4):
+
+            def turn_over(step=step):
+                if 0 < step + 2 < 4:
+                    self.plane(step + 2)
+                self.third(step)
+                if step < 3:
+                    self.first(step + 1, 0)
+
+            def close(step=step):
+                self.fourth(step)
+                if step < 3:
+                    self.first(step + 1, 1)
+
+            found += [turn_over, close]
+            if step < 3:
+                found.append(lambda step=step: self.second(step + 1))
+        return found
+
     @staticmethod
     def semaphores():
-        return [pltpu.SemaphoreType.DMA((7, 4)), pltpu.SemaphoreType.DMA((7, 4))]
+        return [pltpu.SemaphoreType.DMA((8, 4)), pltpu.SemaphoreType.DMA((7, 4))]
 
 
 class Reduce:
@@ -598,19 +646,20 @@
             pltpu.VMEM((4, rows, cut), bf16),
             pltpu.VMEM((4, rows, width - cut), bf16),
             pltpu.VMEM((4, rows, width), bf16),
-            pltpu.SemaphoreType.DMA((5, 4)),
-            pltpu.SemaphoreType.DMA((5, 4)),
+            pltpu.SemaphoreType.DMA((7, 4)),
+            pltpu.SemaphoreType.DMA((7, 4)),
         ]
 
-    def first(self, step):
-        plane = self.planes[step]
+    def first(self, step, part):
+        plane, x, y = self.planes[step], self.x, self.y
+        its_x, its_y = (1 - x, 1 - y) if part == 0 else (x, y)
         self.sends.start(
-            self.parts.at[plane, :, 1 - self.y, :, self.left], self.one_left.at[plane],
-            self.send.at[0, plane], self.receive.at[0, plane], {"y": 1 - self.y},
+            self.parts.at[plane, its_x, 1 - y, :, self.left], self.one_left.at[plane, part],
+            self.send.at[part, plane], self.receive.at[part, plane], {"y": 1 - y},
         )
         self.sends.start(
-            self.parts.at[plane, 1 - self.x, :, :, self.right], self.one_right.at[plane],
-            self.send.at[1, plane], self.receive.at[1, plane], {"x": 1 - self.x},
+            self.parts.at[plane, 1 - x, its_y, :, self.right], self.one_right.at[plane, part],
+            self.send.at[2 + part, plane], self.receive.at[2 + part, plane], {"x": 1 - x},
         )
 
     def add(self, ref, other):
@@ -618,102 +667,59 @@
 
     def second(self, step):
         plane, x, y = self.planes[step], self.x, self.y
-        arrive(self.one_left.at[plane], self.receive.at[0, plane])
+        arrive(self.one_left.at[plane, 0], self.receive.at[0, plane])
         away = self.parts.at[plane, 1 - x, y, :, self.left]
-        self.add(away, self.one_left.at[plane, 1 - x])
-        self.sends.start(away, self.two_left.at[plane], self.send.at[2, plane], self.receive.at[2, plane], {"x": 1 - x})
-        arrive(self.one_right.at[plane], self.receive.at[1, plane])
+        self.add(away, self.one_left.at[plane, 0])
+        self.sends.start(away, self.two_left.at[plane], self.send.at[4, plane], self.receive.at[4, plane], {"x": 1 - x})
+        arrive(self.one_right.at[plane, 0], self.receive.at[2, plane])
         away = self.parts.at[plane, x, 1 - y, :, self.right]
-        self.add(away, self.one_right.at[plane, 1 - y])
-        self.sends.start(away, self.two_right.at[plane], self.send.at[3, plane], self.receive.at[3, plane], {"y": 1 - y})
-        self.add(self.parts.at[plane, x, y, :, self.left], self.one_left.at[plane, x])
-        self.add(self.parts.at[plane, x, y, :, self.right], self.one_right.at[plane, y])
+        self.add(away, self.one_right.at[plane, 0])
+        self.sends.start(away, self.two_right.at[plane], self.send.at[5, plane], self.receive.at[5, plane], {"y": 1 - y})
+
+    def keep(self, step):
+        plane, x, y = self.planes[step], self.x, self.y
+        arrive(self.one_left.at[plane, 1], self.receive.at[1, plane])
+        arrive(self.one_right.at[plane, 1], self.receive.at[3, plane])
+        self.add(self.parts.at[plane, x, y, :, self.left], self.one_left.at[plane, 1])
+        self.add(self.parts.at[plane, x, y, :, self.right], self.one_right.at[plane, 1])
 
     def third(self, step):
         plane, x, y = self.planes[step], self.x, self.y
         here = self.parts.at[plane, x, y]
-        arrive(self.two_left.at[plane], self.receive.at[2, plane])
-        arrive(self.two_right.at[plane], self.receive.at[3, plane])
+        arrive(self.two_left.at[plane], self.receive.at[4, plane])
+        arrive(self.two_right.at[plane], self.receive.at[5, plane])
         self.add(here.at[:, self.left], self.two_left.at[plane])
         self.add(here.at[:, self.right], self.two_right.at[plane])
         if step:
-            self.sends.start(here, self.last.at[self.z], self.send.at[4, plane], self.receive.at[4, self.z], {"z": plane})
+            self.sends.start(here, self.last.at[self.z], self.send.at[6, plane], self.receive.at[6, self.z], {"z": plane})
+
+    def steps(self, order):
+        def begin():
+            self.first(order[0], 0)
+            self.first(order[0], 1)
+
+        found = [begin]
+        for i in range(4):
+
+            def keep(i=i):
+                self.keep(order[i])
+                if i < 3:
+                    self.first(order[i + 1], 0)
+
+            def third(i=i):
+                self.third(order[i])
+                if i < 3:
+                    self.first(order[i + 1], 1)
+
+            found += [lambda i=i: self.second(order[i]), keep, third]
+        return found
 
     def total(self):
         here = self.parts[self.z, self.x, self.y].astype(jnp.float32)
         for plane in self.planes[1:]:
-            arrive(self.last.at[plane], self.receive.at[4, plane])
+            arrive(self.last.at[plane], self.receive.at[6, plane])
             here = here + self.last[plane].astype(jnp.float32)
         return here
-
-
-def gather_call(own, collective):
-    rows, width = own.shape
-
-    def kernel(own_ref, out_ref, send, receive):
-        z, x, y, _ = positions_here()
-        greet(pltpu.get_barrier_semaphore(), near_partners(z, x, y))
-        out_ref[z, x, y] = own_ref[...]
-        sends = Sends()
-        gather = Gather(out_ref, send, receive, width // 2, sends)
-        gather.first(0)
-        gather.begin()
-        gather.second(0)
-        for step in range(1, 4):
-            gather.first(step)
-            gather.second(step)
-        for step in range(4):
-            gather.whole(step)
-        sends.finish()
-
-    vmem = pl.BlockSpec(memory_space=pltpu.VMEM)
-    return pl.pallas_call(
-        kernel,
-        name=f"gather_{collective}",
-        out_shape=jax.ShapeDtypeStruct((4, 2, 2, rows, width), own.dtype),
-        in_specs=[vmem],
-        out_specs=vmem,
-        scratch_shapes=Gather.semaphores(),
-        compiler_params=pltpu.CompilerParams(
-            collective_id=collective, has_side_effects=True, vmem_limit_bytes=VMEM_LIMIT
-        ),
-    )(own)
-
-
-def reduce_call(parts, collective):
-    rows, width = parts.shape[-2:]
-
-    def kernel(parts_ref, out_ref, held, *buffers):
-        z, x, y, _ = positions_here()
-        held[...] = parts_ref[...]
-        greet(pltpu.get_barrier_semaphore(), near_partners(z, x, y))
-        sends = Sends()
-        add = Reduce(held, buffers, width // 2, sends)
-        for step in (3, 2, 1, 0):
-            add.first(step)
-        add.second(3)
-        add.second(2)
-        add.third(3)
-        add.second(1)
-        add.third(2)
-        add.second(0)
-        add.third(1)
-        add.third(0)
-        out_ref[...] = add.total()
-        sends.finish()
-
-    vmem = pl.BlockSpec(memory_space=pltpu.VMEM)
-    return pl.pallas_call(
-        kernel,
-        name=f"reduce_{collective}",
-        out_shape=jax.ShapeDtypeStruct((rows, width), jnp.float32),
-        in_specs=[vmem],
-        out_specs=vmem,
-        scratch_shapes=[pltpu.VMEM(parts.shape, parts.dtype), *Reduce.buffers(rows, width, width // 2)],
-        compiler_params=pltpu.CompilerParams(
-            collective_id=collective, has_side_effects=True, vmem_limit_bytes=VMEM_LIMIT
-        ),
-    )(parts)
 
 
 EXTRA = 128
@@ -756,7 +762,7 @@
     half_tile = tile // 2
     keep = tile + half_tile
 
-    def kernel(own_ref, cot_ref, three_ref, sum_ref, out_ref, dot_ref, expert_ref, shared_ref, held, weights, hidden, gate_grad, up_grad,
+    def kernel(own_ref, cot_ref, three_ref, sum_ref, out_ref, dot_ref, expert0, expert1, expert2, shared_ref, held, weights, hidden, gate_grad, up_grad,
                part_n, part_o, dots_mine, staged, *rest):
         (g_send, g_recv, w_sem, d_send, d_recv, free, x_send, x_recv, s_sem) = rest[:9]
         n_bufs, o_bufs = rest[9:16], rest[16:23]
@@ -832,29 +838,34 @@
 
             lax.fori_loop(0, width // column, one, 0)
 
-        gather.first(0)
-        gather.begin()
-        gather.second(0)
-        gather.first(1)
+        g, n, o = gather.steps(), sum_n.steps((0, 1, 2, 3)), sum_o.steps((0, 1, 2, 3))
+        run(*g[0:4])
         for load in loads:
             load.wait()
-        for step in range(4):
-            gather.whole(step)
-            units_of(step)
-            if step < 3:
-                gather.second(step + 1)
-            if step < 2:
-                gather.first(step + 2)
-            back_of(step)
-            sum_n.first(step)
-            if step:
-                sum_n.second(step - 1)
-            out_of(step)
-            if step > 1:
-                sum_n.third(step - 2)
-            sum_o.first(step)
-            if step:
-                sum_o.second(step - 1)
+        g[4]()
+        units_of(0)
+        g[5]()
+        back_of(0)
+        run(n[0], g[6], g[7])
+        units_of(1)
+        run(n[1], g[8])
+        back_of(1)
+        run(n[2], n[3], g[9], g[10])
+        units_of(2)
+        run(n[4], g[11])
+        back_of(2)
+        run(n[5], n[6], g[12], g[13])
+        units_of(3)
+        n[7]()
+        back_of(3)
+        run(n[8], n[9])
+        out_of(0)
+        run(o[0], n[10])
+        out_of(1)
+        run(n[11], o[1], n[12], o[2], o[3])
+        out_of(2)
+        run(o[4], o[5])
+        out_of(3)
         for i, other in enumerate(others):
             sends.start(dots_mine.at[other["z"], other["x"]], dot_ref.at[z, x, y], d_send.at[i], d_recv.at[z, x, y], other)
         dot_ref[z, x, y] = dots_mine[z, x]
@@ -878,21 +889,15 @@
             lax.fori_loop(0, width // column, one, 0)
 
         away(1 - c, 0)
-        sum_n.second(3)
-        sum_n.third(2)
-        sum_o.third(1)
+        run(o[6], o[7])
         pl.semaphore_wait(free, 1)
         for kind in range(3):
             if kind:
                 away(1 - c, kind)
             sends.start(weights.at[kind, 0:keep], weights.at[kind, keep : 2 * keep], x_send.at[kind], x_recv.at[kind], {"c": 1 - c})
-            if kind == 0:
-                sum_n.third(3)
-                sum_o.second(3)
-                sum_o.third(2)
-            if kind == 1:
-                sum_o.third(3)
-        sum_o.third(0)
+            if kind < 2:
+                run(o[8 + 2 * kind], o[9 + 2 * kind])
+        o[12]()
         writes = []
         for kind in range(3):
             arrive(weights.at[kind, keep : 2 * keep], x_recv.at[kind])
@@ -903,14 +908,14 @@
                 span = pl.ds(pl.multiple_of(i * column, column), column)
                 first = pl.multiple_of(c * tile, 32)
                 value = gradient(kind, first, tile, span)
-                staged[kind % 2, :, span] = value + weights[kind, keep : keep + tile, span].astype(f32)
+                staged[kind % 2, :, span] = (value + weights[kind, keep : keep + tile, span].astype(f32)).astype(bf16)
                 first = pl.multiple_of(routed_units + c * half_tile, 16)
                 value = gradient(kind, first, half_tile, span)
                 shared_ref[kind, :, span] = (value + weights[kind, keep + tile : 2 * keep, span].astype(f32)).astype(bf16)
                 return 0
 
             lax.fori_loop(0, width // column, one, 0)
-            write = pltpu.make_async_copy(staged.at[kind % 2], expert_ref.at[kind], s_sem.at[kind])
+            write = pltpu.make_async_copy(staged.at[kind % 2], (expert0, expert1, expert2)[kind], s_sem.at[kind])
             write.start()
             writes.append(write)
         sum_ref[...] = sum_n.total()
@@ -932,11 +937,11 @@
             jax.ShapeDtypeStruct((rows, width), f32),
             jax.ShapeDtypeStruct((rows, width), f32),
             jax.ShapeDtypeStruct((4, 2, 2, 8, 2 * rows), f32),
-            jax.ShapeDtypeStruct((3, tile, width), f32),
+            *[jax.ShapeDtypeStruct((tile, width), bf16)] * 3,
             jax.ShapeDtypeStruct((3, half_tile, width), bf16),
         ),
         in_specs=[vmem, vmem, anywhere],
-        out_specs=(vmem, vmem, vmem, anywhere, vmem),
+        out_specs=(vmem, vmem, vmem, anywhere, anywhere, anywhere, vmem),
         scratch_shapes=[
             pltpu.VMEM((4, 2, 2, rows, wide), bf16),
             pltpu.VMEM((3, units, width), bf16),
@@ -946,7 +951,7 @@
             pltpu.VMEM((4, 2, 2, rows, width), bf16),
             pltpu.VMEM((4, 2, 2, rows, width), bf16),
             pltpu.VMEM((4, 2, 8, 2 * rows), f32),
-            pltpu.VMEM((2, tile, width), f32),
+            pltpu.VMEM((2, tile, width), bf16),
             *Gather.semaphores(),
             dma((3,)),
             dma((15,)),
@@ -963,30 +968,578 @@
     )(own, cotangents, three)
 
 
-def tree_masks(parent_rows, seg_len):
-    tree_count, segment_count = parent_rows.shape
-    segment_ids = jnp.arange(segment_count, dtype=jnp.int32)
-    step_matrix = (
-        (parent_rows[:, :, None] == segment_ids) & (segment_ids[:, None] > 0)
-    )
-    reached = jnp.broadcast_to(jnp.eye(segment_count, dtype=bool), step_matrix.shape)
-    for _ in range(segment_count):
-        reached = jnp.eye(segment_count, dtype=bool) | jnp.any(
-            step_matrix[:, :, :, None] & reached[:, None, :, :], 2
-        )
-    expanded = jnp.repeat(jnp.repeat(reached, seg_len, 1), seg_len, 2)
-    token_ids = jnp.arange(segment_count * seg_len, dtype=jnp.int32)
-    return expanded & (token_ids[None, :] <= token_ids[:, None])
-
-
-def turn(rows):
-    half = rows.shape[-1] // 2
-    return jnp.concatenate([-rows[..., half:], rows[..., :half]], -1)
-
-
-def turn_back(rows):
-    half = rows.shape[-1] // 2
-    return jnp.concatenate([rows[..., half:], -rows[..., :half]], -1)
+def plane_partners(z, x, y, c):
+    found = []
+    for dz in range(4):
+        for dx in range(2):
+            for dc in range(2):
+                if dz or dx or dc:
+                    found.append({"z": lax.rem(z + dz, 4), "x": (x + dx) % 2, "c": (c + dc) % 2})
+    return found
+
+
+class Plain:
+    def __init__(self):
+        self.open = []
+
+    def start(self, source, target, send, receive, where, same):
+        far = pltpu.make_async_remote_copy(
+            src_ref=source, dst_ref=target, send_sem=send, recv_sem=receive, device_id=where, device_id_type=MESH_ID
+        )
+
+        @pl.when(jnp.logical_not(same))
+        def _():
+            far.start()
+
+        @pl.when(same)
+        def _():
+            pltpu.make_async_copy(source, target, receive).start()
+
+        self.open.append((far, same))
+
+    def finish(self):
+        for far, same in self.open:
+
+            @pl.when(jnp.logical_not(same))
+            def _(far=far):
+                far.wait_send()
+
+        self.open = []
+
+
+def front_call(input_rows, cotangent, project, output, gains, router, vector, positions, parents, bias, table, gate, up, down, experts):
+    bf16, f32 = jnp.bfloat16, jnp.float32
+    rows, width = input_rows.shape[-2:]
+    chunk = 4 * rows
+    tokens = 4 * chunk
+    seq = 2 * rows
+    trees = tokens // seq
+    slice_rows = project.shape[1]
+    half = slice_rows // 2
+    local_heads = project.shape[2] // HD
+    sub = down.shape[0] // trees
+    tile = experts[0].shape[0]
+    routed = 2 * tile
+    units = routed + 2 * sub
+    cut = width // 2
+    late_cut = 3 * width // 4
+    column = width // 2
+    scale = HD ** (-0.5)
+    lines = router.shape[0]
+
+    def kernel(in_ref, cot_ref, project_ref, output_ref, gain1_ref, gain2_ref, router_ref, vector_ref, position_ref, parent_ref,
+               bias_ref, table_ref, gate_ref, up_ref, down_ref, e0, e1, e2,
+               sum_ref, normed_ref, qkv_ref, prob_ref, heads_ref, head_ref, outw_ref, smalls_ref, turns_ref, cots_ref, three_ref,
+               all_ref, parts, small_f, small_v, shared_v, three_v, *rest):
+        (g_send, g_recv, k_send, k_recv, w_send, w_recv, v_send, v_recv, m_send, m_recv, s_send, s_recv, c_send, c_recv, l_sem, e_send,
+         e_recv, o_sem) = rest[:18]
+        z, x, y, c = positions_here()
+        here = z * 2 + x
+        partners = plane_partners(z, x, y, c)
+        other = {"c": 1 - c}
+        sends, plain = Sends(), Plain()
+
+        small_f[...] = jnp.zeros_like(small_f)
+        small_f[0:1, :] = gain1_ref[...].astype(f32)
+        small_f[1:2, :] = gain2_ref[...].astype(f32)
+        small_f[2 : 2 + lines, :] = router_ref[...].astype(f32)
+        small_f[2 + lines : 3 + lines, :] = vector_ref[...].astype(f32)
+        first = c == 0
+        small_f[3 + lines : 4 + lines, 0:seq] = jnp.where(first, position_ref[0:1, :], position_ref[1:2, :]).astype(f32)
+        segments = parent_ref.shape[1]
+        small_f[4 + lines : 5 + lines, 0:segments] = jnp.where(first, parent_ref[0:1, :], parent_ref[1:2, :]).astype(f32)
+        small_f[5 + lines : 8 + lines, 0 : bias_ref.shape[1]] = bias_ref[...].astype(f32)
+        small_v[...] = small_f[...].astype(bf16)
+
+        greet(pltpu.get_barrier_semaphore(), partners + [{"y": 1 - y}])
+        all_ref[z, x, y] = in_ref[c, y]
+        gather = Gather(all_ref, g_send, g_recv, cut, sends)
+        late = Gather(cots_ref, k_send, k_recv, late_cut, sends)
+        add = Reduce(parts, rest[18:], late_cut, sends)
+        a, g, r = gather.steps(), late.steps(), add.steps((3, 2, 1, 0))
+        a[0]()
+        for i, to in enumerate(partners):
+            sends.start(small_v, smalls_ref.at[z, x, c], m_send.at[i], m_recv.at[z, x, c], to)
+        smalls_ref[z, x, c] = small_v[...]
+        for local in range(local_heads):
+            chip = {"z": 2 * c + local // 2, "x": local % 2}
+            home = jnp.logical_and(chip["z"] == z, chip["x"] == x)
+            for part in range(2):
+                where = {**chip, "c": part}
+                same = jnp.logical_and(home, c == part)
+                for i in range(3):
+                    plain.start(
+                        project_ref.at[i, pl.ds(part * half, half), pl.ds(local * HD, HD)],
+                        head_ref.at[here, part, :, pl.ds(i * HD, HD)],
+                        w_send.at[local, part, i], w_recv.at[here, i], where, same,
+                    )
+                plain.start(
+                    output_ref.at[pl.ds(local * HD + part * HD // 2, HD // 2), :],
+                    outw_ref.at[part, :, pl.ds(pl.multiple_of(here * slice_rows, slice_rows), slice_rows)],
+                    w_send.at[local, part, 3], w_recv.at[here, 3], where, same,
+                )
+        mine = pl.ds(pl.multiple_of(c * tile, 16), tile)
+        for i, ref in enumerate((e0, e1, e2)):
+            sends.start(ref, three_v.at[i, mine], e_send.at[i], e_recv.at[i], other)
+            pltpu.make_async_copy(ref, three_v.at[i, mine], l_sem.at[i]).start()
+
+        def flip(i, _):
+            span = pl.ds(pl.multiple_of(i * HD, HD), HD)
+            shared_v[0, span, :] = gate_ref[:, span].astype(f32).T.astype(bf16)
+            shared_v[1, span, :] = up_ref[:, span].astype(f32).T.astype(bf16)
+            shared_v[2, span, :] = down_ref[span, :]
+            return 0
+
+        run(*a[1:3])
+        lax.fori_loop(0, down.shape[0] // HD, flip, 0)
+        run(*a[3:9])
+        place = pl.ds(pl.multiple_of(routed + c * sub, 16), sub)
+        lanes = pl.ds(pl.multiple_of(here * slice_rows, slice_rows), slice_rows)
+
+        def share(i):
+            to_z, to_x = lax.rem(z + i // 2, 4), (x + i % 2) % 2
+            source = shared_v.at[:, pl.ds(pl.multiple_of((to_z * 2 + to_x) * sub, 16), sub)]
+            target = three_v.at[:, place, lanes]
+            if i:
+                sends.start(source, target, s_send.at[i], s_recv.at[here], {"z": to_z, "x": to_x})
+            else:
+                pltpu.make_async_copy(source, target, s_recv.at[here]).start()
+
+        for source in range(trees):
+            for i in range(3):
+                arrive(head_ref.at[source, c, :, pl.ds(i * HD, HD)], w_recv.at[source, i])
+            arrive(outw_ref.at[c, :, pl.ds(source * slice_rows, slice_rows)], w_recv.at[source, 3])
+        sends.start(head_ref.at[:, c], head_ref.at[:, c], v_send.at[0], v_recv.at[0], other)
+        sends.start(outw_ref.at[c], outw_ref.at[c], v_send.at[1], v_recv.at[1], other)
+        share(0)
+        share(4)
+        run(*a[9:])
+        share(5)
+        cots_ref[z, x, y] = cot_ref[c, y]
+        g[0]()
+        for to in partners:
+            spot = (to["z"], to["x"], to["c"])
+            arrive(smalls_ref.at[spot], m_recv.at[spot])
+        gain = jnp.concatenate([smalls_ref[e // 2, e % 2, c, 0:1, :] for e in range(trees)], 1).astype(f32)
+        home_z, home_c = lax.rem(here, 4), here // 4
+        width_of = bias_ref.shape[1]
+        biases = [smalls_ref[home_z, e, home_c, 5 + lines : 8 + lines, 0:width_of] for e in range(2)]
+        row_bias = [jnp.concatenate([b[i : i + 1].astype(f32) for b in biases], 1) for i in range(3)]
+        row_bias = jnp.concatenate(row_bias, 1)
+        arrive(head_ref.at[:, 1 - c], v_recv.at[0])
+        arrive(outw_ref.at[1 - c], v_recv.at[1])
+        query_of = lax.broadcasted_iota(jnp.int32, (seq, seq), 0)
+        key_of = lax.broadcasted_iota(jnp.int32, (seq, seq), 1)
+        segment_of = lax.broadcasted_iota(jnp.int32, (1, seq), 1) // SEG
+        lane = lax.broadcasted_iota(jnp.int32, (seq, HD), 1)
+
+        def attend(step):
+            plane = gather.planes[step]
+
+            def norm(i, _):
+                value = all_ref[plane, i // 2, i % 2].astype(f32)
+                scaled = value * lax.rsqrt(jnp.mean(value * value, -1, keepdims=True) + EPSILON) * gain
+                normed_ref[plane, i // 2, i % 2] = scaled.astype(bf16)
+                return 0
+
+            lax.fori_loop(0, 4, norm, 0)
+            raw = dot_nn(normed_ref[plane].reshape(chunk, width), head_ref[...].reshape(width, 3 * HD)) + row_bias
+            for t in range(2):
+                span = slice(t * seq, (t + 1) * seq)
+                notes = smalls_ref[plane, t, c].astype(f32)
+                hot = (query_of == notes[3 + lines : 4 + lines, 0:seq].astype(jnp.int32)).astype(f32).astype(bf16)
+                turn = dot_tn(hot, table_ref[0]) + dot_tn(hot, table_ref[1])
+                swapped = pltpu.roll(turn, HD // 2, 1)
+                cos = jnp.where(lane < HD // 2, turn, swapped)
+                sin = jnp.where(lane < HD // 2, -swapped, turn)
+                turns_ref[0, plane, span] = cos
+                turns_ref[1, plane, span] = sin
+                reach = []
+                for s in range(segments):
+                    line = (segment_of == s).astype(f32)
+                    for u in range(s):
+                        line = line + (notes[4 + lines : 5 + lines, s : s + 1] == u).astype(f32) * reach[u]
+                    reach.append(line)
+                seen = jnp.concatenate([jnp.broadcast_to(line, (SEG, seq)) for line in reach], 0)
+                allowed = jnp.logical_and(seen > 0.5, key_of <= query_of)
+                turned = []
+                for i in range(2):
+                    value = raw[span, i * HD : (i + 1) * HD]
+                    turned.append((value * cos + pltpu.roll(value, HD // 2, 1) * sin).astype(bf16))
+                turned.append(raw[span, 2 * HD :].astype(bf16))
+                for i in range(3):
+                    qkv_ref[i, plane, span] = turned[i]
+                score = jnp.where(allowed, dot_nt(turned[0], turned[1]) * scale, -1e30)
+                exponent = jnp.exp(score - jnp.max(score, -1, keepdims=True))
+                prob = exponent / jnp.sum(exponent, -1, keepdims=True)
+                prob_ref[plane, t] = prob
+                heads_ref[plane, span] = dot_nn(prob.astype(bf16), turned[2]).astype(bf16)
+
+            def spread_out(i, _):
+                span = pl.ds(pl.multiple_of(i * column, column), column)
+                value = dot_nn(heads_ref[plane], outw_ref[:, :, span].reshape(HD, column))
+                parts[plane, :, :, :, span] = value.astype(bf16).reshape(2, 2, rows, column)
+                return 0
+
+            lax.fori_loop(0, width // column, spread_out, 0)
+
+        attend(3)
+        run(r[0], g[1], g[2])
+        share(6)
+        attend(2)
+        run(r[1], r[2], g[3])
+        share(7)
+        run(r[3], g[4])
+        attend(1)
+        share(2)
+        run(r[4], r[5], g[5])
+        share(3)
+        run(r[6], g[6])
+        attend(0)
+        share(1)
+        for i in range(3):
+            arrive(three_v.at[i, mine], l_sem.at[i])
+            arrive(three_v.at[i, pl.ds(pl.multiple_of((1 - c) * tile, 16), tile)], e_recv.at[i])
+        early = pltpu.make_async_copy(three_v.at[:, pl.ds(0, routed)], three_ref.at[:, pl.ds(0, routed)], o_sem.at[0])
+        early.start()
+        run(r[7], r[8], g[7], r[9], g[8], r[10], g[9], r[11], g[10], r[12], g[11], g[12])
+        sum_ref[...] = add.total()
+        for source in range(trees):
+            arrive(three_v.at[:, place, pl.ds(source * slice_rows, slice_rows)], s_recv.at[source])
+        sends.start(three_v.at[:, place], three_v.at[:, place], c_send, c_recv, other)
+        g[13]()
+        arrive(three_v.at[:, pl.ds(pl.multiple_of(routed + (1 - c) * sub, 16), sub)], c_recv)
+        rest_of = pltpu.make_async_copy(
+            three_v.at[:, pl.ds(routed, units - routed)], three_ref.at[:, pl.ds(routed, units - routed)], o_sem.at[1]
+        )
+        rest_of.start()
+        early.wait()
+        rest_of.wait()
+        plain.finish()
+        sends.finish()
+
+    vmem = pl.BlockSpec(memory_space=pltpu.VMEM)
+    anywhere = pl.BlockSpec(memory_space=pl.ANY)
+    dma = pltpu.SemaphoreType.DMA
+    shape = jax.ShapeDtypeStruct
+    return pl.pallas_call(
+        kernel,
+        name="front",
+        out_shape=(
+            shape((rows, width), f32),
+            shape((4, 2, 2, rows, width), bf16),
+            shape((3, 4, chunk, HD), bf16),
+            shape((4, 2, seq, seq), f32),
+            shape((4, chunk, HD), bf16),
+            shape((trees, 2, half, 3 * HD), bf16),
+            shape((2, HD // 2, width), bf16),
+            shape((4, 2, 2, 16, slice_rows), bf16),
+            shape((2, 4, chunk, HD), f32),
+            shape((4, 2, 2, rows, width), bf16),
+            shape((3, units, width), bf16),
+        ),
+        in_specs=[vmem] * 18,
+        out_specs=(vmem,) * 10 + (anywhere,),
+        scratch_shapes=[
+            pltpu.VMEM((4, 2, 2, rows, width), bf16),
+            pltpu.VMEM((4, 2, 2, rows, width), bf16),
+            pltpu.VMEM((16, slice_rows), f32),
+            pltpu.VMEM((16, slice_rows), bf16),
+            pltpu.VMEM((3, *down.shape), bf16),
+            pltpu.VMEM((3, units, width), bf16),
+            *Gather.semaphores(),
+            *Gather.semaphores(),
+            dma((local_heads, 2, 4)),
+            dma((trees, 4)),
+            dma((2,)),
+            dma((2,)),
+            dma((15,)),
+            dma((4, 2, 2)),
+            dma((trees,)),
+            dma((trees,)),
+            dma,
+            dma,
+            dma((3,)),
+            dma((3,)),
+            dma((3,)),
+            dma((2,)),
+            *Reduce.buffers(rows, width, late_cut),
+        ],
+        compiler_params=pltpu.CompilerParams(collective_id=8, has_side_effects=True, vmem_limit_bytes=VMEM_LIMIT),
+    )(input_rows, cotangent, project, output, *gains, router, vector, positions, parents, bias, table, gate, up, down, *experts)
+
+
+def all_but(z, x, y, c):
+    found = []
+    for dz in range(4):
+        for dx in range(2):
+            for dy in range(2):
+                for dc in range(2):
+                    if dz or dx or dy or dc:
+                        found.append(
+                            {"z": lax.rem(z + dz, 4), "x": (x + dx) % 2, "y": (y + dy) % 2, "c": (c + dc) % 2}
+                        )
+    return found
+
+
+def attention_back_call(own_grad, normed, qkv, probs, heads, head, out_head, turns, input_rows, hidden_grad, gain, lines,
+                        own_output, vectors, shared):
+    bf16, f32 = jnp.bfloat16, jnp.float32
+    rows, width = own_grad.shape
+    chunk = 4 * rows
+    tokens = 4 * chunk
+    seq = 2 * rows
+    trees, _, half, _ = head.shape
+    slice_rows = 2 * half
+    sub = shared.shape[1]
+    cut = 3 * width // 4
+    column = width // 2
+    scale = HD ** (-0.5)
+    local_heads = trees // 2
+
+    def kernel(grad_ref, normed_ref, qkv_ref, prob_ref, heads_ref, head_ref, outw_ref, turns_ref, in_ref, hg_ref, gain_ref,
+               result_ref, vec_ref, shared_ref,
+               layer_ref, ig, pgrad_ref, ograd_ref, gate_ref, up_ref, down_ref, gain1_ref, gain2_ref, router_ref, vector_ref, bias_ref,
+               sgrad_ref,               held, parts, raw_grad, dwp, dwp_got, dwp_sum, dwo, dwo_got, dwo_sum, message, got, bias_sum, *rest):
+        (g_send, g_recv, l_send, l_recv, i_send, i_recv, m_send, m_recv, s_send, s_recv, c_send, c_recv, w_send,
+         w_recv) = rest[:14]
+        z, x, y, c = positions_here()
+        here = z * 2 + x
+        everyone = all_but(z, x, y, c)
+        greet(pltpu.get_barrier_semaphore(), everyone)
+        sends = Sends()
+        plain = Plain()
+        other, across = {"c": 1 - c}, {"y": 1 - y}
+        held[z, x, y] = grad_ref[...]
+        gather = Gather(held, g_send, g_recv, cut, sends)
+        add = Reduce(parts, rest[14:], cut, sends)
+        g, r = gather.steps(), add.steps((0, 1, 2, 3))
+        g[0]()
+        layer_ref[c, y] = result_ref[...]
+        sends.start(layer_ref.at[c, y], layer_ref.at[c, y], l_send.at[0], l_recv.at[0], across)
+        sends.start(layer_ref.at[c, y], layer_ref.at[c, y], l_send.at[1], l_recv.at[1], other)
+
+        def lanes_of(e):
+            return pl.ds(pl.multiple_of(e * slice_rows, slice_rows), slice_rows)
+
+        bias_sum[...] = jnp.zeros_like(bias_sum)
+
+        def attend(step):
+            plane = gather.planes[step]
+            grads = dot_nt(held[plane].reshape(chunk, width), outw_ref[...].reshape(HD, width)).astype(bf16)
+            cos, sin = turns_ref[0, plane], turns_ref[1, plane]
+            for t in range(2):
+                span = slice(t * seq, (t + 1) * seq)
+                prob = prob_ref[plane, t]
+                out_grad = grads[span]
+                query, key, value = (qkv_ref[i, plane, span] for i in range(3))
+                value_grad = dot_tn(prob.astype(bf16), out_grad)
+                prob_grad = dot_nt(out_grad, value)
+                score_grad = (prob * (prob_grad - jnp.sum(prob * prob_grad, -1, keepdims=True))).astype(bf16)
+                sides = [dot_nn(score_grad, key) * scale, dot_tn(score_grad, query) * scale]
+                sides = [s * cos[span] - pltpu.roll(s, HD // 2, 1) * sin[span] for s in sides] + [value_grad]
+                for i in range(3):
+                    side = sides[i].astype(bf16)
+                    raw_grad[plane, span, i * HD : (i + 1) * HD] = side
+                    bias_sum[0:1, i * HD : (i + 1) * HD] += jnp.sum(side.astype(f32), 0, keepdims=True)
+
+            def back(i, _):
+                span = pl.ds(pl.multiple_of(i * column, column), column)
+                weight = head_ref[pl.ds(i * (trees // 2), trees // 2)].reshape(column, 3 * HD)
+                parts[plane, :, :, :, span] = dot_nt(raw_grad[plane], weight).astype(bf16).reshape(2, 2, rows, column)
+                return 0
+
+            lax.fori_loop(0, 2, back, 0)
+
+        def share(i):
+            to_z, to_x = lax.rem(z + i // 2, 4), (x + i % 2) % 2
+            source = shared_ref.at[:, :, lanes_of(to_z * 2 + to_x)]
+            target = sgrad_ref.at[:, pl.ds(pl.multiple_of(here * sub, 16), sub)]
+            if i:
+                sends.start(source, target, s_send.at[i], s_recv.at[here], {"z": to_z, "x": to_x})
+            else:
+                pltpu.make_async_copy(source, target, s_recv.at[here]).start()
+
+        share(0)
+        share(4)
+        run(*g[1:3])
+        share(5)
+        run(*g[3:5])
+        attend(0)
+        run(g[5], r[0], g[6], g[7])
+        share(6)
+        attend(1)
+        run(r[1], g[8], r[2], r[3])
+        share(7)
+        run(g[9], g[10])
+        attend(2)
+        share(2)
+        run(r[4], g[11], r[5])
+        share(3)
+        run(r[6], g[12], g[13])
+        share(1)
+        attend(3)
+        run(r[7], r[8], r[9])
+        arrive(layer_ref.at[c, 1 - y], l_recv.at[0])
+        sends.start(layer_ref.at[c, 1 - y], layer_ref.at[c, 1 - y], l_send.at[2], l_recv.at[2], other)
+
+        def project(e, _):
+            rows_n = normed_ref[:, :, :, :, lanes_of(e)].reshape(tokens, slice_rows)
+            value = dot_tn(rows_n, raw_grad[...].reshape(tokens, 3 * HD))
+            dwp[e] = value.astype(bf16).reshape(2, half, 3 * HD)
+            return 0
+
+        lax.fori_loop(0, trees, project, 0)
+        sends.start(dwp.at[:, 1 - c], dwp_got, c_send.at[0], c_recv.at[0], other)
+        run(r[10], r[11])
+
+        def output(i, _):
+            span = pl.ds(pl.multiple_of(i * column, column), column)
+            rows_g = held[:, :, :, :, span].reshape(tokens, column)
+            value = dot_tn(heads_ref[...].reshape(tokens, HD), rows_g)
+            dwo[:, :, span] = value.astype(bf16).reshape(2, HD // 2, column)
+            return 0
+
+        lax.fori_loop(0, 2, output, 0)
+        sends.start(dwo.at[1 - c], dwo_got, c_send.at[1], c_recv.at[1], other)
+        r[12]()
+        arrive(dwp_got, c_recv.at[0])
+        dwp_sum[...] = (dwp[:, c].astype(f32) + dwp_got[...].astype(f32)).astype(bf16)
+        arrive(dwo_got, c_recv.at[1])
+        dwo_sum[...] = (dwo[c].astype(f32) + dwo_got[...].astype(f32)).astype(bf16)
+        holder = z // 2
+        place = lax.rem(z, 2) * 2 + x
+        for e in range(trees):
+            same = jnp.logical_and(here == e, c == holder)
+            where = {"z": e // 2, "x": e % 2, "c": holder}
+            for i in range(3):
+                plain.start(
+                    dwp_sum.at[e, :, pl.ds(i * HD, HD)],
+                    pgrad_ref.at[i, pl.ds(pl.multiple_of(c * half, 16), half), pl.ds(pl.multiple_of(place * HD, HD), HD)],
+                    w_send.at[e, i], w_recv.at[place, c, i], where, same,
+                )
+            plain.start(
+                dwo_sum.at[:, pl.ds(e * slice_rows, slice_rows)],
+                ograd_ref.at[pl.ds(pl.multiple_of(place * HD + c * (HD // 2), 16), HD // 2), :],
+                w_send.at[e, 3], w_recv.at[place, c, 3], where, same,
+            )
+
+        for source in range(trees):
+            arrive(sgrad_ref.at[:, pl.ds(source * sub, sub)], s_recv.at[source])
+
+        def flip(i, _):
+            span = pl.ds(pl.multiple_of(i * HD, HD), HD)
+            gate_ref[:, span] = sgrad_ref[0, span, :].astype(f32).T.astype(bf16)
+            up_ref[:, span] = sgrad_ref[1, span, :].astype(f32).T.astype(bf16)
+            down_ref[span, :] = sgrad_ref[2, span, :]
+            return 0
+
+        lax.fori_loop(0, trees * sub // HD, flip, 0)
+
+        total = add.total()
+        value = in_ref[c, y].astype(f32)
+        norm = lax.rsqrt(jnp.mean(value * value, -1, keepdims=True) + EPSILON)
+        gain_part = jnp.sum(total * value * norm, 0, keepdims=True)
+        scaled = total * gain_ref[...]
+        ig[c, y] = (
+            hg_ref[...] + norm * scaled - value * norm**3 * jnp.mean(scaled * value, -1, keepdims=True)
+        ).astype(bf16)
+        sends.start(ig.at[c, y], ig.at[c, y], i_send.at[0], i_recv.at[0], across)
+        sends.start(ig.at[c, y], ig.at[c, y], i_send.at[1], i_recv.at[1], other)
+        row = lax.broadcasted_iota(jnp.int32, (16, slice_rows), 0)
+        bias = [
+            jnp.concatenate([bias_sum[0:1, i * HD : (i + 1) * HD], jnp.zeros((1, slice_rows - HD), f32)], 1) for i in range(3)
+        ]
+        for e in range(trees):
+            block = vec_ref[:, e * slice_rows : (e + 1) * slice_rows].astype(f32)
+            block = jnp.where(row == lines + 2, gain_part[:, e * slice_rows : (e + 1) * slice_rows], block)
+            for i in range(3):
+                block = jnp.where(row == lines + 3 + i, bias[i], block)
+            message[e] = block.astype(bf16)
+        for i, to in enumerate(everyone):
+            sends.start(message.at[to["z"] * 2 + to["x"]], got.at[z, x, y, c], m_send.at[i], m_recv.at[z, x, y, c], to)
+        got[z, x, y, c] = message[here]
+        arrive(ig.at[c, 1 - y], i_recv.at[0])
+        sends.start(ig.at[c, 1 - y], ig.at[c, 1 - y], i_send.at[2], i_recv.at[2], other)
+
+        for l in range(local_heads):
+            for part in range(2):
+                for i in range(3):
+                    arrive(pgrad_ref.at[i, pl.ds(part * half, half), pl.ds(l * HD, HD)], w_recv.at[l, part, i])
+                arrive(ograd_ref.at[pl.ds(l * HD + part * (HD // 2), HD // 2), :], w_recv.at[l, part, 3])
+        arrive(layer_ref.at[1 - c, y], l_recv.at[1])
+        arrive(layer_ref.at[1 - c, 1 - y], l_recv.at[2])
+        for to in everyone:
+            spot = (to["z"], to["x"], to["y"], to["c"])
+            arrive(got.at[spot], m_recv.at[spot])
+        small = jnp.sum(got[...].reshape(32, 16, slice_rows).astype(f32), 0)
+        router_ref[...] = small[0:lines]
+        vector_ref[...] = small[lines : lines + 1]
+        gain2_ref[...] = small[lines + 1 : lines + 2]
+        gain1_ref[...] = small[lines + 2 : lines + 3]
+        source_z, source_x = 2 * c + z // 2, lax.rem(z, 2)
+        both = got[source_z, source_x, y, 0].astype(f32) + got[source_z, source_x, y, 1].astype(f32)
+        both = both[:, 0:HD]
+        both = jnp.where(x == 1, pltpu.roll(both, HD // 2, 1), both)
+        bias_ref[...] = both[lines + 3 : lines + 6, 0 : HD // 2]
+        arrive(ig.at[1 - c, y], i_recv.at[1])
+        arrive(ig.at[1 - c, 1 - y], i_recv.at[2])
+        plain.finish()
+        sends.finish()
+
+    vmem = pl.BlockSpec(memory_space=pltpu.VMEM)
+    dma = pltpu.SemaphoreType.DMA
+    shape = jax.ShapeDtypeStruct
+    return pl.pallas_call(
+        kernel,
+        name="attention_back",
+        out_shape=(
+            shape((2, 2, rows, width), bf16),
+            shape((2, 2, rows, width), bf16),
+            shape((3, slice_rows, local_heads * HD), bf16),
+            shape((local_heads * HD, slice_rows), bf16),
+            shape((slice_rows, trees * sub), bf16),
+            shape((slice_rows, trees * sub), bf16),
+            shape((trees * sub, slice_rows), bf16),
+            shape((1, slice_rows), f32),
+            shape((1, slice_rows), f32),
+            shape((lines, slice_rows), f32),
+            shape((1, slice_rows), f32),
+            shape((3, HD // 2), f32),
+        ),
+        in_specs=[vmem] * 14,
+        out_specs=(vmem,) * 12,
+        scratch_shapes=[
+            pltpu.VMEM((3, trees * sub, slice_rows), bf16),
+            pltpu.VMEM((4, 2, 2, rows, width), bf16),
+            pltpu.VMEM((4, 2, 2, rows, width), bf16),
+            pltpu.VMEM((4, chunk, 3 * HD), bf16),
+            pltpu.VMEM((trees, 2, half, 3 * HD), bf16),
+            pltpu.VMEM((trees, half, 3 * HD), bf16),
+            pltpu.VMEM((trees, half, 3 * HD), bf16),
+            pltpu.VMEM((2, HD // 2, width), bf16),
+            pltpu.VMEM((HD // 2, width), bf16),
+            pltpu.VMEM((HD // 2, width), bf16),
+            pltpu.VMEM((trees, 16, slice_rows), bf16),
+            pltpu.VMEM((4, 2, 2, 2, 16, slice_rows), bf16),
+            pltpu.VMEM((8, 3 * HD), f32),
+            *Gather.semaphores(),
+            dma((3,)),
+            dma((3,)),
+            dma((3,)),
+            dma((3,)),
+            dma((31,)),
+            dma((4, 2, 2, 2)),
+            dma((trees,)),
+            dma((trees,)),
+            dma((2,)),
+            dma((2,)),
+            dma((trees, 4)),
+            dma((local_heads, 2, 4)),
+            *Reduce.buffers(rows, width, cut),
+        ],
+        compiler_params=pltpu.CompilerParams(collective_id=10, has_side_effects=True, vmem_limit_bytes=VMEM_LIMIT),
+    )(own_grad, normed, qkv, probs, heads, head, out_head, turns, input_rows, hidden_grad, gain, own_output, vectors, shared)
 
 
 def chip_shards(
@@ -1031,116 +1584,49 @@
 
     own_input = own(layer_input)
     own_cotangent = own(cotangent)
-
-    def mine(array):
-        return lax.dynamic_index_in_dim(array, c, 0, keepdims=False).astype(bf16).reshape(-1)
-
-    pieces = [
-        norm1_gain,
-        norm2_gain,
-        shared_vector,
-        router_weight.T.reshape(-1),
-        project_bias.reshape(-1),
-        mine(positions),
-        mine(parents),
-    ]
-    sizes = [p.shape[0] for p in pieces]
-    small = lax.all_gather(jnp.concatenate(pieces), AXES, axis=0, tiled=False)
-    small = small.reshape(trees, 2, 2, -1)
-    starts = [sum(sizes[:i]) for i in range(len(sizes))]
-
-    def part(i):
-        return small[..., starts[i] : starts[i] + sizes[i]]
-
-    gain_one = part(0)[:, 0, 0].reshape(-1).astype(f32)
-    gain_two = part(1)[:, 0, 0].reshape(-1).astype(f32)
-    vector_full = part(2)[:, 0, 0].reshape(-1)
-    router_full = (
-        part(3)[:, 0, 0]
-        .reshape(trees, expert_count, slice_rows)
-        .transpose(1, 0, 2)
-        .reshape(expert_count, model_width)
-    )
-    small_weights = jnp.concatenate([router_full, vector_full[None]], 0)
-    bias_full = part(4).reshape(trees, 4, 3, -1).transpose(2, 1, 0, 3).reshape(3, -1)
-    head = y * trees + here
-    bias_head = lax.dynamic_slice(bias_full, (0, head * HD), (3, HD)).astype(f32)
-
-    def by_tree(i):
-        return lax.dynamic_index_in_dim(part(i)[:, 0], c, 1, keepdims=False)
-
-    all_positions = by_tree(5).reshape(-1).astype(f32)
-    all_parents = by_tree(6).astype(jnp.int32)
-
-    local_heads = project_weight.shape[2] // HD
-    half_rows = slice_rows // 2
-
-    def swap_cores(array):
-        return lax.all_to_all(array, "c", split_axis=0, concat_axis=0, tiled=True)
-
-    def swap_chips(array):
-        return lax.all_to_all(array, ("z", "x"), split_axis=0, concat_axis=0, tiled=True)
-
-    def join_cores(array, axis):
-        return lax.all_gather(array, "c", axis=axis, tiled=True)
-
-    send = project_weight.transpose(1, 0, 2).reshape(3, 2, half_rows, local_heads, HD)
-    send = send.transpose(1, 3, 0, 2, 4)
-    send = swap_cores(send).reshape(2 * local_heads, 3, half_rows, HD)
-    got = swap_chips(send)
-    got = join_cores(got.transpose(1, 0, 2, 3)[:, :, None], 2)
-    project_head = got.reshape(3, model_width, HD)
-    send = output_weight.reshape(local_heads, HD, 2, half_rows).transpose(2, 0, 1, 3)
-    send = swap_cores(send).reshape(2 * local_heads, HD, half_rows)
-    got = swap_chips(send)
-    got = join_cores(got.transpose(1, 0, 2)[:, :, None], 2)
-    output_head = got.reshape(HD, model_width)
-
-    sub = shared_down.shape[0] // trees
-    send = jnp.stack(
-        [shared_gate.T.reshape(trees, sub, -1), shared_up.T.reshape(trees, sub, -1), shared_down.reshape(trees, sub, -1)],
-        1,
-    )
-    got = swap_chips(send).transpose(1, 2, 0, 3).reshape(3, sub, model_width)
-    shared_three = join_cores(got, 1)
-    expert_three = join_cores(jnp.stack([expert_gate[0].T, expert_up[0].T, expert_down[0]]), 1)
-    routed_units = expert_three.shape[1]
-    three = jnp.concatenate([expert_three, shared_three], 1)
-
-    all_input = gather_call(own_input, 3).reshape(tokens, model_width).astype(f32)
-    all_cotangent = gather_call(own_cotangent, 4)
-    norm_one = lax.rsqrt(jnp.mean(all_input * all_input, -1, keepdims=True) + EPSILON)
-    normed_one = (all_input * norm_one * gain_one).astype(bf16)
+    by_rows = (2, 2, own_rows, model_width)
+
     half_size = HD // 2
     inverse = ROPE_BASE ** (-(jnp.arange(half_size, dtype=f32) * 2.0 / HD))
-    angles = all_positions[:, None] * inverse[None, :]
-    cosine = jnp.cos(angles)
-    sine = jnp.sin(angles)
-    cosine = jnp.concatenate([cosine, cosine], 1)
-    sine = jnp.concatenate([sine, sine], 1)
-    raw = [product(normed_one, project_head[i]) + bias_head[i] for i in range(3)]
-    tree_shape = (trees, seq_rows, HD)
-    queries = (raw[0] * cosine + turn(raw[0]) * sine).astype(bf16).reshape(tree_shape)
-    key_rows = (raw[1] * cosine + turn(raw[1]) * sine).astype(bf16).reshape(tree_shape)
-    values = raw[2].astype(bf16).reshape(tree_shape)
-    allowed = tree_masks(all_parents, SEG)
-    scores = (
-        jnp.einsum("tqd,tkd->tqk", queries, key_rows, preferred_element_type=f32)
-        * score_scale
+    angles = jnp.arange(seq_rows, dtype=f32)[:, None] * inverse[None, :]
+    table = jnp.concatenate([jnp.cos(angles), jnp.sin(angles)], 1)
+    coarse = lax.reduce_precision(table, 8, 7)
+    table = jnp.stack([coarse, table - coarse]).astype(bf16)
+    (
+        attention,
+        normed_one,
+        qkv,
+        attention_probs,
+        heads_out,
+        head_weight,
+        out_weight,
+        smalls,
+        turns,
+        all_cotangent,
+        three,
+    ) = front_call(
+        layer_input.reshape(by_rows),
+        cotangent.reshape(by_rows),
+        project_weight.transpose(1, 0, 2),
+        output_weight,
+        [norm1_gain[None], norm2_gain[None]],
+        router_weight.T,
+        shared_vector[None],
+        positions,
+        parents[:, 0],
+        project_bias,
+        table,
+        shared_gate,
+        shared_up,
+        shared_down,
+        [expert_gate[0].T, expert_up[0].T, expert_down[0]],
     )
-    masked = jnp.where(allowed, scores, -1e30)
-    highest = jnp.max(masked, -1, keepdims=True)
-    exponent = jnp.exp(masked - highest)
-    attention_probs = exponent / jnp.sum(exponent, -1, keepdims=True)
-    probs_low = attention_probs.astype(bf16)
-    heads_out = (
-        jnp.einsum("tqk,tkd->tqd", probs_low, values, preferred_element_type=f32)
-        .astype(bf16)
-        .reshape(tokens, HD)
-    )
-    attention = reduce_call(product(heads_out, output_head).astype(bf16).reshape(blocks), 5)
+    of_core = lax.dynamic_index_in_dim(smalls.reshape(trees, 2, -1, slice_rows), c, 1, keepdims=False)
+    full = of_core[:, : expert_count + 3].transpose(1, 0, 2).reshape(expert_count + 3, model_width)
+    gain_one, gain_two = full[0].astype(f32), full[1].astype(f32)
+    small_weights = full[2:]
+    routed_units = 2 * expert_down.shape[1]
     own_rows_in = own_input.astype(f32)
-    own_norm_one = lax.rsqrt(jnp.mean(own_rows_in * own_rows_in, -1, keepdims=True) + EPSILON)
     hidden_state = own_rows_in + attention
     norm_two = lax.rsqrt(jnp.mean(hidden_state * hidden_state, -1, keepdims=True) + EPSILON)
     own_normed_two = (hidden_state * norm_two * gain_two).astype(bf16)
@@ -1169,7 +1655,7 @@
         ],
         1,
     )
-    normed_sum, ffn_out, dots, expert_sum, shared_sum = experts_call(
+    normed_sum, ffn_out, dots, *expert_sum, shared_sum = experts_call(
         jnp.concatenate([own_normed_two, extra], 1), all_cotangent, three, routed_units
     )
     own_output = (hidden_state + ffn_out).astype(bf16)
@@ -1194,77 +1680,54 @@
         + norm_two * scaled_two
         - hidden_state * norm_two**3 * jnp.mean(scaled_two * hidden_state, -1, keepdims=True)
     )
-    attention_grad = gather_call(hidden_grad_rows.astype(bf16), 6).reshape(tokens, model_width)
-
-    output_grad = product_left(heads_out, attention_grad).astype(bf16)
-    heads_grad = product_right(attention_grad, output_head).astype(bf16).reshape(tree_shape)
-    value_grad = jnp.einsum("tqk,tqd->tkd", probs_low, heads_grad, preferred_element_type=f32)
-    prob_grads = jnp.einsum("tqd,tkd->tqk", heads_grad, values, preferred_element_type=f32)
-    score_grad = (
-        attention_probs
-        * (prob_grads - jnp.sum(attention_probs * prob_grads, -1, keepdims=True))
-    ).astype(bf16)
-    query_grad = jnp.einsum("tqk,tkd->tqd", score_grad, key_rows, preferred_element_type=f32)
-    key_grad = jnp.einsum("tqk,tqd->tkd", score_grad, queries, preferred_element_type=f32)
-    query_grad = (query_grad * score_scale).reshape(tokens, HD)
-    key_grad = (key_grad * score_scale).reshape(tokens, HD)
-    query_grad = query_grad * cosine + turn_back(query_grad * sine)
-    key_grad = key_grad * cosine + turn_back(key_grad * sine)
-    raw_grads = [g.astype(bf16) for g in (query_grad, key_grad, value_grad.reshape(tokens, HD))]
-    bias_grad = jnp.stack([jnp.sum(g.astype(f32), 0) for g in raw_grads])
-    project_grad = jnp.stack([product_left(normed_one, g) for g in raw_grads]).astype(bf16)
-    normed_part = sum(product_right(g, project_head[i]) for i, g in enumerate(raw_grads))
-    normed_one_grad = reduce_call(normed_part.astype(bf16).reshape(blocks), 7)
-    grad_gain_one = jnp.sum(normed_one_grad * own_rows_in * own_norm_one, 0)
-    scaled_one = normed_one_grad * gain_one
-    own_grad = (
-        hidden_grad_rows
-        + own_norm_one * scaled_one
-        - own_rows_in * own_norm_one**3 * jnp.mean(scaled_one * own_rows_in, -1, keepdims=True)
-    )
-    layer_output = lax.all_gather(own_output, ("c", "y"), axis=0, tiled=True).reshape(micro_count, seq_rows, model_width)
-    input_grad = lax.all_gather(own_grad, ("c", "y"), axis=0, tiled=True).reshape(micro_count, seq_rows, model_width)
-
-    bias_place = lax.dynamic_update_slice(jnp.zeros((3, bias_full.shape[1]), f32), bias_grad, (0, head * HD))
-    vectors = jnp.concatenate([grad_small, grad_gain_one[None], grad_gain_two[None]], 0)
-    vectors = lax.psum(jnp.concatenate([vectors.reshape(-1), bias_place.reshape(-1)]), AXES)
-    split = (expert_count + 3) * model_width
-    bias_sum = vectors[split:].reshape(3, -1)
-    vectors = lax.dynamic_slice(vectors[:split].reshape(-1, model_width), (0, here * slice_rows), (expert_count + 3, slice_rows))
-    bias_width = project_bias.shape[1]
-    bias_out = lax.dynamic_slice(bias_sum, (0, ((y * 2 + c) * trees + here) * bias_width), (3, bias_width))
-
-    def sum_cores(array, axis):
-        return lax.psum_scatter(array, "c", scatter_dimension=axis, tiled=True)
-
-    send = project_grad.reshape(3, trees, 2, half_rows, HD)
-    send = sum_cores(send, 2).reshape(3, trees, half_rows, HD).transpose(1, 0, 2, 3)
-    got = swap_chips(send).reshape(2, local_heads, 3, half_rows, HD)
-    got = swap_cores(got).reshape(2, local_heads, 3, half_rows, HD)
-    project_out = got.transpose(0, 3, 2, 1, 4).reshape(slice_rows, 3, local_heads * HD).astype(f32)
-    send = output_grad.reshape(HD, trees, 2, half_rows)
-    send = sum_cores(send, 2).reshape(HD, trees, half_rows).transpose(1, 0, 2)
-    got = swap_chips(send).reshape(2, local_heads, HD, half_rows)
-    got = swap_cores(got).reshape(2, local_heads, HD, half_rows)
-    output_out = got.transpose(1, 2, 0, 3).reshape(local_heads * HD, slice_rows).astype(f32)
-    send = shared_sum.reshape(3, sub, trees, slice_rows).transpose(2, 0, 1, 3)
-    got = swap_chips(send).transpose(1, 0, 2, 3).reshape(3, trees * sub, slice_rows).astype(f32)
-    return (
+    vectors = jnp.concatenate([grad_small, grad_gain_two[None]], 0)
+    vectors = jnp.pad(vectors, ((0, -vectors.shape[0] % 16), (0, 0))).astype(bf16)
+    (
         layer_output,
         input_grad,
-        vectors[expert_count + 1],
         project_out,
+        output_out,
+        gate_out,
+        up_out,
+        down_out,
+        gain_one_out,
+        gain_two_out,
+        router_out,
+        vector_out,
         bias_out,
-        output_out,
-        vectors[expert_count + 2],
-        vectors[:expert_count].T,
-        vectors[expert_count],
-        got[0].T,
-        got[1].T,
-        got[2],
-        expert_sum[0].T[None],
-        expert_sum[1].T[None],
-        expert_sum[2][None],
+    ) = attention_back_call(
+        hidden_grad_rows.astype(bf16),
+        normed_one,
+        qkv,
+        attention_probs,
+        heads_out,
+        head_weight,
+        out_weight,
+        turns,
+        layer_input.reshape(by_rows),
+        hidden_grad_rows,
+        gain_one[None],
+        expert_count,
+        own_output,
+        vectors,
+        shared_sum,
+    )
+    return (
+        layer_output.reshape(layer_input.shape),
+        input_grad.reshape(layer_input.shape).astype(f32),
+        gain_one_out[0],
+        project_out.astype(f32).transpose(1, 0, 2),
+        bias_out,
+        output_out.astype(f32),
+        gain_two_out[0],
+        router_out.T,
+        vector_out[0],
+        gate_out.astype(f32),
+        up_out.astype(f32),
+        down_out.astype(f32),
+        expert_sum[0].astype(f32).T[None],
+        expert_sum[1].astype(f32).T[None],
+        expert_sum[2].astype(f32)[None],
     )
 
 

time: 848 us -> 508 us (0.60)
  waiting for transfers between devices: 230 us -> 0 us
  Pallas kernels: 388 us -> 461 us
  local copies, waits for them, and re-layouts: 67.4 us -> 12.7 us
  matrix products: 44.8 us -> 2.67 us
  starting transfers between devices: 31.8 us -> 0 us
  other arithmetic: 42.2 us -> 20.9 us
  blocking collectives: 16.7 us -> 0 us
  between operations: 17.1 us -> 1.12 us
    psum x1 -> x0, waiting for transfers between devices: 115 us -> none  [chip_shards(): lax.psum(jnp.concatenate([vectors.reshape(-1), bias_place.reshape(-1)]),...]
    pallas_call x5 -> x2, Pallas kernels: 236 us -> 319 us  [the longest x1 169 us: front_call(): pl.pallas_call(kernel, name='front', out_shape=(shape((rows, width), f32)...]
    all_to_all x7 -> x0, waiting for transfers between devices: 79.4 us -> none  [the longest x6 77.9 us: swap_chips(): lax.all_to_all(array, ('z', 'x'), split_axis=0, concat_axis=0, tiled=True)]
    all_gather x5 -> x0, waiting for transfers between devices: 34.3 us -> none  [the longest x1 19.5 us: chip_shards(): lax.all_gather(own_grad, ('c', 'y'), axis=0, tiled=True)]
    all_to_all x7 -> x0, starting transfers between devices: 31 us -> none  [the longest x6 27.5 us: swap_chips(): lax.all_to_all(array, ('z', 'x'), split_axis=0, concat_axis=0, tiled=True)]
    all_to_all x3 -> x0, blocking collectives: 14.3 us -> none  [swap_cores(): return lax.all_to_all(array, 'c', split_axis=0, concat_axis=0, tiled=True)]
    dot_general x5 -> x1, matrix products: 13.3 us -> 0.17 us  [product_right(): lax.dot_general(left_side, right_side, (((1,), (1,)), ((), ())), preferre...]
    slice x13 -> x1, local copies, waits for them, and re-layouts: 13.1 us -> 0.01 us  [chip_shards(): small_weights = full[2:]]
  transfers between devices with their start and end apart: 16 -> 0, of which waited for: 8 -> 0; matrix products, arithmetic and copies ran while one was open for 13% -> 0% of each run, Pallas kernels for 23% -> 0%
where the time goes in v3:
time: 508 us; the launch traced here: 498 us
  Pallas kernels  461 us (91%)
  other arithmetic  20.9 us (4%)
  local copies, waits for them, and re-layouts  12.7 us (2%)
    pallas_call x1, Pallas kernels, front_call(): pl.pallas_call(kernel, name='front', out_shape=(shape((rows, width), f32)...  169 us
    pallas_call x1, Pallas kernels, attention_back_call(): pl.pallas_call(kernel, name='attention_back', out_shape=(shape((2, 2, row...  150 us
    pallas_call x1, Pallas kernels, experts_call(): pl.pallas_call(kernel, name='experts', out_shape=(jax.ShapeDtypeStruct((r...  142 us

profile of v3, /device:TPU:0, one launch (start us, length us, event | category | flops | bytes accessed | tf_op | source)
XLA Modules:
  0.0 498.2 jit_solution(17561864931428314110)
XLA Ops:
  0.7 1.2 broadcast_in_dim.51.gain1_ref
  1.9 1.2 broadcast_in_dim.52.gain2_ref
  3.1 1.2 broadcast_in_dim.53.vector_ref
  4.4 0.8 convert_bitcast_fusion.5
  6.2 168.8 %front.1 = (f32[64,2048]{1,0:T(8,128)}, bf16[4,2,2,64,2048]{4,3,2,1,0:T(8,128)(2,1)}, bf16[3,4,256,128]{3,2,1,0:T(8,128)(2,1)}, f32[4,2,128,128]{3,2,1,0:T(8,128...) custom-call(bf16[2,2,64,2048]{3,2,1,0:T(8,128)(2,1)} %bitcast.87, ...), custom_call_target="tpu_custom_call" | custom-call | tf_op jit(solution)/shard_map/front/pallas_call | solution.py:1225
  174.9 0.9 constant_dynamic-slice_fusion.1
  175.8 1.3 multiply_reduce_fusion.2
  178.8 0.8 concatenate.42.own_ref
  179.6 141.7 %experts.1 = (f32[64,2048]{1,0:T(8,128)}, f32[64,2048]{1,0:T(8,128)}, f32[4,2,2,8,128]{4,3,2,1,0:T(8,128)}, bf16[352,2048]{1,0:T(8,128)(2,1)}, bf16[352,2048]{1,...) custom-call(bf16[64,2176]{1,0:T(8,128)(2,1)} %concatenate.42.own_ref, ...), custom_call_target="tpu_custom_call" | custom-call | flops 39862665216 | bytes 41943040 | tf_op jit(solution)/shard_map/experts/pallas_call | solution.py:933
  321.3 0.9 constant_dynamic-slice_fusion
  322.4 2.3 multiply_reduce_fusion
  324.9 2.1 fusion.17
  327.0 0.7 fusion.4.vec_ref
  327.6 150.3 %attention_back.1 = (bf16[2,2,64,2048]{3,2,1,0:T(8,128)(2,1)}, bf16[2,2,64,2048]{3,2,1,0:T(8,128)(2,1)}, bf16[3,256,512]{2,1,0:T(8,128)(2,1)}, bf16[512,256]{1,0...) custom-call(bf16[64,2048]{1,0:T(8,128)(2,1)} %get-tuple-element.79.g, ...), custom_call_target="tpu_custom_call" | custom-call | tf_op jit(solution)/shard_map/attention_back/pallas_call | solution.py:1493
  477.9 1.8 convert_element_type.112
  479.8 2.3 convert_element_type.113
  482.1 1.2 convert_element_type.114
  483.5 1.2 convert_element_type.115
  484.9 1.4 convert_bitcast_fusion.2
  486.3 1.6 bitcast_convert_fusion.1
  487.9 1.9 bitcast_convert_fusion
  489.9 0.9 copy-done.4
  490.8 3.3 convert_bitcast_fusion
  494.1 1.0 copy.80
  (76 shorter events, 6.3 us)
Async XLA Ops:
  0.6 3.7 copy-start
  477.9 4.2 copy-start.9
  482.1 1.4 copy-start.8
  483.5 1.4 copy-start.7
  484.9 1.4 copy-start.5
  486.3 1.6 copy-start.2
  487.9 1.9 copy-start.3
  487.9 2.8 copy-start.4
  490.8 3.3 copy-start.6
  490.8 7.2 %copy-start.1 = (s32[2,128,4]{1,2,0:T(4,128)S(1)}, s32[2,128,4]{1,2,0:T(4,128)}, u32[]{:S(2)}) copy-start(s32[2,128,4]{1,2,0:T(4,128)} %param.22) | copy-start | bytes 12292
  494.1 1.0 copy-start.14
  494.1 1.6 copy-start.11
  494.1 2.1 copy-start.13
  494.1 2.7 copy-start.10
  494.1 3.3 copy-start.12

commit v4 on v3

--- a/solution.py
+++ b/solution.py
@@ -543,8 +543,8 @@
 class Gather:
     ready = (5, 8, 11, 14)
 
-    def __init__(self, held, send, receive, cut, sends):
-        self.held, self.send, self.receive, self.sends = held, send, receive, sends
+    def __init__(self, held, send, receive, cut, sends, twice=False):
+        self.held, self.send, self.receive, self.sends, self.twice = held, send, receive, sends, twice
         width = held.shape[-1]
         self.left, self.right = pl.ds(0, cut), pl.ds(cut, width - cut)
         self.z, self.x, self.y, _ = positions_here()
@@ -574,21 +574,25 @@
         plane, x, y = self.planes[step], self.x, self.y
         if part == 0:
             self.pass_on(plane, x, y, self.left, 0, "x")
-            self.pass_on(plane, x, y, self.right, 1, "y")
+            if step or not self.twice:
+                self.pass_on(plane, x, y, self.right, 1, "y")
         else:
-            self.pass_on(plane, x, y, self.left, 2, "y")
+            if step or not self.twice:
+                self.pass_on(plane, x, y, self.left, 2, "y")
             self.pass_on(plane, x, y, self.right, 3, "x")
 
     def second(self, step):
         plane, x, y = self.planes[step], self.x, self.y
         arrive(self.block(plane, 1 - x, y, self.left), self.receive.at[0, plane])
         self.pass_on(plane, 1 - x, y, self.left, 4, "y")
-        arrive(self.block(plane, x, 1 - y, self.right), self.receive.at[1, plane])
+        if step or not self.twice:
+            arrive(self.block(plane, x, 1 - y, self.right), self.receive.at[1, plane])
         self.pass_on(plane, x, 1 - y, self.right, 5, "x")
 
     def third(self, step):
         plane, x, y = self.planes[step], self.x, self.y
-        arrive(self.block(plane, x, 1 - y, self.left), self.receive.at[2, plane])
+        if step or not self.twice:
+            arrive(self.block(plane, x, 1 - y, self.left), self.receive.at[2, plane])
         arrive(self.block(plane, 1 - x, y, self.right), self.receive.at[3, plane])
 
     def fourth(self, step):
@@ -762,13 +766,14 @@
     half_tile = tile // 2
     keep = tile + half_tile
 
-    def kernel(own_ref, cot_ref, three_ref, sum_ref, out_ref, dot_ref, expert0, expert1, expert2, shared_ref, held, weights, hidden, gate_grad, up_grad,
+    def kernel(own_ref, cot_in, three_ref, sum_ref, out_ref, dot_ref, expert0, expert1, expert2, shared_ref, cot_ref, held, weights, hidden, gate_grad, up_grad,
                part_n, part_o, dots_mine, staged, *rest):
         (g_send, g_recv, w_sem, d_send, d_recv, free, x_send, x_recv, s_sem) = rest[:9]
         n_bufs, o_bufs = rest[9:16], rest[16:23]
         z, x, y, c = positions_here()
         here = z * 2 + x
         loads = [pltpu.make_async_copy(three_ref.at[i], weights.at[i], w_sem.at[i]) for i in range(3)]
+        loads.append(pltpu.make_async_copy(cot_in, cot_ref, w_sem.at[3]))
         for load in loads:
             load.start()
         others = chips_but(z, x, y)
@@ -858,13 +863,13 @@
         units_of(3)
         n[7]()
         back_of(3)
-        run(n[8], n[9])
+        n[8]()
         out_of(0)
-        run(o[0], n[10])
+        run(o[0], n[9])
         out_of(1)
-        run(n[11], o[1], n[12], o[2], o[3])
+        n[10]()
         out_of(2)
-        run(o[4], o[5])
+        run(o[1], n[11])
         out_of(3)
         for i, other in enumerate(others):
             sends.start(dots_mine.at[other["z"], other["x"]], dot_ref.at[z, x, y], d_send.at[i], d_recv.at[z, x, y], other)
@@ -877,44 +882,47 @@
                 return dot_nn(side[pl.ds(first, count), :], held[:, :, :, :, span].reshape(tokens, column))
             return dot_nn(hidden[pl.ds(first, count), :], cot_ref[:, :, :, :, span].reshape(tokens, column))
 
-        def away(core, kind):
-            def one(i, _):
-                span = pl.ds(pl.multiple_of(i * column, column), column)
-                first = pl.multiple_of(core * tile, 32)
-                weights[kind, 0:tile, span] = gradient(kind, first, tile, span).astype(bf16)
-                first = pl.multiple_of(routed_units + core * half_tile, 16)
-                weights[kind, tile:keep, span] = gradient(kind, first, half_tile, span).astype(bf16)
-                return 0
-
-            lax.fori_loop(0, width // column, one, 0)
-
-        away(1 - c, 0)
-        run(o[6], o[7])
+        def away(kind, i):
+            span = pl.ds(i * column, column)
+            first = pl.multiple_of((1 - c) * tile, 32)
+            weights[kind, 0:tile, span] = gradient(kind, first, tile, span).astype(bf16)
+            first = pl.multiple_of(routed_units + (1 - c) * half_tile, 16)
+            weights[kind, tile:keep, span] = gradient(kind, first, half_tile, span).astype(bf16)
+
+        def stay(kind, i):
+            span = pl.ds(i * column, column)
+            first = pl.multiple_of(c * tile, 32)
+            value = gradient(kind, first, tile, span)
+            staged[kind % 2, :, span] = (value + weights[kind, keep : keep + tile, span].astype(f32)).astype(bf16)
+            first = pl.multiple_of(routed_units + c * half_tile, 16)
+            value = gradient(kind, first, half_tile, span)
+            shared_ref[kind, :, span] = (value + weights[kind, keep + tile : 2 * keep, span].astype(f32)).astype(bf16)
+
+        def hand_over(kind):
+            sends.start(weights.at[kind, 0:keep], weights.at[kind, keep : 2 * keep], x_send.at[kind], x_recv.at[kind], {"c": 1 - c})
+
+        away(0, 0)
+        run(o[2], n[12])
+        away(0, 1)
+        o[3]()
         pl.semaphore_wait(free, 1)
-        for kind in range(3):
-            if kind:
-                away(1 - c, kind)
-            sends.start(weights.at[kind, 0:keep], weights.at[kind, keep : 2 * keep], x_send.at[kind], x_recv.at[kind], {"c": 1 - c})
-            if kind < 2:
-                run(o[8 + 2 * kind], o[9 + 2 * kind])
-        o[12]()
+        hand_over(0)
+        for kind in (1, 2):
+            away(kind, 0)
+            o[2 + 2 * kind]()
+            away(kind, 1)
+            o[3 + 2 * kind]()
+            hand_over(kind)
         writes = []
         for kind in range(3):
             arrive(weights.at[kind, keep : 2 * keep], x_recv.at[kind])
             if kind > 1:
                 writes[kind - 2].wait()
-
-            def one(i, _):
-                span = pl.ds(pl.multiple_of(i * column, column), column)
-                first = pl.multiple_of(c * tile, 32)
-                value = gradient(kind, first, tile, span)
-                staged[kind % 2, :, span] = (value + weights[kind, keep : keep + tile, span].astype(f32)).astype(bf16)
-                first = pl.multiple_of(routed_units + c * half_tile, 16)
-                value = gradient(kind, first, half_tile, span)
-                shared_ref[kind, :, span] = (value + weights[kind, keep + tile : 2 * keep, span].astype(f32)).astype(bf16)
-                return 0
-
-            lax.fori_loop(0, width // column, one, 0)
+            stay(kind, 0)
+            o[8 + 2 * kind]()
+            stay(kind, 1)
+            if kind < 2:
+                o[9 + 2 * kind]()
             write = pltpu.make_async_copy(staged.at[kind % 2], (expert0, expert1, expert2)[kind], s_sem.at[kind])
             write.start()
             writes.append(write)
@@ -940,9 +948,10 @@
             *[jax.ShapeDtypeStruct((tile, width), bf16)] * 3,
             jax.ShapeDtypeStruct((3, half_tile, width), bf16),
         ),
-        in_specs=[vmem, vmem, anywhere],
+        in_specs=[vmem, anywhere, anywhere],
         out_specs=(vmem, vmem, vmem, anywhere, anywhere, anywhere, vmem),
         scratch_shapes=[
+            pltpu.VMEM((4, 2, 2, rows, width), bf16),
             pltpu.VMEM((4, 2, 2, rows, wide), bf16),
             pltpu.VMEM((3, units, width), bf16),
             pltpu.VMEM((units, tokens), bf16),
@@ -953,7 +962,7 @@
             pltpu.VMEM((4, 2, 8, 2 * rows), f32),
             pltpu.VMEM((2, tile, width), bf16),
             *Gather.semaphores(),
-            dma((3,)),
+            dma((4,)),
             dma((15,)),
             dma((4, 2, 2)),
             pltpu.SemaphoreType.REGULAR,
@@ -1029,10 +1038,10 @@
 
     def kernel(in_ref, cot_ref, project_ref, output_ref, gain1_ref, gain2_ref, router_ref, vector_ref, position_ref, parent_ref,
                bias_ref, table_ref, gate_ref, up_ref, down_ref, e0, e1, e2,
-               sum_ref, normed_ref, qkv_ref, prob_ref, heads_ref, head_ref, outw_ref, smalls_ref, turns_ref, cots_ref, three_ref,
-               all_ref, parts, small_f, small_v, shared_v, three_v, *rest):
+               sum_ref, normed_out, qkv_ref, prob_ref, heads_ref, head_ref, outw_ref, smalls_ref, turns_ref, cots_out, three_ref,
+               all_ref, parts, small_f, small_v, shared_v, three_v, cots_ref, normed_ref, *rest):
         (g_send, g_recv, k_send, k_recv, w_send, w_recv, v_send, v_recv, m_send, m_recv, s_send, s_recv, c_send, c_recv, l_sem, e_send,
-         e_recv, o_sem) = rest[:18]
+         e_recv, o_sem, n_sem, k_sem) = rest[:20]
         z, x, y, c = positions_here()
         here = z * 2 + x
         partners = plane_partners(z, x, y, c)
@@ -1053,9 +1062,10 @@
 
         greet(pltpu.get_barrier_semaphore(), partners + [{"y": 1 - y}])
         all_ref[z, x, y] = in_ref[c, y]
-        gather = Gather(all_ref, g_send, g_recv, cut, sends)
-        late = Gather(cots_ref, k_send, k_recv, late_cut, sends)
-        add = Reduce(parts, rest[18:], late_cut, sends)
+        all_ref[z, x, 1 - y] = in_ref[c, 1 - y]
+        gather = Gather(all_ref, g_send, g_recv, cut, sends, True)
+        late = Gather(cots_ref, k_send, k_recv, late_cut, sends, True)
+        add = Reduce(parts, rest[20:], late_cut, sends)
         a, g, r = gather.steps(), late.steps(), add.steps((3, 2, 1, 0))
         a[0]()
         for i, to in enumerate(partners):
@@ -1090,9 +1100,10 @@
             shared_v[2, span, :] = down_ref[span, :]
             return 0
 
-        run(*a[1:3])
-        lax.fori_loop(0, down.shape[0] // HD, flip, 0)
-        run(*a[3:9])
+        flips = down.shape[0] // HD
+        for i in range(8):
+            lax.fori_loop(i * flips // 8, (i + 1) * flips // 8, flip, 0)
+            a[i + 1]()
         place = pl.ds(pl.multiple_of(routed + c * sub, 16), sub)
         lanes = pl.ds(pl.multiple_of(here * slice_rows, slice_rows), slice_rows)
 
@@ -1104,6 +1115,14 @@
                 sends.start(source, target, s_send.at[i], s_recv.at[here], {"z": to_z, "x": to_x})
             else:
                 pltpu.make_async_copy(source, target, s_recv.at[here]).start()
+
+        def hand_on(i):
+            from_z, from_x = lax.rem(z + 4 - i // 2, 4), (x + i % 2) % 2
+            source = from_z * 2 + from_x
+            span = pl.ds(pl.multiple_of(source * slice_rows, slice_rows), slice_rows)
+            piece = three_v.at[:, place, span]
+            arrive(piece, s_recv.at[source])
+            sends.start(piece, piece, c_send.at[i], c_recv.at[source], other)
 
         for source in range(trees):
             for i in range(3):
@@ -1116,6 +1135,7 @@
         run(*a[9:])
         share(5)
         cots_ref[z, x, y] = cot_ref[c, y]
+        cots_ref[z, x, 1 - y] = cot_ref[c, 1 - y]
         g[0]()
         for to in partners:
             spot = (to["z"], to["x"], to["c"])
@@ -1182,6 +1202,17 @@
                 return 0
 
             lax.fori_loop(0, width // column, spread_out, 0)
+            copy = pltpu.make_async_copy(normed_ref.at[plane], normed_out.at[plane], n_sem.at[step])
+            copy.start()
+            saved.append(copy)
+
+        def save(step):
+            plane = gather.planes[step]
+            copy = pltpu.make_async_copy(cots_ref.at[plane], cots_out.at[plane], k_sem.at[step])
+            copy.start()
+            saved.append(copy)
+
+        saved = []
 
         attend(3)
         run(r[0], g[1], g[2])
@@ -1189,12 +1220,17 @@
         attend(2)
         run(r[1], r[2], g[3])
         share(7)
+        hand_on(0)
+        hand_on(4)
         run(r[3], g[4])
+        save(0)
         attend(1)
         share(2)
         run(r[4], r[5], g[5])
+        hand_on(5)
         share(3)
         run(r[6], g[6])
+        hand_on(6)
         attend(0)
         share(1)
         for i in range(3):
@@ -1202,17 +1238,28 @@
             arrive(three_v.at[i, pl.ds(pl.multiple_of((1 - c) * tile, 16), tile)], e_recv.at[i])
         early = pltpu.make_async_copy(three_v.at[:, pl.ds(0, routed)], three_ref.at[:, pl.ds(0, routed)], o_sem.at[0])
         early.start()
-        run(r[7], r[8], g[7], r[9], g[8], r[10], g[9], r[11], g[10], r[12], g[11], g[12])
+        run(r[7], r[8], g[7])
+        save(1)
+        hand_on(7)
+        run(r[9], g[8])
+        hand_on(2)
+        run(r[10], g[9], r[11], g[10])
+        save(2)
+        hand_on(3)
+        run(r[12], g[11], g[12])
+        hand_on(1)
         sum_ref[...] = add.total()
+        g[13]()
+        save(3)
+        theirs = pl.ds(pl.multiple_of(routed + (1 - c) * sub, 16), sub)
         for source in range(trees):
-            arrive(three_v.at[:, place, pl.ds(source * slice_rows, slice_rows)], s_recv.at[source])
-        sends.start(three_v.at[:, place], three_v.at[:, place], c_send, c_recv, other)
-        g[13]()
-        arrive(three_v.at[:, pl.ds(pl.multiple_of(routed + (1 - c) * sub, 16), sub)], c_recv)
+            arrive(three_v.at[:, theirs, pl.ds(source * slice_rows, slice_rows)], c_recv.at[source])
         rest_of = pltpu.make_async_copy(
             three_v.at[:, pl.ds(routed, units - routed)], three_ref.at[:, pl.ds(routed, units - routed)], o_sem.at[1]
         )
         rest_of.start()
+        for copy in saved:
+            copy.wait()
         early.wait()
         rest_of.wait()
         plain.finish()
@@ -1239,7 +1286,7 @@
             shape((3, units, width), bf16),
         ),
         in_specs=[vmem] * 18,
-        out_specs=(vmem,) * 10 + (anywhere,),
+        out_specs=(vmem, anywhere) + (vmem,) * 7 + (anywhere,) * 2,
         scratch_shapes=[
             pltpu.VMEM((4, 2, 2, rows, width), bf16),
             pltpu.VMEM((4, 2, 2, rows, width), bf16),
@@ -1247,6 +1294,8 @@
             pltpu.VMEM((16, slice_rows), bf16),
             pltpu.VMEM((3, *down.shape), bf16),
             pltpu.VMEM((3, units, width), bf16),
+            pltpu.VMEM((4, 2, 2, rows, width), bf16),
+            pltpu.VMEM((4, 2, 2, rows, width), bf16),
             *Gather.semaphores(),
             *Gather.semaphores(),
             dma((local_heads, 2, 4)),
@@ -1257,12 +1306,14 @@
             dma((4, 2, 2)),
             dma((trees,)),
             dma((trees,)),
-            dma,
-            dma,
+            dma((trees,)),
+            dma((trees,)),
             dma((3,)),
             dma((3,)),
             dma((3,)),
             dma((2,)),
+            dma((4,)),
+            dma((4,)),
             *Reduce.buffers(rows, width, late_cut),
         ],
         compiler_params=pltpu.CompilerParams(collective_id=8, has_side_effects=True, vmem_limit_bytes=VMEM_LIMIT),
@@ -1297,22 +1348,24 @@
     scale = HD ** (-0.5)
     local_heads = trees // 2
 
-    def kernel(grad_ref, normed_ref, qkv_ref, prob_ref, heads_ref, head_ref, outw_ref, turns_ref, in_ref, hg_ref, gain_ref,
+    def kernel(grad_ref, normed_in, qkv_ref, prob_ref, heads_ref, head_ref, outw_ref, turns_ref, in_ref, hg_ref, gain_ref,
                result_ref, vec_ref, shared_ref,
                layer_ref, ig, pgrad_ref, ograd_ref, gate_ref, up_ref, down_ref, gain1_ref, gain2_ref, router_ref, vector_ref, bias_ref,
-               sgrad_ref,               held, parts, raw_grad, dwp, dwp_got, dwp_sum, dwo, dwo_got, dwo_sum, message, got, bias_sum, *rest):
+               sgrad_ref, normed_ref,               held, parts, raw_grad, dwp, dwp_got, dwp_sum, dwo, dwo_got, dwo_sum, message, got, bias_sum, *rest):
         (g_send, g_recv, l_send, l_recv, i_send, i_recv, m_send, m_recv, s_send, s_recv, c_send, c_recv, w_send,
-         w_recv) = rest[:14]
+         w_recv, n_sem) = rest[:15]
         z, x, y, c = positions_here()
         here = z * 2 + x
         everyone = all_but(z, x, y, c)
+        load = pltpu.make_async_copy(normed_in, normed_ref, n_sem)
+        load.start()
         greet(pltpu.get_barrier_semaphore(), everyone)
         sends = Sends()
         plain = Plain()
         other, across = {"c": 1 - c}, {"y": 1 - y}
         held[z, x, y] = grad_ref[...]
         gather = Gather(held, g_send, g_recv, cut, sends)
-        add = Reduce(parts, rest[14:], cut, sends)
+        add = Reduce(parts, rest[15:], cut, sends)
         g, r = gather.steps(), add.steps((0, 1, 2, 3))
         g[0]()
         layer_ref[c, y] = result_ref[...]
@@ -1389,6 +1442,7 @@
             dwp[e] = value.astype(bf16).reshape(2, half, 3 * HD)
             return 0
 
+        load.wait()
         lax.fori_loop(0, trees, project, 0)
         sends.start(dwp.at[:, 1 - c], dwp_got, c_send.at[0], c_recv.at[0], other)
         run(r[10], r[11])
@@ -1424,18 +1478,6 @@
                 w_send.at[e, 3], w_recv.at[place, c, 3], where, same,
             )
 
-        for source in range(trees):
-            arrive(sgrad_ref.at[:, pl.ds(source * sub, sub)], s_recv.at[source])
-
-        def flip(i, _):
-            span = pl.ds(pl.multiple_of(i * HD, HD), HD)
-            gate_ref[:, span] = sgrad_ref[0, span, :].astype(f32).T.astype(bf16)
-            up_ref[:, span] = sgrad_ref[1, span, :].astype(f32).T.astype(bf16)
-            down_ref[span, :] = sgrad_ref[2, span, :]
-            return 0
-
-        lax.fori_loop(0, trees * sub // HD, flip, 0)
-
         total = add.total()
         value = in_ref[c, y].astype(f32)
         norm = lax.rsqrt(jnp.mean(value * value, -1, keepdims=True) + EPSILON)
@@ -1459,6 +1501,17 @@
         for i, to in enumerate(everyone):
             sends.start(message.at[to["z"] * 2 + to["x"]], got.at[z, x, y, c], m_send.at[i], m_recv.at[z, x, y, c], to)
         got[z, x, y, c] = message[here]
+        for source in range(trees):
+            arrive(sgrad_ref.at[:, pl.ds(source * sub, sub)], s_recv.at[source])
+
+        def flip(i, _):
+            span = pl.ds(pl.multiple_of(i * HD, HD), HD)
+            gate_ref[:, span] = sgrad_ref[0, span, :].astype(f32).T.astype(bf16)
+            up_ref[:, span] = sgrad_ref[1, span, :].astype(f32).T.astype(bf16)
+            down_ref[span, :] = sgrad_ref[2, span, :]
+            return 0
+
+        lax.fori_loop(0, trees * sub // HD, flip, 0)
         arrive(ig.at[c, 1 - y], i_recv.at[0])
         sends.start(ig.at[c, 1 - y], ig.at[c, 1 - y], i_send.at[2], i_recv.at[2], other)
 
@@ -1507,10 +1560,11 @@
             shape((1, slice_rows), f32),
             shape((3, HD // 2), f32),
         ),
-        in_specs=[vmem] * 14,
+        in_specs=[vmem, pl.BlockSpec(memory_space=pl.ANY)] + [vmem] * 12,
         out_specs=(vmem,) * 12,
         scratch_shapes=[
             pltpu.VMEM((3, trees * sub, slice_rows), bf16),
+            pltpu.VMEM((4, 2, 2, rows, width), bf16),
             pltpu.VMEM((4, 2, 2, rows, width), bf16),
             pltpu.VMEM((4, 2, 2, rows, width), bf16),
             pltpu.VMEM((4, chunk, 3 * HD), bf16),
@@ -1536,10 +1590,48 @@
             dma((2,)),
             dma((trees, 4)),
             dma((local_heads, 2, 4)),
+            dma,
             *Reduce.buffers(rows, width, cut),
         ],
         compiler_params=pltpu.CompilerParams(collective_id=10, has_side_effects=True, vmem_limit_bytes=VMEM_LIMIT),
     )(own_grad, normed, qkv, probs, heads, head, out_head, turns, input_rows, hidden_grad, gain, own_output, vectors, shared)
+
+
+def finish_call(arrays, kinds):
+    count = len(arrays)
+
+    def kernel(*refs):
+        sources, targets = refs[:count], refs[count : 2 * count]
+        narrow, wide = refs[2 * count : 3 * count], refs[3 * count : 4 * count]
+        in_sem, out_sem = refs[4 * count :]
+        reads = [pltpu.make_async_copy(sources[i], narrow[i], in_sem.at[i]) for i in range(count)]
+        for read in reads:
+            read.start()
+        writes = []
+        for i in range(count):
+            reads[i].wait()
+            wide[i][...] = narrow[i][...].astype(kinds[i])
+            write = pltpu.make_async_copy(wide[i], targets[i], out_sem.at[i])
+            write.start()
+            writes.append(write)
+        for write in writes:
+            write.wait()
+
+    anywhere = pl.BlockSpec(memory_space=pl.ANY)
+    return pl.pallas_call(
+        kernel,
+        name="finish",
+        out_shape=tuple(jax.ShapeDtypeStruct(a.shape, kind) for a, kind in zip(arrays, kinds)),
+        in_specs=[anywhere] * count,
+        out_specs=(anywhere,) * count,
+        scratch_shapes=[
+            *[pltpu.VMEM(a.shape, a.dtype) for a in arrays],
+            *[pltpu.VMEM(a.shape, kind) for a, kind in zip(arrays, kinds)],
+            pltpu.SemaphoreType.DMA((count,)),
+            pltpu.SemaphoreType.DMA((count,)),
+        ],
+        compiler_params=pltpu.CompilerParams(vmem_limit_bytes=VMEM_LIMIT),
+    )(*arrays)
 
 
 def chip_shards(
@@ -1712,22 +1804,56 @@
         vectors,
         shared_sum,
     )
+    (
+        expert_gate_out,
+        expert_up_out,
+        expert_down_out,
+        gate_out,
+        up_out,
+        down_out,
+        project_out,
+        output_out,
+        input_grad,
+        layer_output,
+        gain_one_out,
+        gain_two_out,
+        router_out,
+        vector_out,
+        bias_out,
+    ) = finish_call(
+        [
+            *expert_sum,
+            gate_out,
+            up_out,
+            down_out,
+            project_out,
+            output_out,
+            input_grad,
+            layer_output,
+            gain_one_out,
+            gain_two_out,
+            router_out,
+            vector_out,
+            bias_out,
+        ],
+        [f32] * 9 + [bf16] + [f32] * 5,
+    )
     return (
         layer_output.reshape(layer_input.shape),
-        input_grad.reshape(layer_input.shape).astype(f32),
+        input_grad.reshape(layer_input.shape),
         gain_one_out[0],
-        project_out.astype(f32).transpose(1, 0, 2),
+        project_out.transpose(1, 0, 2),
         bias_out,
-        output_out.astype(f32),
+        output_out,
         gain_two_out[0],
         router_out.T,
         vector_out[0],
-        gate_out.astype(f32),
-        up_out.astype(f32),
-        down_out.astype(f32),
-        expert_sum[0].astype(f32).T[None],
-        expert_sum[1].astype(f32).T[None],
-        expert_sum[2].astype(f32)[None],
+        gate_out,
+        up_out,
+        down_out,
+        expert_gate_out.T[None],
+        expert_up_out.T[None],
+        expert_down_out[None],
     )
 
 

time: 508 us -> 487 us (0.959)
  other arithmetic: 20.9 us -> 6.15 us
  local copies, waits for them, and re-layouts: 12.7 us -> 7.52 us
    pallas_call x0 -> x1, Pallas kernels: none -> 9.08 us  [finish_call(): pl.pallas_call(kernel, name='finish', out_shape=tuple((jax.ShapeDtypeStru...]
    convert_element_type x5 -> x0, other arithmetic: 8.18 us -> none  [the longest x1 2.3 us: chip_shards(): gate_out.astype(f32)]
    pallas_call x1, Pallas kernels: 142 us -> 135 us  [experts_call(): pl.pallas_call(kernel, name='experts', out_shape=(jax.ShapeDtypeStruct((r...]
    unnamed x40 -> x8, local copies, waits for them, and re-layouts: 5.88 us -> 0.65 us
    broadcast_in_dim x2 -> x0, other arithmetic: 5.22 us -> none  [the longest x1 3.3 us: chip_shards(): expert_sum[1].astype(f32).T[None]]
where the time goes in v4:
time: 487 us; the launch traced here: 478 us
  Pallas kernels  461 us (95%)
  local copies, waits for them, and re-layouts  7.52 us (2%)
  other arithmetic  6.15 us (1%)
    pallas_call x1, Pallas kernels, front_call(): pl.pallas_call(kernel, name='front', out_shape=(shape((rows, width), f32)...  167 us
    pallas_call x1, Pallas kernels, attention_back_call(): pl.pallas_call(kernel, name='attention_back', out_shape=(shape((2, 2, row...  149 us
    pallas_call x1, Pallas kernels, experts_call(): pl.pallas_call(kernel, name='experts', out_shape=(jax.ShapeDtypeStruct((r...  135 us

profile of v4, /device:TPU:0, one launch (start us, length us, event | category | flops | bytes accessed | tf_op | source)
XLA Modules:
  0.0 478.1 jit_solution(1881586858138031709)
XLA Ops:
  0.7 1.2 broadcast_in_dim.19.gain1_ref
  1.9 1.2 broadcast_in_dim.20.gain2_ref
  3.1 1.2 broadcast_in_dim.21.vector_ref
  4.4 0.8 convert_bitcast_fusion.2
  5.2 0.3 cosine_bitcast_fusion
  5.5 0.6 pad_maximum_fusion.1.table_ref
  6.2 167.0 %front.1 = (f32[64,2048]{1,0:T(8,128)}, bf16[4,2,2,64,2048]{4,3,2,1,0:T(8,128)(2,1)}, bf16[3,4,256,128]{3,2,1,0:T(8,128)(2,1)}, f32[4,2,128,128]{3,2,1,0:T(8,128...) custom-call(bf16[2,2,64,2048]{3,2,1,0:T(8,128)(2,1)} %bitcast.80, ...), custom_call_target="tpu_custom_call" | custom-call | tf_op jit(solution)/shard_map/front/pallas_call | solution.py:1272
  173.2 0.9 constant_dynamic-slice_fusion.1
  174.1 1.3 multiply_reduce_fusion.2
  175.5 0.6 copy.71
  176.1 0.1 multiply_convert_fusion
  176.2 0.2 fusion.22
  176.6 0.1 copy.61
  176.7 0.1 copy.63
  176.8 0.1 copy.64
  177.1 0.8 concatenate.42.own_ref
  177.9 135.2 %experts.1 = (f32[64,2048]{1,0:T(8,128)}, f32[64,2048]{1,0:T(8,128)}, f32[4,2,2,8,128]{4,3,2,1,0:T(8,128)}, bf16[352,2048]{1,0:T(8,128)(2,1)}, bf16[352,2048]{1,...) custom-call(bf16[64,2176]{1,0:T(8,128)(2,1)} %concatenate.42.own_ref, ...), custom_call_target="tpu_custom_call" | custom-call | flops 39862665216 | bytes 41943040 | tf_op jit(solution)/shard_map/experts/pallas_call | solution.py:941
  313.1 0.9 constant_dynamic-slice_fusion
  314.2 2.3 multiply_reduce_fusion
  316.5 0.2 convolution_convert_fusion
  316.7 2.1 fusion.17
  318.8 0.7 fusion.4.vec_ref
  319.4 149.3 %attention_back.1 = (bf16[2,2,64,2048]{3,2,1,0:T(8,128)(2,1)}, bf16[2,2,64,2048]{3,2,1,0:T(8,128)(2,1)}, bf16[3,256,512]{2,1,0:T(8,128)(2,1)}, bf16[512,256]{1,0...) custom-call(bf16[64,2048]{1,0:T(8,128)(2,1)} %get-tuple-element.109., ...), custom_call_target="tpu_custom_call" | custom-call | tf_op jit(solution)/shard_map/attention_back/pallas_call | solution.py:1546
  468.8 9.1 %finish.1 = (f32[352,2048]{1,0:T(8,128)}, f32[352,2048]{1,0:T(8,128)}, f32[352,2048]{1,0:T(8,128)}, f32[256,1408]{1,0:T(8,128)}, f32[256,1408]{1,0:T(8,128)}, /*...) custom-call(bf16[352,2048]{1,0:T(8,128)(2,1)} %get-tuple-element.64., ...), custom_call_target="tpu_custom_call" | custom-call | tf_op jit(solution)/shard_map/finish/pallas_call | solution.py:1621
  (37 shorter events, 0.7 us)
Async XLA Ops:
  0.6 3.7 copy-start
  468.8 9.1 %copy-start.1 = (s32[2,128,4]{1,2,0:T(4,128)S(1)}, s32[2,128,4]{1,2,0:T(4,128)}, u32[]{:S(2)}) copy-start(s32[2,128,4]{1,2,0:T(4,128)} %param.22) | copy-start | bytes 12292

commit v5 on v4

--- a/solution.py
+++ b/solution.py
@@ -497,6 +497,10 @@
     return (z, z + 1 - 2 * (z % 2), 2 - z // 2, 3 * (1 - z // 2))
 
 
+def mirror(z, which):
+    return (z, z + 1 - 2 * (z % 2), lax.rem(z + 2, 4), 3 - z)[which]
+
+
 def greet(barrier, partners):
     for partner in partners:
         pl.semaphore_signal(barrier, inc=1, device_id=partner, device_id_type=MESH_ID)
@@ -1016,7 +1020,7 @@
         self.open = []
 
 
-def front_call(input_rows, cotangent, project, output, gains, router, vector, positions, parents, bias, table, gate, up, down, experts):
+def front_call(input_rows, cotangent, project, output, rows3, router, positions, parents, bias, table, gate, up, down, experts):
     bf16, f32 = jnp.bfloat16, jnp.float32
     rows, width = input_rows.shape[-2:]
     chunk = 4 * rows
@@ -1031,12 +1035,12 @@
     routed = 2 * tile
     units = routed + 2 * sub
     cut = width // 2
-    late_cut = 3 * width // 4
+    late_cut = 5 * width // 8
     column = width // 2
     scale = HD ** (-0.5)
     lines = router.shape[0]
 
-    def kernel(in_ref, cot_ref, project_ref, output_ref, gain1_ref, gain2_ref, router_ref, vector_ref, position_ref, parent_ref,
+    def kernel(in_ref, cot_ref, project_ref, output_ref, gains_ref, router_ref, position_ref, parent_ref,
                bias_ref, table_ref, gate_ref, up_ref, down_ref, e0, e1, e2,
                sum_ref, normed_out, qkv_ref, prob_ref, heads_ref, head_ref, outw_ref, smalls_ref, turns_ref, cots_out, three_ref,
                all_ref, parts, small_f, small_v, shared_v, three_v, cots_ref, normed_ref, *rest):
@@ -1049,10 +1053,9 @@
         sends, plain = Sends(), Plain()
 
         small_f[...] = jnp.zeros_like(small_f)
-        small_f[0:1, :] = gain1_ref[...].astype(f32)
-        small_f[1:2, :] = gain2_ref[...].astype(f32)
+        small_f[0:2, :] = gains_ref[0:2, :].astype(f32)
         small_f[2 : 2 + lines, :] = router_ref[...].astype(f32)
-        small_f[2 + lines : 3 + lines, :] = vector_ref[...].astype(f32)
+        small_f[2 + lines : 3 + lines, :] = gains_ref[2:3, :].astype(f32)
         first = c == 0
         small_f[3 + lines : 4 + lines, 0:seq] = jnp.where(first, position_ref[0:1, :], position_ref[1:2, :]).astype(f32)
         segments = parent_ref.shape[1]
@@ -1108,7 +1111,7 @@
         lanes = pl.ds(pl.multiple_of(here * slice_rows, slice_rows), slice_rows)
 
         def share(i):
-            to_z, to_x = lax.rem(z + i // 2, 4), (x + i % 2) % 2
+            to_z, to_x = mirror(z, i // 2), (x + i % 2) % 2
             source = shared_v.at[:, pl.ds(pl.multiple_of((to_z * 2 + to_x) * sub, 16), sub)]
             target = three_v.at[:, place, lanes]
             if i:
@@ -1117,7 +1120,7 @@
                 pltpu.make_async_copy(source, target, s_recv.at[here]).start()
 
         def hand_on(i):
-            from_z, from_x = lax.rem(z + 4 - i // 2, 4), (x + i % 2) % 2
+            from_z, from_x = mirror(z, i // 2), (x + i % 2) % 2
             source = from_z * 2 + from_x
             span = pl.ds(pl.multiple_of(source * slice_rows, slice_rows), slice_rows)
             piece = three_v.at[:, place, span]
@@ -1285,7 +1288,7 @@
             shape((4, 2, 2, rows, width), bf16),
             shape((3, units, width), bf16),
         ),
-        in_specs=[vmem] * 18,
+        in_specs=[vmem] * 16,
         out_specs=(vmem, anywhere) + (vmem,) * 7 + (anywhere,) * 2,
         scratch_shapes=[
             pltpu.VMEM((4, 2, 2, rows, width), bf16),
@@ -1317,7 +1320,7 @@
             *Reduce.buffers(rows, width, late_cut),
         ],
         compiler_params=pltpu.CompilerParams(collective_id=8, has_side_effects=True, vmem_limit_bytes=VMEM_LIMIT),
-    )(input_rows, cotangent, project, output, *gains, router, vector, positions, parents, bias, table, gate, up, down, *experts)
+    )(input_rows, cotangent, project, output, rows3, router, positions, parents, bias, table, gate, up, down, *experts)
 
 
 def all_but(z, x, y, c):
@@ -1343,7 +1346,7 @@
     trees, _, half, _ = head.shape
     slice_rows = 2 * half
     sub = shared.shape[1]
-    cut = 3 * width // 4
+    cut = 5 * width // 8
     column = width // 2
     scale = HD ** (-0.5)
     local_heads = trees // 2
@@ -1405,7 +1408,7 @@
             lax.fori_loop(0, 2, back, 0)
 
         def share(i):
-            to_z, to_x = lax.rem(z + i // 2, 4), (x + i % 2) % 2
+            to_z, to_x = mirror(z, i // 2), (x + i % 2) % 2
             source = shared_ref.at[:, :, lanes_of(to_z * 2 + to_x)]
             target = sgrad_ref.at[:, pl.ds(pl.multiple_of(here * sub, 16), sub)]
             if i:
@@ -1415,21 +1418,21 @@
 
         share(0)
         share(4)
-        run(*g[1:3])
+        run(*g[1:5])
         share(5)
-        run(*g[3:5])
         attend(0)
-        run(g[5], r[0], g[6], g[7])
+        run(g[5], r[0], g[6])
         share(6)
+        g[7]()
         attend(1)
-        run(r[1], g[8], r[2], r[3])
+        run(r[1], g[8])
         share(7)
-        run(g[9], g[10])
+        run(r[2], r[3], g[9], g[10])
         attend(2)
         share(2)
-        run(r[4], g[11], r[5])
+        run(r[4], g[11], r[5], r[6])
         share(3)
-        run(r[6], g[12], g[13])
+        run(g[12], g[13])
         share(1)
         attend(3)
         run(r[7], r[8], r[9])
@@ -1701,9 +1704,8 @@
         cotangent.reshape(by_rows),
         project_weight.transpose(1, 0, 2),
         output_weight,
-        [norm1_gain[None], norm2_gain[None]],
+        jnp.stack([norm1_gain, norm2_gain, shared_vector]),
         router_weight.T,
-        shared_vector[None],
         positions,
         parents[:, 0],
         project_bias,

time: 487 us -> 486 us (level)
  no operation moved by 1% of the time
where the time goes in v5:
time: 486 us; the launch traced here: 476 us
  Pallas kernels  460 us (95%)
  other arithmetic  6.73 us (1%)
  local copies, waits for them, and re-layouts  5.84 us (1%)
    pallas_call x1, Pallas kernels, front_call(): pl.pallas_call(kernel, name='front', out_shape=(shape((rows, width), f32)...  165 us
    pallas_call x1, Pallas kernels, attention_back_call(): pl.pallas_call(kernel, name='attention_back', out_shape=(shape((2, 2, row...  148 us
    pallas_call x1, Pallas kernels, experts_call(): pl.pallas_call(kernel, name='experts', out_shape=(jax.ShapeDtypeStruct((r...  138 us

profile of v5, /device:TPU:0, one launch (start us, length us, event | category | flops | bytes accessed | tf_op | source)
XLA Modules:
  0.0 476.3 jit_solution(5653611080035356320)
XLA Ops:
  0.7 0.7 stack.18
  1.3 0.7 stack.19
  2.0 0.7 stack.20
  2.7 0.6 pad_maximum_fusion.6.gains_ref
  3.3 0.8 convert_bitcast_fusion.2
  4.1 0.3 cosine_bitcast_fusion
  4.4 0.6 pad_maximum_fusion.1.table_ref
  5.1 164.8 %front.1 = (f32[64,2048]{1,0:T(8,128)}, bf16[4,2,2,64,2048]{4,3,2,1,0:T(8,128)(2,1)}, bf16[3,4,256,128]{3,2,1,0:T(8,128)(2,1)}, f32[4,2,128,128]{3,2,1,0:T(8,128...) custom-call(bf16[2,2,64,2048]{3,2,1,0:T(8,128)(2,1)} %bitcast.80, ...), custom_call_target="tpu_custom_call" | custom-call | tf_op jit(solution)/shard_map/front/pallas_call | solution.py:1275
  169.9 0.9 constant_dynamic-slice_fusion.1
  170.8 1.3 multiply_reduce_fusion.2
  172.1 0.6 copy.71
  172.7 0.1 multiply_convert_fusion
  172.9 0.2 fusion.22
  173.2 0.1 copy.61
  173.4 0.1 copy.64
  173.7 0.8 concatenate.42.own_ref
  174.5 137.7 %experts.1 = (f32[64,2048]{1,0:T(8,128)}, f32[64,2048]{1,0:T(8,128)}, f32[4,2,2,8,128]{4,3,2,1,0:T(8,128)}, bf16[352,2048]{1,0:T(8,128)(2,1)}, bf16[352,2048]{1,...) custom-call(bf16[64,2176]{1,0:T(8,128)(2,1)} %concatenate.42.own_ref, ...), custom_call_target="tpu_custom_call" | custom-call | flops 39862665216 | bytes 41943040 | tf_op jit(solution)/shard_map/experts/pallas_call | solution.py:945
  312.2 0.9 constant_dynamic-slice_fusion
  313.3 2.3 multiply_reduce_fusion
  315.6 0.2 convolution_convert_fusion
  315.8 2.1 fusion.17
  317.9 0.7 fusion.4.vec_ref
  318.6 148.4 %attention_back.1 = (bf16[2,2,64,2048]{3,2,1,0:T(8,128)(2,1)}, bf16[2,2,64,2048]{3,2,1,0:T(8,128)(2,1)}, bf16[3,256,512]{2,1,0:T(8,128)(2,1)}, bf16[512,256]{1,0...) custom-call(bf16[64,2048]{1,0:T(8,128)(2,1)} %get-tuple-element.109., ...), custom_call_target="tpu_custom_call" | custom-call | tf_op jit(solution)/shard_map/attention_back/pallas_call | solution.py:1549
  467.0 9.1 %finish.1 = (f32[352,2048]{1,0:T(8,128)}, f32[352,2048]{1,0:T(8,128)}, f32[352,2048]{1,0:T(8,128)}, f32[256,1408]{1,0:T(8,128)}, f32[256,1408]{1,0:T(8,128)}, /*...) custom-call(bf16[352,2048]{1,0:T(8,128)(2,1)} %get-tuple-element.64., ...), custom_call_target="tpu_custom_call" | custom-call | tf_op jit(solution)/shard_map/finish/pallas_call | solution.py:1624
  (38 shorter events, 0.8 us)
Async XLA Ops:
  0.6 2.6 copy-start
  467.0 9.1 %copy-start.1 = (s32[2,128,4]{1,2,0:T(4,128)S(1)}, s32[2,128,4]{1,2,0:T(4,128)}, u32[]{:S(2)}) copy-start(s32[2,128,4]{1,2,0:T(4,128)} %param.22) | copy-start | bytes 12292
